TPU v7x, 128 devices: a whole 4x4x4 slice. The times are simulated.
128 devices in a mesh: ctx: 64 (over y_lo, z, x, core), batch: 2 (over y_hi).
Axes of the slice: x: 4, y: 4 (y_hi: 2, y_lo: 2; y = y_hi * 2 + y_lo), z: 4, core: 2. Of those that a mesh axis runs over, the one named last changes fastest.
Arguments:
- context: bfloat16 [32768, 2048], P(('batch', 'ctx')), parts along dimension 0, may hold values from -48 to 48
- norm_gain: float32 [2048], replicated, may hold values from 0.1 to 1.9
- query_weight: bfloat16 [2048, 1024], replicated, may hold values from -1 to 1
- key_weight: bfloat16 [2048, 1024], replicated, may hold values from -1 to 1
- value_weight: bfloat16 [2048, 1024], replicated, may hold values from -0.125 to 0.125
- out_weight: bfloat16 [1024, 2048], replicated, may hold values from -3 to 3
Outputs:
- output: bfloat16 [512, 2048], P(('batch', 'ctx')), parts along dimension 0
There are 2 independent parts, one for each index of `batch`. A program takes and returns all parts, laid end to end along the dimension named above; an argument that names none is the same for every part. Nothing has to cross between parts.
All inputs are finite; a program needn't handle non-finite values.
Results may differ from a plain program's by a relative error of at most 0.013.
Values may be sent and summed in bfloat16 or wider, within the bound.
No kernel may reach another device: no remote copies, remote signals or barrier semaphores. Data moves between devices by JAX's collectives and lax.ppermute only.
A program may use at most 320 MiB of HBM per device.

v0:
```python
import jax
import jax.numpy as jnp
from jax import lax
from jax.sharding import PartitionSpec as P

HEADS = 8
HD = 128


def spread(block, axis, owner):
    block = jnp.where(lax.axis_index(axis) == owner, block, jnp.zeros_like(block))
    return lax.psum(block, axis)


def merged_2(value, axis, join):
    pieces = jax.tree.map(lambda part: lax.all_gather(part, axis), value)
    head = jax.tree.map(lambda part: part[0], pieces)
    tail = jax.tree.map(lambda part: part[1:], pieces)
    total, _ = lax.scan(lambda total, slab: (join(total, slab), None), head, tail)
    return total


def layer_norm(token_rows, norm_gain):
    widened = token_rows.astype(jnp.float32)
    centred = widened - jnp.mean(widened, axis=-1, keepdims=True)
    variance = jnp.mean(centred * centred, axis=-1, keepdims=True)
    return (centred * lax.rsqrt(variance + 1e-05) * norm_gain).astype(jnp.bfloat16)


def scale_heads(accum, factor):
    shaped = accum.reshape(accum.shape[0], factor.shape[1], -1)
    return (shaped * factor[:, :, None]).reshape(accum.shape)


def divide_heads(accum, factor):
    shaped = accum.reshape(accum.shape[0], factor.shape[1], -1)
    return (shaped / factor[:, :, None]).reshape(accum.shape)


def combine(first, second):
    peak = jnp.maximum(first[0], second[0])
    weight_first = jnp.exp(first[0] - peak)
    weight_second = jnp.exp(second[0] - peak)
    total = first[1] * weight_first + second[1] * weight_second
    accum = scale_heads(first[2], weight_first) + scale_heads(second[2], weight_second)
    return (peak, total, accum)


def local(context, norm_gain, query_weight, key_weight, value_weight, out_weight):
    devices = lax.axis_size("ctx")
    position = lax.axis_index("ctx")
    shard_len = context.shape[0]
    width = query_weight.shape[1]
    scale = HD ** (-0.5)
    normed = layer_norm(context, norm_gain)
    keys = (
        jnp.dot(normed, key_weight, preferred_element_type=jnp.float32)
        .astype(jnp.bfloat16)
        .reshape(shard_len, HEADS, HD)
    )
    values = (
        jnp.dot(normed, value_weight, preferred_element_type=jnp.float32)
        .astype(jnp.bfloat16)
        .reshape(shard_len, HEADS, HD)
    )
    broadcast_rows = spread(context, "ctx", devices - 1)
    latent_normed = layer_norm(broadcast_rows, norm_gain)
    queries = (
        jnp.dot(latent_normed, query_weight, preferred_element_type=jnp.float32) * scale
    ).astype(jnp.bfloat16)
    key_position = position * shard_len + jnp.arange(shard_len, dtype=jnp.int32)
    first_latent = devices * shard_len - shard_len

    def attend_block(start):
        chosen = queries.reshape(shard_len, HEADS, HD)
        scores = jnp.einsum("qhd,khd->hqk", chosen, keys, preferred_element_type=jnp.float32)
        latent_position = first_latent + start + jnp.arange(shard_len, dtype=jnp.int32)
        visible = key_position[None, :] <= latent_position[:, None]
        scores = jnp.where(visible[None], scores, -jnp.inf)
        peak = jnp.max(scores, axis=-1)
        expo = jnp.exp(scores - peak[:, :, None])
        total = jnp.sum(expo, axis=-1)
        accum = jnp.einsum(
            "hqk,khd->qhd", expo.astype(jnp.bfloat16), values, preferred_element_type=jnp.float32
        )
        return (peak.T, total.T, accum.reshape(shard_len, width))

    starts = jnp.arange(shard_len // shard_len, dtype=jnp.int32) * shard_len
    peaks, totals, accums = lax.map(attend_block, starts)
    peaks = peaks.reshape(shard_len, HEADS)
    totals = totals.reshape(shard_len, HEADS)
    accums = accums.reshape(shard_len, width)
    rows_mine = shard_len // devices
    merged = merged_2((peaks, totals, accums), "ctx", combine)
    first_row = position * rows_mine
    total_mine = lax.dynamic_slice_in_dim(merged[1], first_row, rows_mine, 0)
    accum_mine = lax.dynamic_slice_in_dim(merged[2], first_row, rows_mine, 0)
    attended = divide_heads(accum_mine, total_mine).astype(jnp.bfloat16)
    return jnp.dot(attended, out_weight, preferred_element_type=jnp.float32).astype(jnp.bfloat16)


def solution(mesh):
    return jax.shard_map(
        local,
        mesh=mesh,
        in_specs=(P(("batch", "ctx"), None), P(), P(), P(), P(), P()),
        out_specs=P(("batch", "ctx"), None),
        check_vma=False,
    )
```

profile of v0, /device:TPU:1, one launch (start us, length us, event | category | flops | bytes accessed | tf_op | source)
XLA Modules:
  0.0 1190.2 jit_solution(1155851597761901272)
XLA Ops:
  8.8 3.5 convolution_convert_fusion.1
  13.4 3.5 fusion.16
  16.9 542.9 %all-reduce.2.cloned.1.call-done = bf16[256,2048]{1,0:T(8,128)(2,1)} async-done(((bf16[256,2048]{1,0:T(8,128)(2,1)}), bf16[256,2048]{1,0:T(8,128)(2,1)}) %all-reduce.2.cloned.1.call-update) | async-done | bytes 1048592 | tf_op jit(solution)/shard_map/psum | solution.py:12
  563.1 3.5 fusion.17
  570.0 83.7 %all-gather.1 = f32[16384,8]{0,1:T(8,128)S(1)} all-gather(f32[256,8]{0,1:T(8,128)S(1)} %bitcast.78), channel_id=3, replica_groups=mesh['ctx'=64,'batch'=2] {'ctx'}, dimensions={0}, use_global_device_ids=true | all-gather | bytes 532480 | tf_op jit(solution)/shard_map/all_gather | solution.py:16
  653.7 78.6 %all-gather = f32[16384,8]{0,1:T(8,128)S(1)} all-gather(f32[256,8]{0,1:T(8,128)S(1)} %bitcast.77), channel_id=2, replica_groups=mesh['ctx'=64,'batch'=2] {'ctx'}, dimensions={0}, use_global_device_ids=true | all-gather | bytes 532480 | tf_op jit(solution)/shard_map/all_gather | solution.py:16
  732.4 204.6 %all-gather.4.cloned.1.call-done = f32[64,256,1024]{2,1,0:T(8,128)} async-done(((f32[1,256,1024]{2,1,0:T(8,128)}), f32[64,256,1024]{2,1,0:T(8,128)}) %all-gather.4.cloned.1.call-update) | async-done | bytes 67108880 | tf_op jit(solution)/shard_map/all_gather | solution.py:16
  938.3 43.7 %slice.33 = f32[63,256,1024]{2,1,0:T(8,128)} slice(f32[64,256,1024]{2,1,0:T(8,128)} %all-gather.4.cloned.1.call-done), slice={[1:64], [0:256], [0:1024]} | slice | bytes 132120576 | tf_op jit(solution)/shard_map/slice | solution.py:18
  982.0 197.7 %while.2 = (s32[]{:T(128)}, f32[256,8]{0,1:T(8,128)S(1)}, f32[256,8]{0,1:T(8,128)S(1)}, f32[256,1024]{1,0:T(8,128)S(1)}, f32[63,256,8]{1,2,0:T(8,128)S(1)}, /*in...) while((s32[]{:T(128)}, f32[256,8]{0,1:T(8,128)S(1)}, f32[256,8]{0,1:T(8,128)S(1)}, ...), condition=%wide.region_8.9_spmd, body=%wide.region_7.8_spmd.sunk | while | flops 798722 | bytes 7454821 | solution.py:19
  983.0 2.2 fusion.47
  986.1 2.2 fusion.47
  989.2 2.2 fusion.47
  992.4 2.2 fusion.47
  995.5 2.2 fusion.47
  998.6 2.2 fusion.47
  1001.8 2.2 fusion.47
  1004.9 2.2 fusion.47
  1008.1 2.2 fusion.47
  1011.2 2.2 fusion.47
  1014.3 2.2 fusion.47
  1017.5 2.2 fusion.47
  1020.6 2.2 fusion.47
  1023.7 2.2 fusion.47
  1026.9 2.2 fusion.47
  1030.0 2.2 fusion.47
  1033.2 2.2 fusion.47
  1036.3 2.2 fusion.47
  1039.4 2.2 fusion.47
  1042.6 2.2 fusion.47
  1045.7 2.2 fusion.47
  1058.3 2.2 fusion.47
  1067.7 2.2 fusion.47
  1070.8 2.2 fusion.47
  1080.2 2.2 fusion.47
  1083.4 2.2 fusion.47
  1092.8 2.2 fusion.47
  1095.9 2.2 fusion.47
  1105.3 2.2 fusion.47
  1117.9 2.2 fusion.47
  1127.3 2.2 fusion.47
  1130.4 2.2 fusion.47
  1139.8 2.2 fusion.47
  1143.0 2.2 fusion.47
  1152.4 2.2 fusion.47
  1155.5 2.2 fusion.47
  1165.0 2.2 fusion.47
  1177.5 2.2 fusion.47
  1179.9 3.5 convolution_convert_fusion
  (376 shorter events, 124.6 us)
Async XLA Ops:
  6.5 1.6 copy-start
  6.5 553.3 %all-reduce.2.cloned.1.call-start = ((), (), s32[]{:S(2)}) async-start(), calls=%async_computation | async-start | bytes 2097152 | tf_op jit(solution)/shard_map/psum | solution.py:12
  7.6 1.2 copy-start.3
  7.7 929.3 %all-gather.4.cloned.1.call-start = ((), (), s32[]{:S(2)}) async-start(), calls=%async_computation.1 | async-start | bytes 68157440 | tf_op jit(solution)/shard_map/all_gather | solution.py:16
  559.9 3.2 copy-start.1
  566.6 1.0 copy-start.2
Sparse Core Ops, SparseCore 0:
  9.8 550.0 all-reduce.1
  569.7 367.1 all-gather.3
where the time goes:
time: 1190 us
  waiting for transfers between devices  748 us (63%)
  blocking collectives  162 us (14%)
  other arithmetic  143 us (12%)
  local copies, waits for them, and re-layouts  107 us (9%)
  matrix products  15 us (1%)
  between operations  13.5 us (1%)
    psum x1, waiting for transfers between devices, spread(): return lax.psum(block, axis)  543 us
    all_gather x1, waiting for transfers between devices, merged_2(): pieces = jax.tree.map(lambda part: lax.all_gather(part, axis), value)  205 us
    all_gather x2, blocking collectives, merged_2(): pieces = jax.tree.map(lambda part: lax.all_gather(part, axis), value)  162 us
    add x63, other arithmetic, combine(): scale_heads(first[2], weight_first) + scale_heads(second[2], weight_second)  136 us
    slice x3, local copies, waits for them, and re-layouts, merged_2(): tail = jax.tree.map(lambda part: part[1:], pieces)  43.8 us
    mul x126, local copies, waits for them, and re-layouts, scale_heads(): return (shaped * factor[:, :, None]).reshape(accum.shape)  42.2 us
  transfers between devices with their start and end apart: 2, of which 2 were waited for; matrix products, arithmetic and copies ran while one was open for 1% of the time, Pallas kernels for 0%

commit v1 on v0

v1 whole, which is shorter than its diff:
```python
import functools

import jax
import jax.numpy as jnp
from jax import lax
from jax.experimental import pallas as pl
from jax.experimental.pallas import tpu as pltpu
from jax.sharding import Mesh
from jax.sharding import PartitionSpec as P

HEADS = 8
HD = 128
D = 2048
LAT = 256
ROWS = 256
CTX = 16384
MINE = 4
F32 = jnp.float32
BF16 = jnp.bfloat16
CTX_AXES = ("yl", "z", "x", "core")
SWAP = ((0, 1), (1, 0))
ANY = pl.BlockSpec(memory_space=pl.ANY)
VMEM = pl.BlockSpec(memory_space=pltpu.VMEM)
SMEM = pl.BlockSpec(memory_space=pltpu.SMEM)


def xor_pairs(size, mask):
    return [(i, i ^ mask) for i in range(size)]


def near(i):
    return (i ^ (i >> 1)) & 1


def head_of(yl, z, x, core):
    return core * 4 + (near(x) ^ yl) * 2 + (near(z) ^ yl)


def params(mib):
    return pltpu.CompilerParams(vmem_limit_bytes=mib * 2**20)


def normalise(tokens, gain):
    widened = tokens.astype(F32)
    centred = widened - jnp.mean(widened, axis=-1, keepdims=True)
    variance = jnp.mean(centred * centred, axis=-1, keepdims=True)
    return (centred * lax.rsqrt(variance + 1e-05) * gain).astype(BF16)


def norm_rows(src, gain_ref, dst):
    step = 32

    @pl.loop(0, ROWS // step)
    def _(i):
        at = pl.ds(pl.multiple_of(i * step, step), step)
        dst[at, :] = normalise(src[at, :], gain_ref[...])


def own_kernel(tokens, gain_ref, out):
    norm_rows(tokens, gain_ref, out)


def query_kernel(info, tokens, own, gain_ref, weight, out, q0, q1, q2, q3, wbuf, sems):
    copies = []
    for j in range(4):
        at = pl.ds(pl.multiple_of(info[1 + j] * HD, HD), HD)
        copies.append(pltpu.make_async_copy(weight.at[:, at], wbuf.at[:, pl.ds(j * HD, HD)], sems.at[j]))
        copies[-1].start()
    norm_rows(tokens, gain_ref, out)
    for copy in copies:
        copy.wait()
    scale = HD ** (-0.5)

    def project(rows):
        queries = (jnp.dot(rows[...], wbuf[...], preferred_element_type=F32) * scale).astype(BF16)
        for j, q in enumerate((q0, q1, q2, q3)):
            q[...] = queries[:, j * HD : (j + 1) * HD]

    @pl.when(info[0] == 1)
    def _():
        project(own)

    @pl.when(info[0] == 0)
    def _():
        project(out)


def kv_kernel(info, own, other, wk, wv, o0, o1, o2, o3, wbuf, sems):
    copies = []
    for j in (1, 2, 3, 0):
        at = pl.ds(pl.multiple_of(info[1 + j] * HD, HD), HD)
        pair = []
        for k, weight in enumerate((wk, wv)):
            pair.append(
                pltpu.make_async_copy(weight.at[:, at], wbuf.at[j, :, pl.ds(k * HD, HD)], sems.at[j, k])
            )
            pair[-1].start()
        copies.append(pair)
    for j, out, pair in zip((1, 2, 3, 0), (o1, o2, o3, o0), copies):
        for copy in pair:
            copy.wait()
        for k, rows in enumerate((own, other)):
            out[pl.ds(k * ROWS, ROWS), :] = jnp.dot(
                rows[...], wbuf[j], preferred_element_type=F32
            ).astype(BF16)


def attend_kernel(info, query, kv0, kv1, kv2, kv3, out):
    queries = query[...]
    chunks = (kv0, kv1, kv2, kv3)
    row = lax.broadcasted_iota(jnp.int32, (LAT, ROWS), 0)
    column = lax.broadcasted_iota(jnp.int32, (LAT, ROWS), 1)
    lead = column - row
    scores = []
    for j, kv in enumerate(chunks):
        for half in range(2):
            keys = kv[pl.ds(half * ROWS, ROWS), pl.ds(0, HD)]
            part = lax.dot_general(queries, keys, (((1,), (1,)), ((), ())), preferred_element_type=F32)
            room = CTX - LAT - info[5 + 2 * j + half]
            scores.append(jnp.where(lead <= room, part, -jnp.inf))
    peak = functools.reduce(jnp.maximum, scores)
    peak = jnp.max(peak, axis=-1, keepdims=True)
    total = jnp.zeros((LAT, 1), F32)
    accum = jnp.zeros((LAT, HD), F32)
    for j, kv in enumerate(chunks):
        for half in range(2):
            expo = jnp.exp(scores[2 * j + half] - peak)
            total += jnp.sum(expo, axis=-1, keepdims=True)
            values = kv[pl.ds(half * ROWS, ROWS), pl.ds(HD, HD)]
            accum += jnp.dot(expo.astype(BF16), values, preferred_element_type=F32)
    lane = lax.broadcasted_iota(jnp.int32, (LAT, HD), 1)
    stats = jnp.where(lane < HD // 2, peak, total).reshape(LAT // 8, 8, HD)
    accum = accum.reshape(LAT // 8, 8, HD)
    upper = lax.broadcasted_iota(jnp.int32, (LAT // 8, 8, HD), 1) < MINE
    out[:, 0] = jnp.where(upper, accum, pltpu.roll(stats, MINE, 1))
    out[:, 1] = jnp.where(upper, pltpu.roll(accum, MINE, 1), stats)


def merge_kernel(parts, weight, out):
    lane = lax.broadcasted_iota(jnp.int32, (8, HD), 1) < HD // 2
    row = lax.broadcasted_iota(jnp.int32, (8, HD), 0) < MINE
    members = [[] for _ in range(HEADS)]
    for yl in range(2):
        for z in range(4):
            for x in range(4):
                for core in range(2):
                    members[head_of(yl, z, x, core)].append(((yl * 4 + z) * 4 + x) * 2 + core)
    heads = []
    for group in members:
        accums, peaks, totals = [], [], []
        for source in group:
            block = parts[source]
            stats = pltpu.roll(block, MINE, 0)
            turned = pltpu.roll(stats, HD // 2, 1)
            accums.append(block)
            peaks.append(jnp.where(lane, stats, turned))
            totals.append(jnp.where(lane, turned, stats))
        peak = functools.reduce(jnp.maximum, peaks)
        accum = jnp.zeros((8, HD), F32)
        total = jnp.zeros((8, HD), F32)
        for a, p, t in zip(accums, peaks, totals):
            factor = jnp.exp(p - peak)
            accum += a * factor
            total += t * factor
        heads.append(jnp.where(row, accum / total, 0.0).astype(BF16))
    attended = jnp.concatenate(heads, axis=1)
    result = jnp.dot(attended, weight[...], preferred_element_type=F32).astype(BF16)
    out[...] = result[:MINE]


def shape(*dims, dtype=BF16):
    return jax.ShapeDtypeStruct(dims, dtype)


def local(context, norm_gain, query_weight, key_weight, value_weight, out_weight):
    core = lax.axis_index("core")
    x = lax.axis_index("x")
    z = lax.axis_index("z")
    yl = lax.axis_index("yl")
    gain = norm_gain.reshape(1, D)

    chips = [(yl, z, x), (yl, z, x ^ 1), (yl, z ^ 1, x), (yl ^ 1, z, x)]
    info = [core]
    info += [head_of(b, c, a, core) for b, c, a in chips]
    for b, c, a in chips:
        for half in range(2):
            info.append((((b * 4 + c) * 4 + a) * 2 + (core ^ half)) * ROWS)
    info = jnp.stack(info).astype(jnp.int32)

    other_raw = lax.ppermute(context, "core", SWAP)
    own = pl.pallas_call(
        own_kernel,
        out_shape=shape(ROWS, D),
        in_specs=[VMEM, VMEM],
        out_specs=VMEM,
        compiler_params=params(16),
        cost_estimate=pl.CostEstimate(flops=2**23, bytes_accessed=2**21, transcendentals=0),
    )(context, gain)
    other, *queries = pl.pallas_call(
        query_kernel,
        out_shape=[shape(ROWS, D)] + [shape(LAT, HD)] * 4,
        in_specs=[SMEM, VMEM, VMEM, VMEM, ANY],
        out_specs=[VMEM] * 5,
        scratch_shapes=[pltpu.VMEM((D, 4 * HD), BF16), pltpu.SemaphoreType.DMA((4,))],
        compiler_params=params(24),
        cost_estimate=pl.CostEstimate(flops=2**29, bytes_accessed=2**22, transcendentals=0),
    )(info, other_raw, own, gain, query_weight)

    def hop(value, dx, dz, dy):
        pairs = []
        for b in range(2):
            for c in range(4):
                for a in range(4):
                    pairs.append(((b * 4 + c) * 4 + a, ((b ^ dy) * 4 + (c ^ dz)) * 4 + (a ^ dx)))
        return lax.ppermute(value, ("yl", "z", "x"), pairs)

    dx1, dx3, dz1, dz3, dy = near(x), (x >> 1) ^ 1, near(z), (z >> 1) ^ 1, yl ^ 1
    by_x = hop(queries[1], 1, 0, 0)
    by_z = hop(queries[2], 0, 1, 0)
    by_y = hop(queries[3], 0, 0, 1)

    kv = pl.pallas_call(
        kv_kernel,
        out_shape=[shape(2 * ROWS, 2 * HD)] * 4,
        in_specs=[SMEM, VMEM, VMEM, ANY, ANY],
        out_specs=[VMEM] * 4,
        scratch_shapes=[pltpu.VMEM((4, D, 2 * HD), BF16), pltpu.SemaphoreType.DMA((4, 2))],
        compiler_params=params(24),
        cost_estimate=pl.CostEstimate(flops=2**31, bytes_accessed=2**23, transcendentals=0),
    )(info, own, other, key_weight, value_weight)

    query = jnp.where(dx1 == 1, by_x, jnp.where(dz1 == 1, by_z, jnp.where(dy == 1, by_y, queries[0])))
    far_x, far_z, far_xz = hop(query, 3, 0, 0), hop(query, 0, 3, 0), hop(query, 3, 3, 0)
    kv_x = hop(kv[1], 1, 0, 0)
    kv_z = hop(kv[2], 0, 1, 0)
    kv_y = hop(kv[3], 0, 0, 1)
    query = jnp.where(
        dx3 == 1, jnp.where(dz3 == 1, far_xz, far_x), jnp.where(dz3 == 1, far_z, query)
    )
    across = hop(query, 1, 1, 1)
    query = jnp.where(dx1 + dz1 + dy >= 2, across, query)

    parts = pl.pallas_call(
        attend_kernel,
        out_shape=shape(LAT // 8, 2, 8, HD, dtype=F32),
        in_specs=[SMEM] + [VMEM] * 5,
        out_specs=VMEM,
        compiler_params=params(24),
        cost_estimate=pl.CostEstimate(flops=2**28, bytes_accessed=2**21, transcendentals=2**19),
    )(info, query, kv[0], kv_x, kv_z, kv_y)
    parts = lax.all_to_all(parts.reshape(64, 8, HD), CTX_AXES, 0, 0)
    return pl.pallas_call(
        merge_kernel,
        out_shape=shape(MINE, D),
        in_specs=[VMEM, VMEM],
        out_specs=VMEM,
        compiler_params=params(24),
        cost_estimate=pl.CostEstimate(flops=2**25, bytes_accessed=2**22, transcendentals=2**16),
    )(parts, out_weight)


def solution(mesh):
    fine = Mesh(mesh.devices.reshape(2, 4, 4, 2, 2), CTX_AXES + ("batch",))
    rows = P(("batch",) + CTX_AXES, None)
    return jax.shard_map(
        local,
        mesh=fine,
        in_specs=(rows, P(), P(), P(), P(), P()),
        out_specs=rows,
        check_vma=False,
    )
```

time: 1190 us -> 70.1 us (0.06)
  waiting for transfers between devices: 748 us -> 11.1 us
  other arithmetic: 143 us -> 0.04 us
  blocking collectives: 162 us -> 19.2 us
  local copies, waits for them, and re-layouts: 107 us -> 11.4 us
  matrix products: 15 us -> 0 us
  starting transfers between devices: 0.04 us -> 14.9 us
  between operations: 13.5 us -> 0.1 us
  Pallas kernels: 0 us -> 13 us
    psum x1 -> x0, waiting for transfers between devices: 543 us -> none  [spread(): return lax.psum(block, axis)]
    all_gather x1 -> x0, waiting for transfers between devices: 205 us -> none  [merged_2(): pieces = jax.tree.map(lambda part: lax.all_gather(part, axis), value)]
    all_gather x2 -> x0, blocking collectives: 162 us -> none  [merged_2(): pieces = jax.tree.map(lambda part: lax.all_gather(part, axis), value)]
    add x127 -> x0, other arithmetic: 137 us -> none  [the longest x63 136 us: combine(): scale_heads(first[2], weight_first) + scale_heads(second[2], weight_second)]
    slice x5 -> x0, local copies, waits for them, and re-layouts: 43.8 us -> none  [the longest x3 43.8 us: merged_2(): tail = jax.tree.map(lambda part: part[1:], pieces)]
    mul x126 -> x0, local copies, waits for them, and re-layouts: 42.2 us -> none  [scale_heads(): return (shaped * factor[:, :, None]).reshape(accum.shape)]
    all_to_all x0 -> x1, blocking collectives: none -> 19.2 us  [local(): parts = lax.all_to_all(parts.reshape(64, 8, HD), CTX_AXES, 0, 0)]
    exp x126 -> x0, local copies, waits for them, and re-layouts: 15.7 us -> none  [the longest x63 7.99 us: combine(): weight_first = jnp.exp(first[0] - peak)]
  transfers between devices with their start and end apart: 2 -> 11, of which waited for: 2 -> 6; matrix products, arithmetic and copies ran while one was open for 1% -> 0% of each run, Pallas kernels for 0% -> 9%
where the time goes in v1:
time: 70.1 us; the launch traced here: 69.7 us
  blocking collectives  19.2 us (27%)
  starting transfers between devices  14.9 us (21%)
  Pallas kernels  13 us (19%)
  local copies, waits for them, and re-layouts  11.4 us (16%)
  waiting for transfers between devices  11.1 us (16%)
    all_to_all x1, blocking collectives, local(): parts = lax.all_to_all(parts.reshape(64, 8, HD), CTX_AXES, 0, 0)  19.2 us
    ppermute x10, starting transfers between devices, hop(): return lax.ppermute(value, ('yl', 'z', 'x'), pairs)  13.4 us
    unnamed x14, local copies, waits for them, and re-layouts  11.4 us
    ppermute x10, waiting for transfers between devices, hop(): return lax.ppermute(value, ('yl', 'z', 'x'), pairs)  11.1 us
    pallas_call x1, Pallas kernels, local(): pl.pallas_call(kv_kernel, out_shape=[shape(2 * ROWS, 2 * HD)] * 4, in_spe...  4.56 us
    pallas_call x1, Pallas kernels, local(): pl.pallas_call(query_kernel, out_shape=[shape(ROWS, D)] + [shape(LAT, HD)...  3.66 us
    pallas_call x1, Pallas kernels, local(): pl.pallas_call(own_kernel, out_shape=shape(ROWS, D), in_specs=[VMEM, VMEM...  1.8 us
    pallas_call x1, Pallas kernels, local(): pl.pallas_call(attend_kernel, out_shape=shape(LAT // 8, 2, 8, HD, dtype=F...  1.6 us
  transfers between devices with their start and end apart: 11, of which 6 were waited for; matrix products, arithmetic and copies ran while one was open for 0% of the time, Pallas kernels for 9%

profile of v1, /device:TPU:1, one launch (start us, length us, event | category | flops | bytes accessed | tf_op | source)
XLA Modules:
  0.0 69.7 jit_solution(4284089849741070452)
XLA Ops:
  0.0 1.4 %collective-permute-start = (bf16[256,2048]{1,0:T(8,128)(2,1)}, bf16[256,2048]{1,0:T(8,128)(2,1)S(1)}, u32[]{:S(2)}, u32[]{:S(2)}) collective-permute-start(bf16[256,2048]{1,0:T(8,128)(2,1)} %tokens.1), channel_id=1, source_target_pairs={{0,2},{2,0},{1,3},{3,1},{4,6},{6,4},{5,7},{7,5},{8,10},{10,8},{9,1... | collective-permute-start | bytes 3145736 | tf_op jit(solution)/shard_map/ppermute | solution.py:190
  1.4 0.1 stack.55.info
  1.5 0.0 copy-start.4
  1.5 1.2 %copy-done.4 = bf16[256,2048]{1,0:T(8,128)(2,1)S(1)} copy-done((bf16[256,2048]{1,0:T(8,128)(2,1)S(1)}, bf16[256,2048]{1,0:T(8,128)(2,1)}, u32[]{:S(2)}) %copy-start.4) | copy-done | bytes 1048600
  2.7 0.0 copy-start.5
  2.7 0.7 copy-done.5
  3.4 1.8 %shard_map.64.own = bf16[256,2048]{1,0:T(8,128)(2,1)S(1)} custom-call(bf16[256,2048]{1,0:T(8,128)(2,1)S(1)} %copy-done.4, f32[1,2048]{1,0:T(1,128)S(1)} %bitcast.16), custom_call_target="tpu_custom_call" | custom-call | flops 8388608 | bytes 2097152 | tf_op jit(solution)/shard_map/pallas_call | solution.py:191
  5.2 0.0 collective-permute-done.tokens
  5.3 0.0 copy-start
  5.3 2.2 %copy-done = bf16[2048,1024]{1,0:T(8,128)(2,1)S(1)} copy-done((bf16[2048,1024]{1,0:T(8,128)(2,1)S(1)}, bf16[2048,1024]{1,0:T(8,128)(2,1)}, u32[]{:S(2)}) %copy-start) | copy-done | bytes 4194328
  7.4 0.0 copy-start.6
  7.4 0.7 copy-done.6
  8.1 3.7 %shard_map.65 = (bf16[256,2048]{1,0:T(8,128)(2,1)S(1)}, bf16[256,128]{1,0:T(8,128)(2,1)S(1)}, bf16[256,128]{1,0:T(8,128)(2,1)S(1)}, bf16[256,128]{1,0:T(8,128)(2,1)S(1)}, bf16[256,128]{1,0:T(8,128)(2,1)S(1)}) custom-call(s32[13]{0:T(128)S(1)} %stack.55.info, bf16[256,2048]{1,0:T(8,128)(2,1)S(1)} %collective-permute-done.tokens, ...), custom_call_target="tpu_custom_call" | custom-call | flops 536870912 | bytes 4194304 | tf_op jit(solution)/shard_map/pallas_call | solution.py:199
  11.8 1.4 %collective-permute-start.1 = (bf16[256,128]{1,0:T(8,128)(2,1)S(1)}, bf16[256,128]{1,0:T(8,128)(2,1)S(1)}, u32[]{:S(2)}, u32[]{:S(2)}) collective-permute-start(bf16[256,128]{1,0:T(8,128)(2,1)S(1)} %get-tuple-element.14), channel_id=1, source_target_pairs={{0,4},{4,0},{8,12},{12,8},{16,20},{20,16},{24,28},{28,24},{32,36},... | collective-permute-start | bytes 196616 | tf_op jit(solution)/shard_map/ppermute | solution.py:215
  13.2 1.6 %collective-permute-start.2 = (bf16[256,128]{1,0:T(8,128)(2,1)S(1)}, bf16[256,128]{1,0:T(8,128)(2,1)S(1)}, u32[]{:S(2)}, u32[]{:S(2)}) collective-permute-start(bf16[256,128]{1,0:T(8,128)(2,1)S(1)} %get-tuple-element.15), channel_id=1, source_target_pairs={{0,16},{4,20},{8,24},{12,28},{16,0},{20,4},{24,8},{28,12},{32,48},... | collective-permute-start | bytes 196616 | tf_op jit(solution)/shard_map/ppermute | solution.py:215
  14.8 1.3 %collective-permute-start.3 = (bf16[256,128]{1,0:T(8,128)(2,1)S(1)}, bf16[256,128]{1,0:T(8,128)(2,1)S(1)}, u32[]{:S(2)}, u32[]{:S(2)}) collective-permute-start(bf16[256,128]{1,0:T(8,128)(2,1)S(1)} %get-tuple-element.16), channel_id=1, source_target_pairs={{0,64},{4,68},{8,72},{12,76},{16,80},{20,84},{24,88},{28,92},{32,9... | collective-permute-start | bytes 196616 | tf_op jit(solution)/shard_map/ppermute | solution.py:215
  16.1 0.0 collective-permute-done.1
  16.1 0.8 %collective-permute-done.2 = bf16[256,128]{1,0:T(8,128)(2,1)S(1)} collective-permute-done((bf16[256,128]{1,0:T(8,128)(2,1)S(1)}, bf16[256,128]{1,0:T(8,128)(2,1)S(1)}, u32[]{:S(2)}, u32[]{:S(2)}) %collective-permute-start.2) | collective-permute-done | bytes 65568 | tf_op jit(solution)/shard_map/ppermute | solution.py:215
  17.0 1.0 %collective-permute-done.3 = bf16[256,128]{1,0:T(8,128)(2,1)S(1)} collective-permute-done((bf16[256,128]{1,0:T(8,128)(2,1)S(1)}, bf16[256,128]{1,0:T(8,128)(2,1)S(1)}, u32[]{:S(2)}, u32[]{:S(2)}) %collective-permute-start.3) | collective-permute-done | bytes 65568 | tf_op jit(solution)/shard_map/ppermute | solution.py:215
  18.0 2.6 %collective-permute-start.6 = (bf16[256,128]{1,0:T(8,128)(2,1)S(1)}, bf16[256,128]{1,0:T(8,128)(2,1)S(1)}, u32[]{:S(2)}, u32[]{:S(2)}) collective-permute-start(bf16[256,128]{1,0:T(8,128)(2,1)S(1)} %select_select_fusion.1), channel_id=1, source_target_pairs={{0,48},{4,52},{8,56},{12,60},{16,32},{20,36},{24,40},{28,44},{32,1... | collective-permute-start | bytes 196616 | tf_op jit(solution)/shard_map/ppermute | solution.py:215
  20.6 1.7 %collective-permute-start.4 = (bf16[256,128]{1,0:T(8,128)(2,1)S(1)}, bf16[256,128]{1,0:T(8,128)(2,1)S(1)}, u32[]{:S(2)}, u32[]{:S(2)}) collective-permute-start(bf16[256,128]{1,0:T(8,128)(2,1)S(1)} %select_select_fusion.1), channel_id=1, source_target_pairs={{0,60},{4,56},{8,52},{12,48},{16,44},{20,40},{24,36},{28,32},{32,2... | collective-permute-start | bytes 196616 | tf_op jit(solution)/shard_map/ppermute | solution.py:215
  22.2 0.9 %collective-permute-start.5 = (bf16[256,128]{1,0:T(8,128)(2,1)S(1)}, bf16[256,128]{1,0:T(8,128)(2,1)S(1)}, u32[]{:S(2)}, u32[]{:S(2)}) collective-permute-start(bf16[256,128]{1,0:T(8,128)(2,1)S(1)} %select_select_fusion.1), channel_id=1, source_target_pairs={{0,12},{4,8},{8,4},{12,0},{16,28},{20,24},{24,20},{28,16},{32,44},... | collective-permute-start | bytes 196616 | tf_op jit(solution)/shard_map/ppermute | solution.py:215
  23.1 0.0 collective-permute-done.6
  23.1 3.9 %collective-permute-done.4 = bf16[256,128]{1,0:T(8,128)(2,1)S(1)} collective-permute-done((bf16[256,128]{1,0:T(8,128)(2,1)S(1)}, bf16[256,128]{1,0:T(8,128)(2,1)S(1)}, u32[]{:S(2)}, u32[]{:S(2)}) %collective-permute-start.4) | collective-permute-done | bytes 65568 | tf_op jit(solution)/shard_map/ppermute | solution.py:215
  27.0 0.0 collective-permute-done.5
  27.0 0.1 collective-permute-start.7
  27.1 0.0 copy-start.1
  27.1 2.2 %copy-done.1 = bf16[2048,1024]{1,0:T(8,128)(2,1)S(1)} copy-done((bf16[2048,1024]{1,0:T(8,128)(2,1)S(1)}, bf16[2048,1024]{1,0:T(8,128)(2,1)}, u32[]{:S(2)}) %copy-start.1) | copy-done | bytes 4194328
  29.3 0.0 copy-start.2
  29.3 2.2 %copy-done.2 = bf16[2048,1024]{1,0:T(8,128)(2,1)S(1)} copy-done((bf16[2048,1024]{1,0:T(8,128)(2,1)S(1)}, bf16[2048,1024]{1,0:T(8,128)(2,1)}, u32[]{:S(2)}) %copy-start.2) | copy-done | bytes 4194328
  31.5 4.6 %shard_map.66 = (bf16[512,256]{1,0:T(8,128)(2,1)S(1)}, bf16[512,256]{1,0:T(8,128)(2,1)S(1)}, bf16[512,256]{1,0:T(8,128)(2,1)S(1)}, bf16[512,256]{1,0:T(8,128)(2,1)S(1)}) custom-call(s32[13]{0:T(128)S(1)} %stack.55.info, bf16[256,2048]{1,0:T(8,128)(2,1)S(1)} %shard_map.64.own, bf16[256,2048]{1,0:T(8,128)(2,1)S(1)} %get-tuple-element.18.other, ...), custom_call_target="tpu_custom_call" | custom-call | flops 2147483648 | bytes 8388608 | tf_op jit(solution)/shard_map/pallas_call | solution.py:222
  36.1 2.6 %collective-permute-start.8 = (bf16[512,256]{1,0:T(8,128)(2,1)S(1)}, bf16[512,256]{1,0:T(8,128)(2,1)S(1)}, u32[]{:S(2)}, u32[]{:S(2)}) collective-permute-start(bf16[512,256]{1,0:T(8,128)(2,1)S(1)} %get-tuple-element.20), channel_id=1, source_target_pairs={{0,4},{4,0},{8,12},{12,8},{16,20},{20,16},{24,28},{28,24},{32,36},... | collective-permute-start | bytes 786440 | tf_op jit(solution)/shard_map/ppermute | solution.py:215
  38.7 1.1 %collective-permute-start.9 = (bf16[512,256]{1,0:T(8,128)(2,1)S(1)}, bf16[512,256]{1,0:T(8,128)(2,1)S(1)}, u32[]{:S(2)}, u32[]{:S(2)}) collective-permute-start(bf16[512,256]{1,0:T(8,128)(2,1)S(1)} %get-tuple-element.21), channel_id=1, source_target_pairs={{0,16},{4,20},{8,24},{12,28},{16,0},{20,4},{24,8},{28,12},{32,48},... | collective-permute-start | bytes 786440 | tf_op jit(solution)/shard_map/ppermute | solution.py:215
  39.8 0.2 collective-permute-start.10
  40.0 0.0 collective-permute-done.7
  40.0 2.5 %collective-permute-done.8.kv1 = bf16[512,256]{1,0:T(8,128)(2,1)S(1)} collective-permute-done((bf16[512,256]{1,0:T(8,128)(2,1)S(1)}, bf16[512,256]{1,0:T(8,128)(2,1)S(1)}, u32[]{:S(2)}, u32[]{:S(2)}) %collective-permute-start.8) | collective-permute-done | bytes 262176 | tf_op jit(solution)/shard_map/ppermute | solution.py:215
  42.5 1.8 %collective-permute-done.9.kv2 = bf16[512,256]{1,0:T(8,128)(2,1)S(1)} collective-permute-done((bf16[512,256]{1,0:T(8,128)(2,1)S(1)}, bf16[512,256]{1,0:T(8,128)(2,1)S(1)}, u32[]{:S(2)}, u32[]{:S(2)}) %collective-permute-start.9) | collective-permute-done | bytes 262176 | tf_op jit(solution)/shard_map/ppermute | solution.py:215
  44.2 1.1 %collective-permute-done.10.kv3 = bf16[512,256]{1,0:T(8,128)(2,1)S(1)} collective-permute-done((bf16[512,256]{1,0:T(8,128)(2,1)S(1)}, bf16[512,256]{1,0:T(8,128)(2,1)S(1)}, u32[]{:S(2)}, u32[]{:S(2)}) %collective-permute-start.10) | collective-permute-done | bytes 262176 | tf_op jit(solution)/shard_map/ppermute | solution.py:215
  45.3 1.6 %shard_map.67 = f32[32,2,8,128]{3,2,1,0:T(8,128)S(1)} custom-call(s32[13]{0:T(128)S(1)} %stack.55.info, bf16[256,128]{1,0:T(8,128)(2,1)S(1)} %broadcast_select_fusion.query, bf16[512,256]{1,0:T(8,128)(2,1)S(1)} %get-tuple-element.19.kv0, bf16[512,256]{1,0:T(8,128)(2,1)S(1)} %collective-permute-done.8.kv1, bf16[512,256]{1,0:T(8,128)(2,1)S(1)} %collective-permute-done.9.kv2, ...), custom_call_target="tpu_custom_call" | custom-call | flops 268435456 | bytes 2097152 | tf_op jit(solution)/shard_map/pallas_call | solution.py:243
  46.9 19.2 %all_to_all.5.parts = f32[64,8,128]{2,1,0:T(8,128)S(1)} all-to-all(f32[64,8,128]{2,1,0:T(8,128)S(1)} %bitcast.15), channel_id=1, replica_groups=mesh['yl'=2,'z'=4,'x'=4,'core'=2,'batch'=2] {'yl','z','x','core'}, dimensions={0} | all-to-all | bytes 524288 | tf_op jit(solution)/shard_map/all_to_all | solution.py:251
  66.2 0.0 copy-start.3
  66.2 2.2 %copy-done.3 = bf16[1024,2048]{1,0:T(8,128)(2,1)S(1)} copy-done((bf16[1024,2048]{1,0:T(8,128)(2,1)S(1)}, bf16[1024,2048]{1,0:T(8,128)(2,1)}, u32[]{:S(2)}) %copy-start.3) | copy-done | bytes 4194328
  68.3 1.4 %shard_map.68 = bf16[4,2048]{1,0:T(4,128)(2,1)} custom-call(f32[64,8,128]{2,1,0:T(8,128)S(1)} %all_to_all.5.parts, bf16[1024,2048]{1,0:T(8,128)(2,1)S(1)} %copy-done.3), custom_call_target="tpu_custom_call" | custom-call | flops 33554432 | bytes 4194304 | tf_op jit(solution)/shard_map/pallas_call | solution.py:252
  (3 shorter events, 0.0 us)
Async XLA Ops:
  0.0 5.2 %collective-permute-start = (bf16[256,2048]{1,0:T(8,128)(2,1)}, bf16[256,2048]{1,0:T(8,128)(2,1)S(1)}, u32[]{:S(2)}, u32[]{:S(2)}) collective-permute-start(bf16[256,2048]{1,0:T(8,128)(2,1)} %tokens.1), channel_id=1, source_target_pairs={{0,2},{2,0},{1,3},{3,1},{4,6},{6,4},{5,7},{7,5},{8,10},{10,8},{9,1... | collective-permute-start | bytes 3145736 | tf_op jit(solution)/shard_map/ppermute | solution.py:190
  1.5 1.2 %copy-start.4 = (bf16[256,2048]{1,0:T(8,128)(2,1)S(1)}, bf16[256,2048]{1,0:T(8,128)(2,1)}, u32[]{:S(2)}) copy-start(bf16[256,2048]{1,0:T(8,128)(2,1)} %tokens.1) | copy-start | bytes 3145732
  2.7 0.7 copy-start.5
  5.3 2.2 %copy-start = (bf16[2048,1024]{1,0:T(8,128)(2,1)S(1)}, bf16[2048,1024]{1,0:T(8,128)(2,1)}, u32[]{:S(2)}) copy-start(bf16[2048,1024]{1,0:T(8,128)(2,1)} %weight.2) | copy-start | bytes 12582916
  7.4 0.7 copy-start.6
  11.8 4.3 %collective-permute-start.1 = (bf16[256,128]{1,0:T(8,128)(2,1)S(1)}, bf16[256,128]{1,0:T(8,128)(2,1)S(1)}, u32[]{:S(2)}, u32[]{:S(2)}) collective-permute-start(bf16[256,128]{1,0:T(8,128)(2,1)S(1)} %get-tuple-element.14), channel_id=1, source_target_pairs={{0,4},{4,0},{8,12},{12,8},{16,20},{20,16},{24,28},{28,24},{32,36},... | collective-permute-start | bytes 196616 | tf_op jit(solution)/shard_map/ppermute | solution.py:215
  13.2 3.8 %collective-permute-start.2 = (bf16[256,128]{1,0:T(8,128)(2,1)S(1)}, bf16[256,128]{1,0:T(8,128)(2,1)S(1)}, u32[]{:S(2)}, u32[]{:S(2)}) collective-permute-start(bf16[256,128]{1,0:T(8,128)(2,1)S(1)} %get-tuple-element.15), channel_id=1, source_target_pairs={{0,16},{4,20},{8,24},{12,28},{16,0},{20,4},{24,8},{28,12},{32,48},... | collective-permute-start | bytes 196616 | tf_op jit(solution)/shard_map/ppermute | solution.py:215
  14.8 3.1 %collective-permute-start.3 = (bf16[256,128]{1,0:T(8,128)(2,1)S(1)}, bf16[256,128]{1,0:T(8,128)(2,1)S(1)}, u32[]{:S(2)}, u32[]{:S(2)}) collective-permute-start(bf16[256,128]{1,0:T(8,128)(2,1)S(1)} %get-tuple-element.16), channel_id=1, source_target_pairs={{0,64},{4,68},{8,72},{12,76},{16,80},{20,84},{24,88},{28,92},{32,9... | collective-permute-start | bytes 196616 | tf_op jit(solution)/shard_map/ppermute | solution.py:215
  18.0 5.2 %collective-permute-start.6 = (bf16[256,128]{1,0:T(8,128)(2,1)S(1)}, bf16[256,128]{1,0:T(8,128)(2,1)S(1)}, u32[]{:S(2)}, u32[]{:S(2)}) collective-permute-start(bf16[256,128]{1,0:T(8,128)(2,1)S(1)} %select_select_fusion.1), channel_id=1, source_target_pairs={{0,48},{4,52},{8,56},{12,60},{16,32},{20,36},{24,40},{28,44},{32,1... | collective-permute-start | bytes 196616 | tf_op jit(solution)/shard_map/ppermute | solution.py:215
  20.6 6.4 %collective-permute-start.4 = (bf16[256,128]{1,0:T(8,128)(2,1)S(1)}, bf16[256,128]{1,0:T(8,128)(2,1)S(1)}, u32[]{:S(2)}, u32[]{:S(2)}) collective-permute-start(bf16[256,128]{1,0:T(8,128)(2,1)S(1)} %select_select_fusion.1), channel_id=1, source_target_pairs={{0,60},{4,56},{8,52},{12,48},{16,44},{20,40},{24,36},{28,32},{32,2... | collective-permute-start | bytes 196616 | tf_op jit(solution)/shard_map/ppermute | solution.py:215
  22.2 4.8 %collective-permute-start.5 = (bf16[256,128]{1,0:T(8,128)(2,1)S(1)}, bf16[256,128]{1,0:T(8,128)(2,1)S(1)}, u32[]{:S(2)}, u32[]{:S(2)}) collective-permute-start(bf16[256,128]{1,0:T(8,128)(2,1)S(1)} %select_select_fusion.1), channel_id=1, source_target_pairs={{0,12},{4,8},{8,4},{12,0},{16,28},{20,24},{24,20},{28,16},{32,44},... | collective-permute-start | bytes 196616 | tf_op jit(solution)/shard_map/ppermute | solution.py:215
  27.0 12.9 %collective-permute-start.7 = (bf16[256,128]{1,0:T(8,128)(2,1)S(1)}, bf16[256,128]{1,0:T(8,128)(2,1)S(1)}, u32[]{:S(2)}, u32[]{:S(2)}) collective-permute-start(bf16[256,128]{1,0:T(8,128)(2,1)S(1)} %select_select_fusion), channel_id=1, source_target_pairs={{0,84},{4,80},{8,92},{12,88},{16,68},{20,64},{24,76},{28,72},{32,1... | collective-permute-start | bytes 196616 | tf_op jit(solution)/shard_map/ppermute | solution.py:215
  27.1 2.2 %copy-start.1 = (bf16[2048,1024]{1,0:T(8,128)(2,1)S(1)}, bf16[2048,1024]{1,0:T(8,128)(2,1)}, u32[]{:S(2)}) copy-start(bf16[2048,1024]{1,0:T(8,128)(2,1)} %wk.1) | copy-start | bytes 12582916
  29.3 2.2 %copy-start.2 = (bf16[2048,1024]{1,0:T(8,128)(2,1)S(1)}, bf16[2048,1024]{1,0:T(8,128)(2,1)}, u32[]{:S(2)}) copy-start(bf16[2048,1024]{1,0:T(8,128)(2,1)} %wv.1) | copy-start | bytes 12582916
  36.1 6.4 %collective-permute-start.8 = (bf16[512,256]{1,0:T(8,128)(2,1)S(1)}, bf16[512,256]{1,0:T(8,128)(2,1)S(1)}, u32[]{:S(2)}, u32[]{:S(2)}) collective-permute-start(bf16[512,256]{1,0:T(8,128)(2,1)S(1)} %get-tuple-element.20), channel_id=1, source_target_pairs={{0,4},{4,0},{8,12},{12,8},{16,20},{20,16},{24,28},{28,24},{32,36},... | collective-permute-start | bytes 786440 | tf_op jit(solution)/shard_map/ppermute | solution.py:215
  38.7 5.5 %collective-permute-start.9 = (bf16[512,256]{1,0:T(8,128)(2,1)S(1)}, bf16[512,256]{1,0:T(8,128)(2,1)S(1)}, u32[]{:S(2)}, u32[]{:S(2)}) collective-permute-start(bf16[512,256]{1,0:T(8,128)(2,1)S(1)} %get-tuple-element.21), channel_id=1, source_target_pairs={{0,16},{4,20},{8,24},{12,28},{16,0},{20,4},{24,8},{28,12},{32,48},... | collective-permute-start | bytes 786440 | tf_op jit(solution)/shard_map/ppermute | solution.py:215
  39.8 5.5 %collective-permute-start.10 = (bf16[512,256]{1,0:T(8,128)(2,1)S(1)}, bf16[512,256]{1,0:T(8,128)(2,1)S(1)}, u32[]{:S(2)}, u32[]{:S(2)}) collective-permute-start(bf16[512,256]{1,0:T(8,128)(2,1)S(1)} %get-tuple-element.22), channel_id=1, source_target_pairs={{0,64},{4,68},{8,72},{12,76},{16,80},{20,84},{24,88},{28,92},{32,9... | collective-permute-start | bytes 786440 | tf_op jit(solution)/shard_map/ppermute | solution.py:215
  66.2 2.2 %copy-start.3 = (bf16[1024,2048]{1,0:T(8,128)(2,1)S(1)}, bf16[1024,2048]{1,0:T(8,128)(2,1)}, u32[]{:S(2)}) copy-start(bf16[1024,2048]{1,0:T(8,128)(2,1)} %weight.3) | copy-start | bytes 12582916

commit v2 on v1

v2 whole, which is shorter than its diff:
```python
import functools

import jax
import jax.numpy as jnp
from jax import lax
from jax.experimental import pallas as pl
from jax.experimental.pallas import tpu as pltpu
from jax.sharding import Mesh
from jax.sharding import PartitionSpec as P

HEADS = 8
HD = 128
D = 2048
LAT = 256
ROWS = 256
CTX = 16384
MINE = 4
FETCHED = 2
F32 = jnp.float32
BF16 = jnp.bfloat16
CTX_AXES = ("yl", "z", "xh", "xl", "core")
SWAP = ((0, 1), (1, 0))
HBM = pl.BlockSpec(memory_space=pltpu.HBM)
VMEM = pl.BlockSpec(memory_space=pltpu.VMEM)
SMEM = pl.BlockSpec(memory_space=pltpu.SMEM)


def near(i):
    return (i ^ (i >> 1)) & 1


def head_of(yl, z, x, core):
    return core * 4 + near(x) * 2 + yl


def params(mib):
    return pltpu.CompilerParams(vmem_limit_bytes=mib * 2**20)


def normalise(tokens, gain):
    widened = tokens.astype(F32)
    centred = widened - jnp.mean(widened, axis=-1, keepdims=True)
    variance = jnp.mean(centred * centred, axis=-1, keepdims=True)
    return (centred * lax.rsqrt(variance + 1e-05) * gain).astype(BF16)


def fetch_heads(weight, heads, dst, offset, sem):
    at = pl.ds(pl.multiple_of(heads * HD, HD), HD)
    copy = pltpu.make_async_copy(weight.at[:, at], dst.at[:, pl.ds(offset, HD)], sem)
    copy.start()
    return copy


def own_kernel(info, tokens, gain_ref, wq, wk, wv, out, columns, gain, kv_columns, rows, sems):
    first = pltpu.make_async_copy(tokens, rows, sems.at[12])
    first.start()
    second = pltpu.make_async_copy(gain_ref, gain, sems.at[13])
    second.start()
    copies = [fetch_heads(wq, info[1 + j], columns, j * HD, sems.at[j]) for j in range(4)]
    for j in range(4):
        for k, weight in enumerate((wk, wv)):
            copies.append(
                fetch_heads(weight, info[1 + j], kv_columns, (2 * j + k) * HD, sems.at[4 + 2 * j + k])
            )
    first.wait()
    second.wait()
    out[...] = normalise(rows[...], gain[...])
    for copy in copies:
        copy.wait()


def query_kernel(info, tokens, own, gain, weight, out, q0, q1, q2, q3):
    out[...] = normalise(tokens[...], gain[...])
    latents = jnp.where(info[0] == 1, own[...], out[...])
    queries = jnp.dot(latents, weight[...], preferred_element_type=F32) * HD ** (-0.5)
    queries = queries.astype(BF16)
    for j, q in enumerate((q0, q1, q2, q3)):
        q[...] = queries[:, j * HD : (j + 1) * HD]


def kv_kernel(own, other, weight, out, done, sems):
    writes = []
    for k, rows in enumerate((own, other)):
        at = pl.ds(k * ROWS, ROWS)
        projected = jnp.dot(rows[...], weight[...], preferred_element_type=F32).astype(BF16)
        for j in range(4):
            done[j, at, :] = projected[:, j * 2 * HD : (j + 1) * 2 * HD]
        writes.append(pltpu.make_async_copy(done.at[:, at], out.at[:, at], sems.at[k]))
        writes[-1].start()
    for write in writes:
        write.wait()


def fetch_kernel(wo, *rest):
    *pieces, sems = rest
    copies = []
    for j, piece in enumerate(pieces):
        copies.append(pltpu.make_async_copy(wo.at[pl.ds(j * 2 * HD, 2 * HD)], piece, sems.at[j]))
        copies[-1].start()
    for copy in copies:
        copy.wait()


def thirds(value):
    first = value.astype(BF16).astype(F32)
    second = (value - first).astype(BF16).astype(F32)
    return [first, second, value - first - second]


def attend_kernel(info, query, kv, out):
    queries = query[...]
    row = lax.broadcasted_iota(jnp.int32, (LAT, ROWS), 0)
    column = lax.broadcasted_iota(jnp.int32, (LAT, ROWS), 1)
    lead = column - row
    scores = []
    for j in range(4):
        for half in range(2):
            keys = kv[j, pl.ds(half * ROWS, ROWS), pl.ds(0, HD)]
            part = lax.dot_general(queries, keys, (((1,), (1,)), ((), ())), preferred_element_type=F32)
            room = CTX - LAT - info[5 + 2 * j + half]
            scores.append(jnp.where(lead <= room, part, -jnp.inf))
    peak = functools.reduce(jnp.maximum, scores)
    peak = jnp.max(peak, axis=-1, keepdims=True)
    total = jnp.zeros((LAT, 1), F32)
    accum = jnp.zeros((LAT, HD), F32)
    for j in range(4):
        for half in range(2):
            expo = jnp.exp(scores[2 * j + half] - peak)
            total += jnp.sum(expo, axis=-1, keepdims=True)
            values = kv[j, pl.ds(half * ROWS, ROWS), pl.ds(HD, HD)]
            accum += jnp.dot(expo.astype(BF16), values, preferred_element_type=F32)
    lane = lax.broadcasted_iota(jnp.int32, (LAT, HD), 1)
    stats = jnp.zeros((LAT, HD), F32)
    for k, piece in enumerate(thirds(peak) + thirds(total)):
        stats = jnp.where(lane == k, piece, stats)
    stats = stats.reshape(LAT // 8, 8, HD)
    accum = accum.reshape(LAT // 8, 8, HD)
    upper = lax.broadcasted_iota(jnp.int32, (LAT // 8, 8, HD), 1) < MINE
    out[:, 0] = jnp.where(upper, accum, pltpu.roll(stats, MINE, 1)).astype(BF16)
    out[:, 1] = jnp.where(upper, pltpu.roll(accum, MINE, 1), stats).astype(BF16)


def merge_kernel(parts, weight, *rest):
    *pieces, out, wbuf, sems = rest
    copies = []
    for j in range(4 - FETCHED):
        at = pl.ds((FETCHED + j) * 2 * HD, 2 * HD)
        copies.append(pltpu.make_async_copy(weight.at[at], wbuf.at[j], sems.at[j]))
        copies[-1].start()
    row = lax.broadcasted_iota(jnp.int32, (8, HD), 0) < MINE
    k = lax.broadcasted_iota(jnp.int32, (HD, 2 * HD), 0)
    n = lax.broadcasted_iota(jnp.int32, (HD, 2 * HD), 1)
    lead = k - jnp.where(n < HD, 0, 3)
    pick = jnp.where((lead >= 0) & (lead < 3), 1.0, 0.0).astype(BF16)
    stats = jnp.dot(parts[...].reshape(8 * 64, HD), pick, preferred_element_type=F32)
    stats = stats.reshape(64, 8, 2 * HD)
    members = [[] for _ in range(HEADS)]
    for yl in range(2):
        for z in range(4):
            for x in range(4):
                for core in range(2):
                    members[head_of(yl, z, x, core)].append(((yl * 4 + z) * 4 + x) * 2 + core)
    heads = []
    for group in members:
        accums, peaks, totals = [], [], []
        for source in group:
            block = pltpu.roll(stats[source], MINE, 0)
            accums.append(parts[source].astype(F32))
            peaks.append(block[:, :HD])
            totals.append(block[:, HD:])
        peak = functools.reduce(jnp.maximum, peaks)
        accum = jnp.zeros((8, HD), F32)
        total = jnp.zeros((8, HD), F32)
        for a, p, t in zip(accums, peaks, totals):
            factor = jnp.exp(p - peak)
            accum += a * factor
            total += t * factor
        heads.append(jnp.where(row, accum / total, 0.0).astype(BF16))
    result = jnp.zeros((8, D), F32)
    for j in range(4):
        attended = jnp.concatenate(heads[2 * j : 2 * j + 2], axis=1)
        if j < FETCHED:
            rows = pieces[j][...]
        else:
            copies[j - FETCHED].wait()
            rows = wbuf[j - FETCHED]
        result += jnp.dot(attended, rows, preferred_element_type=F32)
    out[...] = result.astype(BF16)[:MINE]


def shape(*dims, dtype=BF16):
    return jax.ShapeDtypeStruct(dims, dtype)


def local(context, norm_gain, query_weight, key_weight, value_weight, out_weight):
    core = lax.axis_index("core")
    x = lax.axis_index(("xh", "xl"))
    z = lax.axis_index("z")
    yl = lax.axis_index("yl")
    gain = norm_gain.reshape(1, D)
    in_hbm = functools.partial(pltpu.with_memory_space_constraint, memory_space=pltpu.HBM)
    gain, query_weight, key_weight, value_weight, out_weight = map(
        in_hbm, (gain, query_weight, key_weight, value_weight, out_weight)
    )

    chips = [(b, z, (x & 2) + a) for b in range(2) for a in range(2)]
    info = [core]
    info += [head_of(b, c, a, core) for b, c, a in chips]
    for b, c, a in chips:
        for half in range(2):
            info.append((((b * 4 + c) * 4 + a) * 2 + (core ^ half)) * ROWS)
    info = jnp.stack(info).astype(jnp.int32)
    info, odd, low, left, ends, front = lax.optimization_barrier(
        (info, near(x) == 1, yl == 0, x < 2, (z & 1) == 0, z < 2)
    )

    other_raw = lax.ppermute(context, "core", SWAP)
    own, query_columns, gain, kv_columns = pl.pallas_call(
        own_kernel,
        out_shape=[shape(ROWS, D), shape(D, 4 * HD), shape(1, D, dtype=F32), shape(D, 8 * HD)],
        in_specs=[SMEM] + [HBM] * 5,
        out_specs=[VMEM] * 4,
        scratch_shapes=[pltpu.VMEM((ROWS, D), BF16), pltpu.SemaphoreType.DMA((14,))],
        compiler_params=params(16),
        cost_estimate=pl.CostEstimate(flops=2**23, bytes_accessed=2**23, transcendentals=0),
    )(info, in_hbm(context), gain, query_weight, key_weight, value_weight)
    other, *queries = pl.pallas_call(
        query_kernel,
        out_shape=[shape(ROWS, D)] + [shape(LAT, HD)] * 4,
        in_specs=[SMEM] + [VMEM] * 4,
        out_specs=[VMEM] * 5,
        compiler_params=params(24),
        cost_estimate=pl.CostEstimate(flops=2**29, bytes_accessed=2**21, transcendentals=0),
    )(info, other_raw, own, gain, query_columns)

    def hop(value, dx, dz, dy):
        pairs = []
        for b in range(2):
            for c in range(4):
                for a in range(4):
                    pairs.append(((b * 4 + c) * 4 + a, ((b ^ dy) * 4 + (c ^ dz)) * 4 + (a ^ dx)))
        return lax.ppermute(value, ("yl", "z", "xh", "xl"), pairs)

    by_x = hop(queries[2], 1, 0, 0)
    by_y = hop(queries[1], 0, 0, 1)
    by_xy = hop(queries[0], 1, 0, 1)

    kv = pl.pallas_call(
        kv_kernel,
        out_shape=shape(4, 2 * ROWS, 2 * HD),
        in_specs=[VMEM] * 3,
        out_specs=HBM,
        scratch_shapes=[pltpu.VMEM((4, 2 * ROWS, 2 * HD), BF16), pltpu.SemaphoreType.DMA((2,))],
        compiler_params=params(24),
        cost_estimate=pl.CostEstimate(flops=2**31, bytes_accessed=2**22, transcendentals=0),
    )(own, other, kv_columns)

    query = jnp.where(
        odd, jnp.where(low, by_xy, by_x), jnp.where(low, by_y, queries[3])
    )
    query, kv = lax.optimization_barrier((query, kv))
    kv = lax.all_to_all(kv, ("yl", "xl"), 0, 0)
    along = [query] + [hop(query, 0, d, 0) for d in (1, 2, 3)]
    out_rows = pl.pallas_call(
        fetch_kernel,
        out_shape=[shape(2 * HD, D)] * FETCHED,
        in_specs=[HBM],
        out_specs=[VMEM] * FETCHED,
        scratch_shapes=[pltpu.SemaphoreType.DMA((FETCHED,))],
        compiler_params=params(16),
        cost_estimate=pl.CostEstimate(flops=1, bytes_accessed=2**26, transcendentals=0),
    )(out_weight)
    query = jnp.where(
        front, jnp.where(ends, along[3], along[2]), jnp.where(ends, along[1], along[0])
    )
    query, *out_rows = lax.optimization_barrier((query, *out_rows))
    across = hop(query, 3, 0, 0)
    query = jnp.where(left, across, query)

    parts = pl.pallas_call(
        attend_kernel,
        out_shape=shape(LAT // 8, 2, 8, HD),
        in_specs=[SMEM] + [VMEM] * 2,
        out_specs=VMEM,
        compiler_params=params(16),
        cost_estimate=pl.CostEstimate(flops=2**28, bytes_accessed=2**21, transcendentals=2**19),
    )(info, query, kv)
    parts = lax.all_to_all(parts.reshape(64, 8, HD), CTX_AXES, 0, 0)
    return pl.pallas_call(
        merge_kernel,
        out_shape=shape(MINE, D),
        in_specs=[VMEM, HBM] + [VMEM] * FETCHED,
        out_specs=VMEM,
        scratch_shapes=[pltpu.VMEM((4 - FETCHED, 2 * HD, D), BF16), pltpu.SemaphoreType.DMA((4,))],
        compiler_params=params(16),
        cost_estimate=pl.CostEstimate(flops=2**25, bytes_accessed=2**22, transcendentals=2**16),
    )(parts, out_weight, *out_rows)


def solution(mesh):
    fine = Mesh(mesh.devices.reshape(2, 4, 2, 2, 2, 2), CTX_AXES + ("batch",))
    rows = P(("batch",) + CTX_AXES, None)
    return jax.shard_map(
        local,
        mesh=fine,
        in_specs=(rows, P(), P(), P(), P(), P()),
        out_specs=rows,
        check_vma=False,
    )
```

time: 70.1 us -> 54.4 us (0.78)
  local copies, waits for them, and re-layouts: 11.4 us -> 0.09 us
  waiting for transfers between devices: 11.1 us -> 4.36 us
  Pallas kernels: 13 us -> 14.7 us
    unnamed x14 -> x0, local copies, waits for them, and re-layouts: 11.4 us -> none
    ppermute x10 -> x7, waiting for transfers between devices: 11.1 us -> 4.35 us  [hop(): return lax.ppermute(value, ('yl', 'z', 'xh', 'xl'), pairs)]
    all_to_all x0 -> x1, starting transfers between devices: none -> 3.67 us  [local(): kv = lax.all_to_all(kv, ('yl', 'xl'), 0, 0)]
    pallas_call x4 -> x5, Pallas kernels: 9.31 us -> 12.9 us  [the longest x1 3.94 us: local(): pl.pallas_call(own_kernel, out_shape=[shape(ROWS, D), shape(D, 4 * HD), s...]
    ppermute x10 -> x7, starting transfers between devices: 13.4 us -> 10.2 us  [hop(): return lax.ppermute(value, ('yl', 'z', 'xh', 'xl'), pairs)]
    pallas_call x1, Pallas kernels: 3.66 us -> 1.86 us  [local(): pl.pallas_call(query_kernel, out_shape=[shape(ROWS, D)] + [shape(LAT, HD)...]
  transfers between devices with their start and end apart: 11 -> 9, of which waited for: 6 -> 3; matrix products, arithmetic and copies ran while one was open for 0% -> 0% of each run, Pallas kernels for 9% -> 16%
where the time goes in v2:
time: 54.4 us; the launch traced here: 54.1 us
  blocking collectives  19.5 us (36%)
  starting transfers between devices  15.3 us (28%)
  Pallas kernels  14.7 us (27%)
  waiting for transfers between devices  4.36 us (8%)
    all_to_all x1, blocking collectives, local(): parts = lax.all_to_all(parts.reshape(64, 8, HD), CTX_AXES, 0, 0)  19.5 us
    ppermute x7, starting transfers between devices, hop(): return lax.ppermute(value, ('yl', 'z', 'xh', 'xl'), pairs)  10.2 us
    ppermute x7, waiting for transfers between devices, hop(): return lax.ppermute(value, ('yl', 'z', 'xh', 'xl'), pairs)  4.35 us
    pallas_call x1, Pallas kernels, local(): pl.pallas_call(own_kernel, out_shape=[shape(ROWS, D), shape(D, 4 * HD), s...  3.94 us
    all_to_all x1, starting transfers between devices, local(): kv = lax.all_to_all(kv, ('yl', 'xl'), 0, 0)  3.67 us
    pallas_call x1, Pallas kernels, local(): pl.pallas_call(kv_kernel, out_shape=shape(4, 2 * ROWS, 2 * HD), in_specs=...  3.14 us
    pallas_call x1, Pallas kernels, local(): pl.pallas_call(merge_kernel, out_shape=shape(MINE, D), in_specs=[VMEM, HB...  2.58 us
    pallas_call x1, Pallas kernels, local(): pl.pallas_call(query_kernel, out_shape=[shape(ROWS, D)] + [shape(LAT, HD)...  1.86 us
  transfers between devices with their start and end apart: 9, of which 3 were waited for; matrix products, arithmetic and copies ran while one was open for 0% of the time, Pallas kernels for 16%

profile of v2, /device:TPU:1, one launch (start us, length us, event | category | flops | bytes accessed | tf_op | source)
XLA Modules:
  0.0 54.1 jit_solution(7521551920025343349)
XLA Ops:
  0.0 1.4 %collective-permute-start = (bf16[256,2048]{1,0:T(8,128)(2,1)}, bf16[256,2048]{1,0:T(8,128)(2,1)S(1)}, u32[]{:S(2)}, u32[]{:S(2)}) collective-permute-start(bf16[256,2048]{1,0:T(8,128)(2,1)} %tokens.1), channel_id=1, source_target_pairs={{0,2},{2,0},{1,3},{3,1},{4,6},{6,4},{5,7},{7,5},{8,10},{10,8},{9,1... | collective-permute-start | bytes 3145736 | tf_op jit(solution)/shard_map/ppermute | solution.py:217
  1.4 0.1 stack.55.info
  1.5 3.9 %shard_map.64 = (bf16[256,2048]{1,0:T(8,128)(2,1)S(1)}, bf16[2048,512]{1,0:T(8,128)(2,1)S(1)}, f32[1,2048]{1,0:T(1,128)S(1)}, bf16[2048,1024]{1,0:T(8,128)(2,1)S(1)}) custom-call(s32[13]{0:T(128)S(1)} %stack.55.info, bf16[256,2048]{1,0:T(8,128)(2,1)} %tokens.1, f32[1,2048]{1,0:T(1,128)} %bitcast.16, bf16[2048,1024]{1,0:T(8,128)(2,1)} %wq.1, ...), custom_call_target="tpu_custom_call" | custom-call | flops 8388608 | bytes 8388608 | tf_op jit(solution)/shard_map/pallas_call | solution.py:218
  5.5 0.0 collective-permute-done.tokens
  5.5 1.9 %shard_map.65 = (bf16[256,2048]{1,0:T(8,128)(2,1)S(1)}, bf16[256,128]{1,0:T(8,128)(2,1)S(1)}, bf16[256,128]{1,0:T(8,128)(2,1)S(1)}, bf16[256,128]{1,0:T(8,128)(2,1)S(1)}, bf16[256,128]{1,0:T(8,128)(2,1)S(1)}) custom-call(s32[13]{0:T(128)S(1)} %stack.55.info, bf16[256,2048]{1,0:T(8,128)(2,1)S(1)} %collective-permute-done.tokens, ...), custom_call_target="tpu_custom_call" | custom-call | flops 536870912 | bytes 2097152 | tf_op jit(solution)/shard_map/pallas_call | solution.py:227
  7.3 2.4 %collective-permute-start.1 = (bf16[256,128]{1,0:T(8,128)(2,1)S(1)}, bf16[256,128]{1,0:T(8,128)(2,1)S(1)}, u32[]{:S(2)}, u32[]{:S(2)}) collective-permute-start(bf16[256,128]{1,0:T(8,128)(2,1)S(1)} %get-tuple-element.36), channel_id=1, source_target_pairs={{0,68},{4,64},{8,76},{12,72},{16,84},{20,80},{24,92},{28,88},{32,1... | collective-permute-start | bytes 196616 | tf_op jit(solution)/shard_map/ppermute | solution.py:242
  9.7 0.3 collective-permute-start.2
  10.0 0.1 collective-permute-start.3
  10.1 3.1 %shard_map.66 = bf16[4,512,256]{2,1,0:T(8,128)(2,1)} custom-call(bf16[256,2048]{1,0:T(8,128)(2,1)S(1)} %get-tuple-element.33.own, bf16[256,2048]{1,0:T(8,128)(2,1)S(1)} %get-tuple-element.40.other, bf16[2048,1024]{1,0:T(8,128)(2,1)S(1)} %get-tuple-element.41.weight), custom_call_target="tpu_custom_call" | custom-call | flops 2147483648 | bytes 4194304 | tf_op jit(solution)/shard_map/pallas_call | solution.py:248
  13.3 0.0 collective-permute-done.1
  13.3 0.3 collective-permute-done.2
  13.5 0.0 collective-permute-done.3
  13.5 3.7 %all-to-all-start = ((bf16[4,512,256]{2,1,0:T(8,128)(2,1)}), bf16[4,512,256]{2,1,0:T(8,128)(2,1)S(1)}, u32[]{:S(2)}, u32[]{:S(2)}) async-start(bf16[4,512,256]{2,1,0:T(8,128)(2,1)} %shard_map.66), calls=%async_computation | async-start | bytes 2097152 | tf_op jit(solution)/shard_map/all_to_all | solution.py:262
  17.2 3.8 %collective-permute-start.4 = (bf16[256,128]{1,0:T(8,128)(2,1)S(1)}, bf16[256,128]{1,0:T(8,128)(2,1)S(1)}, u32[]{:S(2)}, u32[]{:S(2)}) collective-permute-start(bf16[256,128]{1,0:T(8,128)(2,1)S(1)} %select_select_fusion.1), channel_id=1, source_target_pairs={{0,48},{4,52},{8,56},{12,60},{16,32},{20,36},{24,40},{28,44},{32,1... | collective-permute-start | bytes 196616 | tf_op jit(solution)/shard_map/ppermute | solution.py:242
  21.0 0.0 collective-permute-start.5
  21.0 0.6 %collective-permute-start.6 = (bf16[256,128]{1,0:T(8,128)(2,1)S(1)}, bf16[256,128]{1,0:T(8,128)(2,1)S(1)}, u32[]{:S(2)}, u32[]{:S(2)}) collective-permute-start(bf16[256,128]{1,0:T(8,128)(2,1)S(1)} %select_select_fusion.1), channel_id=1, source_target_pairs={{0,16},{4,20},{8,24},{12,28},{16,0},{20,4},{24,8},{28,12},{32,48},... | collective-permute-start | bytes 196616 | tf_op jit(solution)/shard_map/ppermute | solution.py:242
  21.6 1.6 %shard_map.67 = (bf16[256,2048]{1,0:T(8,128)(2,1)S(1)}, bf16[256,2048]{1,0:T(8,128)(2,1)S(1)}) custom-call(bf16[1024,2048]{1,0:T(8,128)(2,1)} %weight.1), custom_call_target="tpu_custom_call" | custom-call | flops 1 | bytes 67108864 | tf_op jit(solution)/shard_map/pallas_call | solution.py:264
  23.2 0.0 collective-permute-done.4
  23.2 2.4 %collective-permute-done.5 = bf16[256,128]{1,0:T(8,128)(2,1)S(1)} collective-permute-done((bf16[256,128]{1,0:T(8,128)(2,1)S(1)}, bf16[256,128]{1,0:T(8,128)(2,1)S(1)}, u32[]{:S(2)}, u32[]{:S(2)}) %collective-permute-start.5) | collective-permute-done | bytes 65568 | tf_op jit(solution)/shard_map/ppermute | solution.py:242
  25.6 0.0 collective-permute-done.6
  25.6 3.0 %collective-permute-start.7 = (bf16[256,128]{1,0:T(8,128)(2,1)S(1)}, bf16[256,128]{1,0:T(8,128)(2,1)S(1)}, u32[]{:S(2)}, u32[]{:S(2)}) collective-permute-start(bf16[256,128]{1,0:T(8,128)(2,1)S(1)} %select_select_fusion), channel_id=1, source_target_pairs={{0,12},{4,8},{8,4},{12,0},{16,28},{20,24},{24,20},{28,16},{32,44},... | collective-permute-start | bytes 196616 | tf_op jit(solution)/shard_map/ppermute | solution.py:242
  28.7 1.7 %collective-permute-done.7 = bf16[256,128]{1,0:T(8,128)(2,1)S(1)} collective-permute-done((bf16[256,128]{1,0:T(8,128)(2,1)S(1)}, bf16[256,128]{1,0:T(8,128)(2,1)S(1)}, u32[]{:S(2)}, u32[]{:S(2)}) %collective-permute-start.7) | collective-permute-done | bytes 65568 | tf_op jit(solution)/shard_map/ppermute | solution.py:242
  30.3 0.0 all-to-all-done.kv
  30.3 1.7 %shard_map.68 = bf16[32,2,8,128]{3,2,1,0:T(8,128)(2,1)S(1)} custom-call(s32[13]{0:T(128)S(1)} %stack.55.info, bf16[256,128]{1,0:T(8,128)(2,1)S(1)} %broadcast_select_fusion.query, bf16[4,512,256]{2,1,0:T(8,128)(2,1)S(1)} %all-to-all-done.kv), custom_call_target="tpu_custom_call" | custom-call | flops 268435456 | bytes 2097152 | tf_op jit(solution)/shard_map/pallas_call | solution.py:280
  32.0 19.5 %all_to_all.10.parts = bf16[64,8,128]{2,1,0:T(8,128)(2,1)S(1)} all-to-all(bf16[64,8,128]{2,1,0:T(8,128)(2,1)S(1)} %bitcast.15), channel_id=1, replica_groups=mesh['yl'=2,'z'=4,'xh'=2,'xl'=2,'core'=2,'batch'=2] {'yl','z','xh','xl',..., dimensions={0} | all-to-all | bytes 262144 | tf_op jit(solution)/shard_map/all_to_all | solution.py:288
  51.5 2.6 %shard_map.69 = bf16[4,2048]{1,0:T(4,128)(2,1)} custom-call(bf16[64,8,128]{2,1,0:T(8,128)(2,1)S(1)} %all_to_all.10.parts, bf16[1024,2048]{1,0:T(8,128)(2,1)} %weight.1, bf16[256,2048]{1,0:T(8,128)(2,1)S(1)} %get-tuple-element.47.rest_0_, bf16[256,2048]{1,0:T(8,128)(2,1)S(1)} %get-tuple-element.48.rest_1_), custom_call_target="tpu_custom_call" | custom-call | flops 33554432 | bytes 4194304 | tf_op jit(solution)/shard_map/pallas_call | solution.py:289
  (3 shorter events, 0.0 us)
Async XLA Ops:
  0.0 5.5 %collective-permute-start = (bf16[256,2048]{1,0:T(8,128)(2,1)}, bf16[256,2048]{1,0:T(8,128)(2,1)S(1)}, u32[]{:S(2)}, u32[]{:S(2)}) collective-permute-start(bf16[256,2048]{1,0:T(8,128)(2,1)} %tokens.1), channel_id=1, source_target_pairs={{0,2},{2,0},{1,3},{3,1},{4,6},{6,4},{5,7},{7,5},{8,10},{10,8},{9,1... | collective-permute-start | bytes 3145736 | tf_op jit(solution)/shard_map/ppermute | solution.py:217
  7.3 5.9 %collective-permute-start.1 = (bf16[256,128]{1,0:T(8,128)(2,1)S(1)}, bf16[256,128]{1,0:T(8,128)(2,1)S(1)}, u32[]{:S(2)}, u32[]{:S(2)}) collective-permute-start(bf16[256,128]{1,0:T(8,128)(2,1)S(1)} %get-tuple-element.36), channel_id=1, source_target_pairs={{0,68},{4,64},{8,76},{12,72},{16,84},{20,80},{24,92},{28,88},{32,1... | collective-permute-start | bytes 196616 | tf_op jit(solution)/shard_map/ppermute | solution.py:242
  9.7 3.8 %collective-permute-start.2 = (bf16[256,128]{1,0:T(8,128)(2,1)S(1)}, bf16[256,128]{1,0:T(8,128)(2,1)S(1)}, u32[]{:S(2)}, u32[]{:S(2)}) collective-permute-start(bf16[256,128]{1,0:T(8,128)(2,1)S(1)} %get-tuple-element.37), channel_id=1, source_target_pairs={{0,4},{4,0},{8,12},{12,8},{16,20},{20,16},{24,28},{28,24},{32,36},... | collective-permute-start | bytes 196616 | tf_op jit(solution)/shard_map/ppermute | solution.py:242
  10.0 3.5 %collective-permute-start.3 = (bf16[256,128]{1,0:T(8,128)(2,1)S(1)}, bf16[256,128]{1,0:T(8,128)(2,1)S(1)}, u32[]{:S(2)}, u32[]{:S(2)}) collective-permute-start(bf16[256,128]{1,0:T(8,128)(2,1)S(1)} %get-tuple-element.38), channel_id=1, source_target_pairs={{0,64},{4,68},{8,72},{12,76},{16,80},{20,84},{24,88},{28,92},{32,9... | collective-permute-start | bytes 196616 | tf_op jit(solution)/shard_map/ppermute | solution.py:242
  13.5 16.8 %all-to-all-start = ((bf16[4,512,256]{2,1,0:T(8,128)(2,1)}), bf16[4,512,256]{2,1,0:T(8,128)(2,1)S(1)}, u32[]{:S(2)}, u32[]{:S(2)}) async-start(bf16[4,512,256]{2,1,0:T(8,128)(2,1)} %shard_map.66), calls=%async_computation | async-start | bytes 2097152 | tf_op jit(solution)/shard_map/all_to_all | solution.py:262
  17.2 5.9 %collective-permute-start.4 = (bf16[256,128]{1,0:T(8,128)(2,1)S(1)}, bf16[256,128]{1,0:T(8,128)(2,1)S(1)}, u32[]{:S(2)}, u32[]{:S(2)}) collective-permute-start(bf16[256,128]{1,0:T(8,128)(2,1)S(1)} %select_select_fusion.1), channel_id=1, source_target_pairs={{0,48},{4,52},{8,56},{12,60},{16,32},{20,36},{24,40},{28,44},{32,1... | collective-permute-start | bytes 196616 | tf_op jit(solution)/shard_map/ppermute | solution.py:242
  21.0 4.6 %collective-permute-start.5 = (bf16[256,128]{1,0:T(8,128)(2,1)S(1)}, bf16[256,128]{1,0:T(8,128)(2,1)S(1)}, u32[]{:S(2)}, u32[]{:S(2)}) collective-permute-start(bf16[256,128]{1,0:T(8,128)(2,1)S(1)} %select_select_fusion.1), channel_id=1, source_target_pairs={{0,32},{4,36},{8,40},{12,44},{16,48},{20,52},{24,56},{28,60},{32,0... | collective-permute-start | bytes 196616 | tf_op jit(solution)/shard_map/ppermute | solution.py:242
  21.0 4.6 %collective-permute-start.6 = (bf16[256,128]{1,0:T(8,128)(2,1)S(1)}, bf16[256,128]{1,0:T(8,128)(2,1)S(1)}, u32[]{:S(2)}, u32[]{:S(2)}) collective-permute-start(bf16[256,128]{1,0:T(8,128)(2,1)S(1)} %select_select_fusion.1), channel_id=1, source_target_pairs={{0,16},{4,20},{8,24},{12,28},{16,0},{20,4},{24,8},{28,12},{32,48},... | collective-permute-start | bytes 196616 | tf_op jit(solution)/shard_map/ppermute | solution.py:242
  25.6 4.7 %collective-permute-start.7 = (bf16[256,128]{1,0:T(8,128)(2,1)S(1)}, bf16[256,128]{1,0:T(8,128)(2,1)S(1)}, u32[]{:S(2)}, u32[]{:S(2)}) collective-permute-start(bf16[256,128]{1,0:T(8,128)(2,1)S(1)} %select_select_fusion), channel_id=1, source_target_pairs={{0,12},{4,8},{8,4},{12,0},{16,28},{20,24},{24,20},{28,16},{32,44},... | collective-permute-start | bytes 196616 | tf_op jit(solution)/shard_map/ppermute | solution.py:242

commit v3 on v2

--- a/solution.py
+++ b/solution.py
@@ -15,7 +15,7 @@
 ROWS = 256
 CTX = 16384
 MINE = 4
-FETCHED = 2
+FETCHED = 3
 F32 = jnp.float32
 BF16 = jnp.bfloat16
 CTX_AXES = ("yl", "z", "xh", "xl", "core")
@@ -91,13 +91,18 @@
         write.wait()
 
 
+def fetch_rows(wo, pieces, first, sems):
+    copies = []
+    for j, piece in enumerate(pieces):
+        at = pl.ds((first + j) * 2 * HD, 2 * HD)
+        copies.append(pltpu.make_async_copy(wo.at[at], piece, sems.at[j]))
+        copies[-1].start()
+    return copies
+
+
 def fetch_kernel(wo, *rest):
     *pieces, sems = rest
-    copies = []
-    for j, piece in enumerate(pieces):
-        copies.append(pltpu.make_async_copy(wo.at[pl.ds(j * 2 * HD, 2 * HD)], piece, sems.at[j]))
-        copies[-1].start()
-    for copy in copies:
+    for copy in fetch_rows(wo, pieces, 0, sems):
         copy.wait()
 
 
@@ -107,7 +112,9 @@
     return [first, second, value - first - second]
 
 
-def attend_kernel(info, query, kv, out):
+def attend_kernel(info, query, kv, wo, out, *rest):
+    *pieces, sems = rest
+    copies = fetch_rows(wo, pieces, FETCHED, sems)
     queries = query[...]
     row = lax.broadcasted_iota(jnp.int32, (LAT, ROWS), 0)
     column = lax.broadcasted_iota(jnp.int32, (LAT, ROWS), 1)
@@ -138,15 +145,12 @@
     upper = lax.broadcasted_iota(jnp.int32, (LAT // 8, 8, HD), 1) < MINE
     out[:, 0] = jnp.where(upper, accum, pltpu.roll(stats, MINE, 1)).astype(BF16)
     out[:, 1] = jnp.where(upper, pltpu.roll(accum, MINE, 1), stats).astype(BF16)
-
-
-def merge_kernel(parts, weight, *rest):
-    *pieces, out, wbuf, sems = rest
-    copies = []
-    for j in range(4 - FETCHED):
-        at = pl.ds((FETCHED + j) * 2 * HD, 2 * HD)
-        copies.append(pltpu.make_async_copy(weight.at[at], wbuf.at[j], sems.at[j]))
-        copies[-1].start()
+    for copy in copies:
+        copy.wait()
+
+
+def merge_kernel(parts, *rest):
+    *pieces, out = rest
     row = lax.broadcasted_iota(jnp.int32, (8, HD), 0) < MINE
     k = lax.broadcasted_iota(jnp.int32, (HD, 2 * HD), 0)
     n = lax.broadcasted_iota(jnp.int32, (HD, 2 * HD), 1)
@@ -177,14 +181,9 @@
             total += t * factor
         heads.append(jnp.where(row, accum / total, 0.0).astype(BF16))
     result = jnp.zeros((8, D), F32)
-    for j in range(4):
+    for j, piece in enumerate(pieces):
         attended = jnp.concatenate(heads[2 * j : 2 * j + 2], axis=1)
-        if j < FETCHED:
-            rows = pieces[j][...]
-        else:
-            copies[j - FETCHED].wait()
-            rows = wbuf[j - FETCHED]
-        result += jnp.dot(attended, rows, preferred_element_type=F32)
+        result += jnp.dot(attended, piece[...], preferred_element_type=F32)
     out[...] = result.astype(BF16)[:MINE]
 
 
@@ -258,7 +257,6 @@
     query = jnp.where(
         odd, jnp.where(low, by_xy, by_x), jnp.where(low, by_y, queries[3])
     )
-    query, kv = lax.optimization_barrier((query, kv))
     kv = lax.all_to_all(kv, ("yl", "xl"), 0, 0)
     along = [query] + [hop(query, 0, d, 0) for d in (1, 2, 3)]
     out_rows = pl.pallas_call(
@@ -277,24 +275,24 @@
     across = hop(query, 3, 0, 0)
     query = jnp.where(left, across, query)
 
-    parts = pl.pallas_call(
+    parts, *more_rows = pl.pallas_call(
         attend_kernel,
-        out_shape=shape(LAT // 8, 2, 8, HD),
-        in_specs=[SMEM] + [VMEM] * 2,
-        out_specs=VMEM,
+        out_shape=[shape(LAT // 8, 2, 8, HD)] + [shape(2 * HD, D)] * (4 - FETCHED),
+        in_specs=[SMEM] + [VMEM] * 2 + [HBM],
+        out_specs=[VMEM] * (5 - FETCHED),
+        scratch_shapes=[pltpu.SemaphoreType.DMA((4 - FETCHED,))],
         compiler_params=params(16),
         cost_estimate=pl.CostEstimate(flops=2**28, bytes_accessed=2**21, transcendentals=2**19),
-    )(info, query, kv)
+    )(info, query, kv, out_weight)
     parts = lax.all_to_all(parts.reshape(64, 8, HD), CTX_AXES, 0, 0)
     return pl.pallas_call(
         merge_kernel,
         out_shape=shape(MINE, D),
-        in_specs=[VMEM, HBM] + [VMEM] * FETCHED,
+        in_specs=[VMEM] * 5,
         out_specs=VMEM,
-        scratch_shapes=[pltpu.VMEM((4 - FETCHED, 2 * HD, D), BF16), pltpu.SemaphoreType.DMA((4,))],
         compiler_params=params(16),
         cost_estimate=pl.CostEstimate(flops=2**25, bytes_accessed=2**22, transcendentals=2**16),
-    )(parts, out_weight, *out_rows)
+    )(parts, *out_rows, *more_rows)
 
 
 def solution(mesh):

time: 54.4 us -> 53 us (0.974)
  waiting for transfers between devices: 4.36 us -> 2.74 us
  local copies, waits for them, and re-layouts: 0.09 us -> 1.08 us
    ppermute x7, waiting for transfers between devices: 4.35 us -> 2.73 us  [hop(): return lax.ppermute(value, ('yl', 'z', 'xh', 'xl'), pairs)]
    unnamed x0 -> x4, local copies, waits for them, and re-layouts: none -> 0.99 us
    pallas_call x2, Pallas kernels: 4.23 us -> 3.38 us  [the longest x1 1.78 us: local(): pl.pallas_call(attend_kernel, out_shape=[shape(LAT // 8, 2, 8, HD)] + [sh...]
  transfers between devices with their start and end apart: 9 -> 9, of which waited for: 3 -> 2; matrix products, arithmetic and copies ran while one was open for 0% -> 0% of each run, Pallas kernels for 16% -> 17%
where the time goes in v3:
time: 53 us; the launch traced here: 52.7 us
  blocking collectives  19.2 us (36%)
  starting transfers between devices  15.3 us (29%)
  Pallas kernels  14.2 us (27%)
  waiting for transfers between devices  2.74 us (5%)
  local copies, waits for them, and re-layouts  1.08 us (2%)
    all_to_all x1, blocking collectives, local(): parts = lax.all_to_all(parts.reshape(64, 8, HD), CTX_AXES, 0, 0)  19.2 us
    ppermute x7, starting transfers between devices, hop(): return lax.ppermute(value, ('yl', 'z', 'xh', 'xl'), pairs)  10.4 us
    pallas_call x1, Pallas kernels, local(): pl.pallas_call(own_kernel, out_shape=[shape(ROWS, D), shape(D, 4 * HD), s...  3.94 us
    all_to_all x1, starting transfers between devices, local(): kv = lax.all_to_all(kv, ('yl', 'xl'), 0, 0)  3.55 us
    pallas_call x1, Pallas kernels, local(): pl.pallas_call(kv_kernel, out_shape=shape(4, 2 * ROWS, 2 * HD), in_specs=...  3.16 us
    ppermute x7, waiting for transfers between devices, hop(): return lax.ppermute(value, ('yl', 'z', 'xh', 'xl'), pairs)  2.73 us
    pallas_call x1, Pallas kernels, local(): pl.pallas_call(fetch_kernel, out_shape=[shape(2 * HD, D)] * FETCHED, in_s...  1.88 us
    pallas_call x1, Pallas kernels, local(): pl.pallas_call(query_kernel, out_shape=[shape(ROWS, D)] + [shape(LAT, HD)...  1.86 us
  transfers between devices with their start and end apart: 9, of which 2 were waited for; matrix products, arithmetic and copies ran while one was open for 0% of the time, Pallas kernels for 17%

profile of v3, /device:TPU:1, one launch (start us, length us, event | category | flops | bytes accessed | tf_op | source)
XLA Modules:
  0.0 52.7 jit_solution(13559430521155829649)
XLA Ops:
  0.0 1.4 %collective-permute-start = (bf16[256,2048]{1,0:T(8,128)(2,1)}, bf16[256,2048]{1,0:T(8,128)(2,1)S(1)}, u32[]{:S(2)}, u32[]{:S(2)}) collective-permute-start(bf16[256,2048]{1,0:T(8,128)(2,1)} %tokens.1), channel_id=1, source_target_pairs={{0,2},{2,0},{1,3},{3,1},{4,6},{6,4},{5,7},{7,5},{8,10},{10,8},{9,1... | collective-permute-start | bytes 3145736 | tf_op jit(solution)/shard_map/ppermute | solution.py:216
  1.4 0.1 stack.55.info
  1.5 3.9 %shard_map.64 = (bf16[256,2048]{1,0:T(8,128)(2,1)S(1)}, bf16[2048,512]{1,0:T(8,128)(2,1)S(1)}, f32[1,2048]{1,0:T(1,128)S(1)}, bf16[2048,1024]{1,0:T(8,128)(2,1)S(1)}) custom-call(s32[13]{0:T(128)S(1)} %stack.55.info, bf16[256,2048]{1,0:T(8,128)(2,1)} %tokens.1, f32[1,2048]{1,0:T(1,128)} %bitcast.16, bf16[2048,1024]{1,0:T(8,128)(2,1)} %wq.1, ...), custom_call_target="tpu_custom_call" | custom-call | flops 8388608 | bytes 8388608 | tf_op jit(solution)/shard_map/pallas_call | solution.py:217
  5.5 0.0 collective-permute-done.tokens
  5.5 1.9 %shard_map.65 = (bf16[256,2048]{1,0:T(8,128)(2,1)S(1)}, bf16[256,128]{1,0:T(8,128)(2,1)S(1)}, bf16[256,128]{1,0:T(8,128)(2,1)S(1)}, bf16[256,128]{1,0:T(8,128)(2,1)S(1)}, bf16[256,128]{1,0:T(8,128)(2,1)S(1)}) custom-call(s32[13]{0:T(128)S(1)} %stack.55.info, bf16[256,2048]{1,0:T(8,128)(2,1)S(1)} %collective-permute-done.tokens, ...), custom_call_target="tpu_custom_call" | custom-call | flops 536870912 | bytes 2097152 | tf_op jit(solution)/shard_map/pallas_call | solution.py:226
  7.3 2.4 %collective-permute-start.1 = (bf16[256,128]{1,0:T(8,128)(2,1)S(1)}, bf16[256,128]{1,0:T(8,128)(2,1)S(1)}, u32[]{:S(2)}, u32[]{:S(2)}) collective-permute-start(bf16[256,128]{1,0:T(8,128)(2,1)S(1)} %get-tuple-element.38), channel_id=1, source_target_pairs={{0,68},{4,64},{8,76},{12,72},{16,84},{20,80},{24,92},{28,88},{32,1... | collective-permute-start | bytes 196616 | tf_op jit(solution)/shard_map/ppermute | solution.py:241
  9.7 0.3 collective-permute-start.2
  10.0 0.1 collective-permute-start.3
  10.1 3.2 %shard_map.67 = bf16[4,512,256]{2,1,0:T(8,128)(2,1)} custom-call(bf16[256,2048]{1,0:T(8,128)(2,1)S(1)} %get-tuple-element.35.own, bf16[256,2048]{1,0:T(8,128)(2,1)S(1)} %get-tuple-element.46.other, bf16[2048,1024]{1,0:T(8,128)(2,1)S(1)} %get-tuple-element.47.weight), custom_call_target="tpu_custom_call" | custom-call | flops 2147483648 | bytes 4194304 | tf_op jit(solution)/shard_map/pallas_call | solution.py:247
  13.3 3.6 %all-to-all-start = ((bf16[4,512,256]{2,1,0:T(8,128)(2,1)}), bf16[4,512,256]{2,1,0:T(8,128)(2,1)S(1)}, u32[]{:S(2)}, u32[]{:S(2)}) async-start(bf16[4,512,256]{2,1,0:T(8,128)(2,1)} %shard_map.67), calls=%async_computation | async-start | bytes 2097152 | tf_op jit(solution)/shard_map/all_to_all | solution.py:260
  16.8 0.0 collective-permute-done.1
  16.8 0.0 collective-permute-done.2
  16.8 0.0 collective-permute-done.3
  16.9 3.9 %collective-permute-start.4 = (bf16[256,128]{1,0:T(8,128)(2,1)S(1)}, bf16[256,128]{1,0:T(8,128)(2,1)S(1)}, u32[]{:S(2)}, u32[]{:S(2)}) collective-permute-start(bf16[256,128]{1,0:T(8,128)(2,1)S(1)} %select_select_fusion.1), channel_id=1, source_target_pairs={{0,48},{4,52},{8,56},{12,60},{16,32},{20,36},{24,40},{28,44},{32,1... | collective-permute-start | bytes 196616 | tf_op jit(solution)/shard_map/ppermute | solution.py:241
  20.8 0.0 collective-permute-start.5
  20.8 0.7 %collective-permute-start.6 = (bf16[256,128]{1,0:T(8,128)(2,1)S(1)}, bf16[256,128]{1,0:T(8,128)(2,1)S(1)}, u32[]{:S(2)}, u32[]{:S(2)}) collective-permute-start(bf16[256,128]{1,0:T(8,128)(2,1)S(1)} %select_select_fusion.1), channel_id=1, source_target_pairs={{0,16},{4,20},{8,24},{12,28},{16,0},{20,4},{24,8},{28,12},{32,48},... | collective-permute-start | bytes 196616 | tf_op jit(solution)/shard_map/ppermute | solution.py:241
  21.4 1.9 %shard_map.66 = (bf16[256,2048]{1,0:T(8,128)(2,1)S(1)}, bf16[256,2048]{1,0:T(8,128)(2,1)S(1)}, bf16[256,2048]{1,0:T(8,128)(2,1)S(1)}) custom-call(bf16[1024,2048]{1,0:T(8,128)(2,1)} %wo.3), custom_call_target="tpu_custom_call" | custom-call | flops 1 | bytes 67108864 | tf_op jit(solution)/shard_map/pallas_call | solution.py:262
  23.3 0.0 copy-start
  23.3 1.0 %copy-done = bf16[256,2048]{1,0:T(8,128)(2,1)} copy-done((bf16[256,2048]{1,0:T(8,128)(2,1)}, bf16[256,2048]{1,0:T(8,128)(2,1)S(1)}, u32[]{:S(2)}) %copy-start) | copy-done | bytes 1048600
  24.3 0.0 collective-permute-done.4
  24.3 1.1 %collective-permute-done.5 = bf16[256,128]{1,0:T(8,128)(2,1)S(1)} collective-permute-done((bf16[256,128]{1,0:T(8,128)(2,1)S(1)}, bf16[256,128]{1,0:T(8,128)(2,1)S(1)}, u32[]{:S(2)}, u32[]{:S(2)}) %collective-permute-start.5) | collective-permute-done | bytes 65568 | tf_op jit(solution)/shard_map/ppermute | solution.py:241
  25.4 0.0 collective-permute-done.6
  25.4 3.0 %collective-permute-start.7 = (bf16[256,128]{1,0:T(8,128)(2,1)S(1)}, bf16[256,128]{1,0:T(8,128)(2,1)S(1)}, u32[]{:S(2)}, u32[]{:S(2)}) collective-permute-start(bf16[256,128]{1,0:T(8,128)(2,1)S(1)} %select_select_fusion), channel_id=1, source_target_pairs={{0,12},{4,8},{8,4},{12,0},{16,28},{20,24},{24,20},{28,16},{32,44},... | collective-permute-start | bytes 196616 | tf_op jit(solution)/shard_map/ppermute | solution.py:241
  28.4 1.7 %collective-permute-done.7 = bf16[256,128]{1,0:T(8,128)(2,1)S(1)} collective-permute-done((bf16[256,128]{1,0:T(8,128)(2,1)S(1)}, bf16[256,128]{1,0:T(8,128)(2,1)S(1)}, u32[]{:S(2)}, u32[]{:S(2)}) %collective-permute-start.7) | collective-permute-done | bytes 65568 | tf_op jit(solution)/shard_map/ppermute | solution.py:241
  30.1 0.0 all-to-all-done.kv
  30.1 0.0 copy-start.1
  30.1 1.8 %shard_map.68 = (bf16[32,2,8,128]{3,2,1,0:T(8,128)(2,1)S(1)}, bf16[256,2048]{1,0:T(8,128)(2,1)S(1)}) custom-call(s32[13]{0:T(128)S(1)} %stack.55.info, bf16[256,128]{1,0:T(8,128)(2,1)S(1)} %broadcast_select_fusion.query, bf16[4,512,256]{2,1,0:T(8,128)(2,1)S(1)} %all-to-all-done.kv, bf16[1024,2048]{1,0:T(8,128)(2,1)} %wo.3), custom_call_target="tpu_custom_call" | custom-call | flops 268435456 | bytes 2097152 | tf_op jit(solution)/shard_map/pallas_call | solution.py:278
  31.9 19.2 %all_to_all.10.parts = bf16[64,8,128]{2,1,0:T(8,128)(2,1)S(1)} all-to-all(bf16[64,8,128]{2,1,0:T(8,128)(2,1)S(1)} %bitcast.15), channel_id=1, replica_groups=mesh['yl'=2,'z'=4,'xh'=2,'xl'=2,'core'=2,'batch'=2] {'yl','z','xh','xl',..., dimensions={0} | all-to-all | bytes 262144 | tf_op jit(solution)/shard_map/all_to_all | solution.py:287
  51.1 0.0 copy-done.1
  51.1 1.6 %shard_map.69 = bf16[4,2048]{1,0:T(4,128)(2,1)} custom-call(bf16[64,8,128]{2,1,0:T(8,128)(2,1)S(1)} %all_to_all.10.parts, bf16[256,2048]{1,0:T(8,128)(2,1)S(1)} %get-tuple-element.49.rest_0_, bf16[256,2048]{1,0:T(8,128)(2,1)S(1)} %get-tuple-element.50.rest_1_, bf16[256,2048]{1,0:T(8,128)(2,1)S(1)} %copy-done.1, bf16[256,2048]{1,0:T(8,128)(2,1)S(1)} %get-tuple-element.52.rest_3_), custom_call_target="tpu_custom_call" | custom-call | flops 33554432 | bytes 4194304 | tf_op jit(solution)/shard_map/pallas_call | solution.py:288
  (3 shorter events, 0.0 us)
Async XLA Ops:
  0.0 5.5 %collective-permute-start = (bf16[256,2048]{1,0:T(8,128)(2,1)}, bf16[256,2048]{1,0:T(8,128)(2,1)S(1)}, u32[]{:S(2)}, u32[]{:S(2)}) collective-permute-start(bf16[256,2048]{1,0:T(8,128)(2,1)} %tokens.1), channel_id=1, source_target_pairs={{0,2},{2,0},{1,3},{3,1},{4,6},{6,4},{5,7},{7,5},{8,10},{10,8},{9,1... | collective-permute-start | bytes 3145736 | tf_op jit(solution)/shard_map/ppermute | solution.py:216
  7.3 9.5 %collective-permute-start.1 = (bf16[256,128]{1,0:T(8,128)(2,1)S(1)}, bf16[256,128]{1,0:T(8,128)(2,1)S(1)}, u32[]{:S(2)}, u32[]{:S(2)}) collective-permute-start(bf16[256,128]{1,0:T(8,128)(2,1)S(1)} %get-tuple-element.38), channel_id=1, source_target_pairs={{0,68},{4,64},{8,76},{12,72},{16,84},{20,80},{24,92},{28,88},{32,1... | collective-permute-start | bytes 196616 | tf_op jit(solution)/shard_map/ppermute | solution.py:241
  9.7 7.1 %collective-permute-start.2 = (bf16[256,128]{1,0:T(8,128)(2,1)S(1)}, bf16[256,128]{1,0:T(8,128)(2,1)S(1)}, u32[]{:S(2)}, u32[]{:S(2)}) collective-permute-start(bf16[256,128]{1,0:T(8,128)(2,1)S(1)} %get-tuple-element.39), channel_id=1, source_target_pairs={{0,4},{4,0},{8,12},{12,8},{16,20},{20,16},{24,28},{28,24},{32,36},... | collective-permute-start | bytes 196616 | tf_op jit(solution)/shard_map/ppermute | solution.py:241
  10.0 6.9 %collective-permute-start.3 = (bf16[256,128]{1,0:T(8,128)(2,1)S(1)}, bf16[256,128]{1,0:T(8,128)(2,1)S(1)}, u32[]{:S(2)}, u32[]{:S(2)}) collective-permute-start(bf16[256,128]{1,0:T(8,128)(2,1)S(1)} %get-tuple-element.40), channel_id=1, source_target_pairs={{0,64},{4,68},{8,72},{12,76},{16,80},{20,84},{24,88},{28,92},{32,9... | collective-permute-start | bytes 196616 | tf_op jit(solution)/shard_map/ppermute | solution.py:241
  13.3 16.8 %all-to-all-start = ((bf16[4,512,256]{2,1,0:T(8,128)(2,1)}), bf16[4,512,256]{2,1,0:T(8,128)(2,1)S(1)}, u32[]{:S(2)}, u32[]{:S(2)}) async-start(bf16[4,512,256]{2,1,0:T(8,128)(2,1)} %shard_map.67), calls=%async_computation | async-start | bytes 2097152 | tf_op jit(solution)/shard_map/all_to_all | solution.py:260
  16.9 7.4 %collective-permute-start.4 = (bf16[256,128]{1,0:T(8,128)(2,1)S(1)}, bf16[256,128]{1,0:T(8,128)(2,1)S(1)}, u32[]{:S(2)}, u32[]{:S(2)}) collective-permute-start(bf16[256,128]{1,0:T(8,128)(2,1)S(1)} %select_select_fusion.1), channel_id=1, source_target_pairs={{0,48},{4,52},{8,56},{12,60},{16,32},{20,36},{24,40},{28,44},{32,1... | collective-permute-start | bytes 196616 | tf_op jit(solution)/shard_map/ppermute | solution.py:241
  20.8 4.6 %collective-permute-start.5 = (bf16[256,128]{1,0:T(8,128)(2,1)S(1)}, bf16[256,128]{1,0:T(8,128)(2,1)S(1)}, u32[]{:S(2)}, u32[]{:S(2)}) collective-permute-start(bf16[256,128]{1,0:T(8,128)(2,1)S(1)} %select_select_fusion.1), channel_id=1, source_target_pairs={{0,32},{4,36},{8,40},{12,44},{16,48},{20,52},{24,56},{28,60},{32,0... | collective-permute-start | bytes 196616 | tf_op jit(solution)/shard_map/ppermute | solution.py:241
  20.8 4.6 %collective-permute-start.6 = (bf16[256,128]{1,0:T(8,128)(2,1)S(1)}, bf16[256,128]{1,0:T(8,128)(2,1)S(1)}, u32[]{:S(2)}, u32[]{:S(2)}) collective-permute-start(bf16[256,128]{1,0:T(8,128)(2,1)S(1)} %select_select_fusion.1), channel_id=1, source_target_pairs={{0,16},{4,20},{8,24},{12,28},{16,0},{20,4},{24,8},{28,12},{32,48},... | collective-permute-start | bytes 196616 | tf_op jit(solution)/shard_map/ppermute | solution.py:241
  23.3 1.0 %copy-start = (bf16[256,2048]{1,0:T(8,128)(2,1)}, bf16[256,2048]{1,0:T(8,128)(2,1)S(1)}, u32[]{:S(2)}) copy-start(bf16[256,2048]{1,0:T(8,128)(2,1)S(1)} %get-tuple-element.51.rest_2_) | copy-start | bytes 3145732
  25.4 4.7 %collective-permute-start.7 = (bf16[256,128]{1,0:T(8,128)(2,1)S(1)}, bf16[256,128]{1,0:T(8,128)(2,1)S(1)}, u32[]{:S(2)}, u32[]{:S(2)}) collective-permute-start(bf16[256,128]{1,0:T(8,128)(2,1)S(1)} %select_select_fusion), channel_id=1, source_target_pairs={{0,12},{4,8},{8,4},{12,0},{16,28},{20,24},{24,20},{28,16},{32,44},... | collective-permute-start | bytes 196616 | tf_op jit(solution)/shard_map/ppermute | solution.py:241
  30.1 21.0 %copy-start.1 = (bf16[256,2048]{1,0:T(8,128)(2,1)S(1)}, bf16[256,2048]{1,0:T(8,128)(2,1)}, u32[]{:S(2)}) copy-start(bf16[256,2048]{1,0:T(8,128)(2,1)} %copy-done) | copy-start | bytes 3145732

commit v4 on v3

--- a/solution.py
+++ b/solution.py
@@ -37,6 +37,10 @@
     return pltpu.CompilerParams(vmem_limit_bytes=mib * 2**20)
 
 
+def mine(info):
+    return pl.ds(pl.multiple_of(info[0] * 4 * HD, 4 * HD), 4 * HD)
+
+
 def normalise(tokens, gain):
     widened = tokens.astype(F32)
     centred = widened - jnp.mean(widened, axis=-1, keepdims=True)
@@ -44,29 +48,18 @@
     return (centred * lax.rsqrt(variance + 1e-05) * gain).astype(BF16)
 
 
-def fetch_heads(weight, heads, dst, offset, sem):
-    at = pl.ds(pl.multiple_of(heads * HD, HD), HD)
-    copy = pltpu.make_async_copy(weight.at[:, at], dst.at[:, pl.ds(offset, HD)], sem)
-    copy.start()
-    return copy
-
-
-def own_kernel(info, tokens, gain_ref, wq, wk, wv, out, columns, gain, kv_columns, rows, sems):
-    first = pltpu.make_async_copy(tokens, rows, sems.at[12])
-    first.start()
-    second = pltpu.make_async_copy(gain_ref, gain, sems.at[13])
-    second.start()
-    copies = [fetch_heads(wq, info[1 + j], columns, j * HD, sems.at[j]) for j in range(4)]
-    for j in range(4):
-        for k, weight in enumerate((wk, wv)):
-            copies.append(
-                fetch_heads(weight, info[1 + j], kv_columns, (2 * j + k) * HD, sems.at[4 + 2 * j + k])
-            )
-    first.wait()
-    second.wait()
+def own_kernel(info, tokens, gain_ref, wq, out, columns, gain, rows, sems):
+    copies = [
+        pltpu.make_async_copy(tokens, rows, sems.at[0]),
+        pltpu.make_async_copy(gain_ref, gain, sems.at[1]),
+        pltpu.make_async_copy(wq.at[:, mine(info)], columns, sems.at[2]),
+    ]
+    for copy in copies:
+        copy.start()
+    copies[0].wait()
+    copies[1].wait()
     out[...] = normalise(rows[...], gain[...])
-    for copy in copies:
-        copy.wait()
+    copies[2].wait()
 
 
 def query_kernel(info, tokens, own, gain, weight, out, q0, q1, q2, q3):
@@ -78,15 +71,18 @@
         q[...] = queries[:, j * HD : (j + 1) * HD]
 
 
-def kv_kernel(own, other, weight, out, done, sems):
+def kv_kernel(info, own, other, wk, wv, out, done, sems):
     writes = []
     for k, rows in enumerate((own, other)):
         at = pl.ds(k * ROWS, ROWS)
-        projected = jnp.dot(rows[...], weight[...], preferred_element_type=F32).astype(BF16)
-        for j in range(4):
-            done[j, at, :] = projected[:, j * 2 * HD : (j + 1) * 2 * HD]
-        writes.append(pltpu.make_async_copy(done.at[:, at], out.at[:, at], sems.at[k]))
-        writes[-1].start()
+        keys = jnp.dot(rows[...], wk[:, mine(info)], preferred_element_type=F32).astype(BF16)
+        values = jnp.dot(rows[...], wv[:, mine(info)], preferred_element_type=F32).astype(BF16)
+        for h in range(4):
+            done[h, at, pl.ds(0, HD)] = keys[:, h * HD : (h + 1) * HD]
+            done[h, at, pl.ds(HD, HD)] = values[:, h * HD : (h + 1) * HD]
+        for h in range(4):
+            writes.append(pltpu.make_async_copy(done.at[h, at], out.at[info[1 + h], at], sems.at[4 * k + h]))
+            writes[-1].start()
     for write in writes:
         write.wait()
 
@@ -198,13 +194,10 @@
     yl = lax.axis_index("yl")
     gain = norm_gain.reshape(1, D)
     in_hbm = functools.partial(pltpu.with_memory_space_constraint, memory_space=pltpu.HBM)
-    gain, query_weight, key_weight, value_weight, out_weight = map(
-        in_hbm, (gain, query_weight, key_weight, value_weight, out_weight)
-    )
+    gain, query_weight, out_weight = map(in_hbm, (gain, query_weight, out_weight))
 
     chips = [(b, z, (x & 2) + a) for b in range(2) for a in range(2)]
-    info = [core]
-    info += [head_of(b, c, a, core) for b, c, a in chips]
+    info = [core] + [(h & 1) * 2 + ((h >> 1) ^ (x >> 1)) for h in range(4)]
     for b, c, a in chips:
         for half in range(2):
             info.append((((b * 4 + c) * 4 + a) * 2 + (core ^ half)) * ROWS)
@@ -214,15 +207,15 @@
     )
 
     other_raw = lax.ppermute(context, "core", SWAP)
-    own, query_columns, gain, kv_columns = pl.pallas_call(
+    own, query_columns, gain = pl.pallas_call(
         own_kernel,
-        out_shape=[shape(ROWS, D), shape(D, 4 * HD), shape(1, D, dtype=F32), shape(D, 8 * HD)],
-        in_specs=[SMEM] + [HBM] * 5,
-        out_specs=[VMEM] * 4,
-        scratch_shapes=[pltpu.VMEM((ROWS, D), BF16), pltpu.SemaphoreType.DMA((14,))],
+        out_shape=[shape(ROWS, D), shape(D, 4 * HD), shape(1, D, dtype=F32)],
+        in_specs=[SMEM] + [HBM] * 3,
+        out_specs=[VMEM] * 3,
+        scratch_shapes=[pltpu.VMEM((ROWS, D), BF16), pltpu.SemaphoreType.DMA((3,))],
         compiler_params=params(16),
         cost_estimate=pl.CostEstimate(flops=2**23, bytes_accessed=2**23, transcendentals=0),
-    )(info, in_hbm(context), gain, query_weight, key_weight, value_weight)
+    )(info, in_hbm(context), gain, query_weight)
     other, *queries = pl.pallas_call(
         query_kernel,
         out_shape=[shape(ROWS, D)] + [shape(LAT, HD)] * 4,
@@ -240,22 +233,22 @@
                     pairs.append(((b * 4 + c) * 4 + a, ((b ^ dy) * 4 + (c ^ dz)) * 4 + (a ^ dx)))
         return lax.ppermute(value, ("yl", "z", "xh", "xl"), pairs)
 
-    by_x = hop(queries[2], 1, 0, 0)
-    by_y = hop(queries[1], 0, 0, 1)
-    by_xy = hop(queries[0], 1, 0, 1)
+    by_x = hop(queries[3], 1, 0, 0)
+    by_y = hop(queries[0], 0, 0, 1)
+    by_xy = hop(queries[2], 1, 0, 1)
 
     kv = pl.pallas_call(
         kv_kernel,
         out_shape=shape(4, 2 * ROWS, 2 * HD),
-        in_specs=[VMEM] * 3,
+        in_specs=[SMEM] + [VMEM] * 4,
         out_specs=HBM,
-        scratch_shapes=[pltpu.VMEM((4, 2 * ROWS, 2 * HD), BF16), pltpu.SemaphoreType.DMA((2,))],
+        scratch_shapes=[pltpu.VMEM((4, 2 * ROWS, 2 * HD), BF16), pltpu.SemaphoreType.DMA((8,))],
         compiler_params=params(24),
         cost_estimate=pl.CostEstimate(flops=2**31, bytes_accessed=2**22, transcendentals=0),
-    )(own, other, kv_columns)
+    )(info, own, other, key_weight, value_weight)
 
     query = jnp.where(
-        odd, jnp.where(low, by_xy, by_x), jnp.where(low, by_y, queries[3])
+        odd, jnp.where(low, by_xy, by_x), jnp.where(low, by_y, queries[1])
     )
     kv = lax.all_to_all(kv, ("yl", "xl"), 0, 0)
     along = [query] + [hop(query, 0, d, 0) for d in (1, 2, 3)]

time: 53 us -> 52.5 us (level)
    pallas_call x1, Pallas kernels: 3.94 us -> 2.76 us  [local(): pl.pallas_call(own_kernel, out_shape=[shape(ROWS, D), shape(D, 4 * HD), s...]
    pallas_call x1, Pallas kernels: 3.16 us -> 3.79 us  [local(): pl.pallas_call(kv_kernel, out_shape=shape(4, 2 * ROWS, 2 * HD), in_specs=...]
  transfers between devices with their start and end apart: 9 -> 9, of which waited for: 2 -> 2; matrix products, arithmetic and copies ran while one was open for 0% -> 0% of each run, Pallas kernels for 17% -> 16%
where the time goes in v4:
time: 52.5 us; the launch traced here: 52.2 us
  blocking collectives  19.2 us (37%)
  starting transfers between devices  15.3 us (29%)
  Pallas kernels  13.7 us (26%)
  waiting for transfers between devices  2.73 us (5%)
  local copies, waits for them, and re-layouts  1.1 us (2%)
    all_to_all x1, blocking collectives, local(): parts = lax.all_to_all(parts.reshape(64, 8, HD), CTX_AXES, 0, 0)  19.2 us
    ppermute x7, starting transfers between devices, hop(): return lax.ppermute(value, ('yl', 'z', 'xh', 'xl'), pairs)  10.4 us
    pallas_call x1, Pallas kernels, local(): pl.pallas_call(kv_kernel, out_shape=shape(4, 2 * ROWS, 2 * HD), in_specs=...  3.79 us
    all_to_all x1, starting transfers between devices, local(): kv = lax.all_to_all(kv, ('yl', 'xl'), 0, 0)  3.55 us
    pallas_call x1, Pallas kernels, local(): pl.pallas_call(own_kernel, out_shape=[shape(ROWS, D), shape(D, 4 * HD), s...  2.76 us
    ppermute x7, waiting for transfers between devices, hop(): return lax.ppermute(value, ('yl', 'z', 'xh', 'xl'), pairs)  2.72 us
    pallas_call x1, Pallas kernels, local(): pl.pallas_call(fetch_kernel, out_shape=[shape(2 * HD, D)] * FETCHED, in_s...  1.88 us
    pallas_call x1, Pallas kernels, local(): pl.pallas_call(query_kernel, out_shape=[shape(ROWS, D)] + [shape(LAT, HD)...  1.87 us
  transfers between devices with their start and end apart: 9, of which 2 were waited for; matrix products, arithmetic and copies ran while one was open for 0% of the time, Pallas kernels for 16%

profile of v4, /device:TPU:1, one launch (start us, length us, event | category | flops | bytes accessed | tf_op | source)
XLA Modules:
  0.0 52.2 jit_solution(6977035452085437827)
XLA Ops:
  0.0 1.4 %collective-permute-start = (bf16[256,2048]{1,0:T(8,128)(2,1)}, bf16[256,2048]{1,0:T(8,128)(2,1)S(1)}, u32[]{:S(2)}, u32[]{:S(2)}) collective-permute-start(bf16[256,2048]{1,0:T(8,128)(2,1)} %tokens.1), channel_id=1, source_target_pairs={{0,2},{2,0},{1,3},{3,1},{4,6},{6,4},{5,7},{7,5},{8,10},{10,8},{9,1... | collective-permute-start | bytes 3145736 | tf_op jit(solution)/shard_map/ppermute | solution.py:209
  1.4 0.1 stack.55.info
  1.5 0.0 copy-start
  1.5 0.0 copy-start.1
  1.5 2.8 %shard_map.64 = (bf16[256,2048]{1,0:T(8,128)(2,1)S(1)}, bf16[2048,512]{1,0:T(8,128)(2,1)S(1)}, f32[1,2048]{1,0:T(1,128)S(1)}) custom-call(s32[13]{0:T(128)S(1)} %stack.55.info, bf16[256,2048]{1,0:T(8,128)(2,1)} %tokens.1, f32[1,2048]{1,0:T(1,128)} %bitcast.16, bf16[2048,1024]{1,0:T(8,128)(2,1)} %wq.1), custom_call_target="tpu_custom_call" | custom-call | flops 8388608 | bytes 8388608 | tf_op jit(solution)/shard_map/pallas_call | solution.py:210
  4.3 0.0 collective-permute-done.tokens
  4.3 1.9 %shard_map.65 = (bf16[256,2048]{1,0:T(8,128)(2,1)S(1)}, bf16[256,128]{1,0:T(8,128)(2,1)S(1)}, bf16[256,128]{1,0:T(8,128)(2,1)S(1)}, bf16[256,128]{1,0:T(8,128)(2,1)S(1)}, bf16[256,128]{1,0:T(8,128)(2,1)S(1)}) custom-call(s32[13]{0:T(128)S(1)} %stack.55.info, bf16[256,2048]{1,0:T(8,128)(2,1)S(1)} %collective-permute-done.tokens, ...), custom_call_target="tpu_custom_call" | custom-call | flops 536870912 | bytes 2097152 | tf_op jit(solution)/shard_map/pallas_call | solution.py:219
  6.2 2.4 %collective-permute-start.1 = (bf16[256,128]{1,0:T(8,128)(2,1)S(1)}, bf16[256,128]{1,0:T(8,128)(2,1)S(1)}, u32[]{:S(2)}, u32[]{:S(2)}) collective-permute-start(bf16[256,128]{1,0:T(8,128)(2,1)S(1)} %get-tuple-element.37), channel_id=1, source_target_pairs={{0,68},{4,64},{8,76},{12,72},{16,84},{20,80},{24,92},{28,88},{32,1... | collective-permute-start | bytes 196616 | tf_op jit(solution)/shard_map/ppermute | solution.py:234
  8.6 0.3 collective-permute-start.2
  8.8 0.1 collective-permute-start.3
  9.0 0.0 copy-done
  9.0 0.0 copy-done.1
  9.0 3.8 %shard_map.67 = bf16[4,512,256]{2,1,0:T(8,128)(2,1)} custom-call(s32[13]{0:T(128)S(1)} %stack.55.info, bf16[256,2048]{1,0:T(8,128)(2,1)S(1)} %get-tuple-element.34.own, bf16[256,2048]{1,0:T(8,128)(2,1)S(1)} %get-tuple-element.45.other, bf16[2048,1024]{1,0:T(8,128)(2,1)S(1)} %copy-done, bf16[2048,1024]{1,0:T(8,128)(2,1)S(1)} %copy-done.1), custom_call_target="tpu_custom_call" | custom-call | flops 2147483648 | bytes 4194304 | tf_op jit(solution)/shard_map/pallas_call | solution.py:240
  12.8 3.6 %all-to-all-start = ((bf16[4,512,256]{2,1,0:T(8,128)(2,1)}), bf16[4,512,256]{2,1,0:T(8,128)(2,1)S(1)}, u32[]{:S(2)}, u32[]{:S(2)}) async-start(bf16[4,512,256]{2,1,0:T(8,128)(2,1)} %shard_map.67), calls=%async_computation | async-start | bytes 2097152 | tf_op jit(solution)/shard_map/all_to_all | solution.py:253
  16.3 0.0 collective-permute-done.1
  16.3 0.0 collective-permute-done.2
  16.3 0.0 collective-permute-done.3
  16.4 3.9 %collective-permute-start.4 = (bf16[256,128]{1,0:T(8,128)(2,1)S(1)}, bf16[256,128]{1,0:T(8,128)(2,1)S(1)}, u32[]{:S(2)}, u32[]{:S(2)}) collective-permute-start(bf16[256,128]{1,0:T(8,128)(2,1)S(1)} %select_select_fusion.1), channel_id=1, source_target_pairs={{0,48},{4,52},{8,56},{12,60},{16,32},{20,36},{24,40},{28,44},{32,1... | collective-permute-start | bytes 196616 | tf_op jit(solution)/shard_map/ppermute | solution.py:234
  20.3 0.0 collective-permute-start.5
  20.3 0.7 %collective-permute-start.6 = (bf16[256,128]{1,0:T(8,128)(2,1)S(1)}, bf16[256,128]{1,0:T(8,128)(2,1)S(1)}, u32[]{:S(2)}, u32[]{:S(2)}) collective-permute-start(bf16[256,128]{1,0:T(8,128)(2,1)S(1)} %select_select_fusion.1), channel_id=1, source_target_pairs={{0,16},{4,20},{8,24},{12,28},{16,0},{20,4},{24,8},{28,12},{32,48},... | collective-permute-start | bytes 196616 | tf_op jit(solution)/shard_map/ppermute | solution.py:234
  20.9 1.9 %shard_map.66 = (bf16[256,2048]{1,0:T(8,128)(2,1)S(1)}, bf16[256,2048]{1,0:T(8,128)(2,1)S(1)}, bf16[256,2048]{1,0:T(8,128)(2,1)S(1)}) custom-call(bf16[1024,2048]{1,0:T(8,128)(2,1)} %wo.3), custom_call_target="tpu_custom_call" | custom-call | flops 1 | bytes 67108864 | tf_op jit(solution)/shard_map/pallas_call | solution.py:255
  22.8 0.0 copy-start.2
  22.8 1.0 %copy-done.2 = bf16[256,2048]{1,0:T(8,128)(2,1)} copy-done((bf16[256,2048]{1,0:T(8,128)(2,1)}, bf16[256,2048]{1,0:T(8,128)(2,1)S(1)}, u32[]{:S(2)}) %copy-start.2) | copy-done | bytes 1048600
  23.8 0.0 collective-permute-done.4
  23.8 1.1 %collective-permute-done.5 = bf16[256,128]{1,0:T(8,128)(2,1)S(1)} collective-permute-done((bf16[256,128]{1,0:T(8,128)(2,1)S(1)}, bf16[256,128]{1,0:T(8,128)(2,1)S(1)}, u32[]{:S(2)}, u32[]{:S(2)}) %collective-permute-start.5) | collective-permute-done | bytes 65568 | tf_op jit(solution)/shard_map/ppermute | solution.py:234
  24.9 0.0 collective-permute-done.6
  24.9 3.0 %collective-permute-start.7 = (bf16[256,128]{1,0:T(8,128)(2,1)S(1)}, bf16[256,128]{1,0:T(8,128)(2,1)S(1)}, u32[]{:S(2)}, u32[]{:S(2)}) collective-permute-start(bf16[256,128]{1,0:T(8,128)(2,1)S(1)} %select_select_fusion), channel_id=1, source_target_pairs={{0,12},{4,8},{8,4},{12,0},{16,28},{20,24},{24,20},{28,16},{32,44},... | collective-permute-start | bytes 196616 | tf_op jit(solution)/shard_map/ppermute | solution.py:234
  27.9 1.7 %collective-permute-done.7 = bf16[256,128]{1,0:T(8,128)(2,1)S(1)} collective-permute-done((bf16[256,128]{1,0:T(8,128)(2,1)S(1)}, bf16[256,128]{1,0:T(8,128)(2,1)S(1)}, u32[]{:S(2)}, u32[]{:S(2)}) %collective-permute-start.7) | collective-permute-done | bytes 65568 | tf_op jit(solution)/shard_map/ppermute | solution.py:234
  29.6 0.0 all-to-all-done.kv
  29.6 0.0 copy-start.3
  29.6 1.8 %shard_map.68 = (bf16[32,2,8,128]{3,2,1,0:T(8,128)(2,1)S(1)}, bf16[256,2048]{1,0:T(8,128)(2,1)S(1)}) custom-call(s32[13]{0:T(128)S(1)} %stack.55.info, bf16[256,128]{1,0:T(8,128)(2,1)S(1)} %broadcast_select_fusion.query, bf16[4,512,256]{2,1,0:T(8,128)(2,1)S(1)} %all-to-all-done.kv, bf16[1024,2048]{1,0:T(8,128)(2,1)} %wo.3), custom_call_target="tpu_custom_call" | custom-call | flops 268435456 | bytes 2097152 | tf_op jit(solution)/shard_map/pallas_call | solution.py:271
  31.4 19.2 %all_to_all.10.parts = bf16[64,8,128]{2,1,0:T(8,128)(2,1)S(1)} all-to-all(bf16[64,8,128]{2,1,0:T(8,128)(2,1)S(1)} %bitcast.15), channel_id=1, replica_groups=mesh['yl'=2,'z'=4,'xh'=2,'xl'=2,'core'=2,'batch'=2] {'yl','z','xh','xl',..., dimensions={0} | all-to-all | bytes 262144 | tf_op jit(solution)/shard_map/all_to_all | solution.py:280
  50.6 0.0 copy-done.3
  50.6 1.6 %shard_map.69 = bf16[4,2048]{1,0:T(4,128)(2,1)} custom-call(bf16[64,8,128]{2,1,0:T(8,128)(2,1)S(1)} %all_to_all.10.parts, bf16[256,2048]{1,0:T(8,128)(2,1)S(1)} %get-tuple-element.47.rest_0_, bf16[256,2048]{1,0:T(8,128)(2,1)S(1)} %get-tuple-element.48.rest_1_, bf16[256,2048]{1,0:T(8,128)(2,1)S(1)} %copy-done.3, bf16[256,2048]{1,0:T(8,128)(2,1)S(1)} %get-tuple-element.50.rest_3_), custom_call_target="tpu_custom_call" | custom-call | flops 33554432 | bytes 4194304 | tf_op jit(solution)/shard_map/pallas_call | solution.py:281
  (3 shorter events, 0.0 us)
Async XLA Ops:
  0.0 4.3 %collective-permute-start = (bf16[256,2048]{1,0:T(8,128)(2,1)}, bf16[256,2048]{1,0:T(8,128)(2,1)S(1)}, u32[]{:S(2)}, u32[]{:S(2)}) collective-permute-start(bf16[256,2048]{1,0:T(8,128)(2,1)} %tokens.1), channel_id=1, source_target_pairs={{0,2},{2,0},{1,3},{3,1},{4,6},{6,4},{5,7},{7,5},{8,10},{10,8},{9,1... | collective-permute-start | bytes 3145736 | tf_op jit(solution)/shard_map/ppermute | solution.py:209
  1.5 7.5 %copy-start = (bf16[2048,1024]{1,0:T(8,128)(2,1)S(1)}, bf16[2048,1024]{1,0:T(8,128)(2,1)}, u32[]{:S(2)}) copy-start(bf16[2048,1024]{1,0:T(8,128)(2,1)} %wk.1) | copy-start | bytes 12582916
  1.5 7.4 %copy-start.1 = (bf16[2048,1024]{1,0:T(8,128)(2,1)S(1)}, bf16[2048,1024]{1,0:T(8,128)(2,1)}, u32[]{:S(2)}) copy-start(bf16[2048,1024]{1,0:T(8,128)(2,1)} %wv.1) | copy-start | bytes 12582916
  6.2 10.1 %collective-permute-start.1 = (bf16[256,128]{1,0:T(8,128)(2,1)S(1)}, bf16[256,128]{1,0:T(8,128)(2,1)S(1)}, u32[]{:S(2)}, u32[]{:S(2)}) collective-permute-start(bf16[256,128]{1,0:T(8,128)(2,1)S(1)} %get-tuple-element.37), channel_id=1, source_target_pairs={{0,68},{4,64},{8,76},{12,72},{16,84},{20,80},{24,92},{28,88},{32,1... | collective-permute-start | bytes 196616 | tf_op jit(solution)/shard_map/ppermute | solution.py:234
  8.6 7.7 %collective-permute-start.2 = (bf16[256,128]{1,0:T(8,128)(2,1)S(1)}, bf16[256,128]{1,0:T(8,128)(2,1)S(1)}, u32[]{:S(2)}, u32[]{:S(2)}) collective-permute-start(bf16[256,128]{1,0:T(8,128)(2,1)S(1)} %get-tuple-element.38), channel_id=1, source_target_pairs={{0,4},{4,0},{8,12},{12,8},{16,20},{20,16},{24,28},{28,24},{32,36},... | collective-permute-start | bytes 196616 | tf_op jit(solution)/shard_map/ppermute | solution.py:234
  8.8 7.5 %collective-permute-start.3 = (bf16[256,128]{1,0:T(8,128)(2,1)S(1)}, bf16[256,128]{1,0:T(8,128)(2,1)S(1)}, u32[]{:S(2)}, u32[]{:S(2)}) collective-permute-start(bf16[256,128]{1,0:T(8,128)(2,1)S(1)} %get-tuple-element.39), channel_id=1, source_target_pairs={{0,64},{4,68},{8,72},{12,76},{16,80},{20,84},{24,88},{28,92},{32,9... | collective-permute-start | bytes 196616 | tf_op jit(solution)/shard_map/ppermute | solution.py:234
  12.8 16.8 %all-to-all-start = ((bf16[4,512,256]{2,1,0:T(8,128)(2,1)}), bf16[4,512,256]{2,1,0:T(8,128)(2,1)S(1)}, u32[]{:S(2)}, u32[]{:S(2)}) async-start(bf16[4,512,256]{2,1,0:T(8,128)(2,1)} %shard_map.67), calls=%async_computation | async-start | bytes 2097152 | tf_op jit(solution)/shard_map/all_to_all | solution.py:253
  16.4 7.4 %collective-permute-start.4 = (bf16[256,128]{1,0:T(8,128)(2,1)S(1)}, bf16[256,128]{1,0:T(8,128)(2,1)S(1)}, u32[]{:S(2)}, u32[]{:S(2)}) collective-permute-start(bf16[256,128]{1,0:T(8,128)(2,1)S(1)} %select_select_fusion.1), channel_id=1, source_target_pairs={{0,48},{4,52},{8,56},{12,60},{16,32},{20,36},{24,40},{28,44},{32,1... | collective-permute-start | bytes 196616 | tf_op jit(solution)/shard_map/ppermute | solution.py:234
  20.3 4.6 %collective-permute-start.5 = (bf16[256,128]{1,0:T(8,128)(2,1)S(1)}, bf16[256,128]{1,0:T(8,128)(2,1)S(1)}, u32[]{:S(2)}, u32[]{:S(2)}) collective-permute-start(bf16[256,128]{1,0:T(8,128)(2,1)S(1)} %select_select_fusion.1), channel_id=1, source_target_pairs={{0,32},{4,36},{8,40},{12,44},{16,48},{20,52},{24,56},{28,60},{32,0... | collective-permute-start | bytes 196616 | tf_op jit(solution)/shard_map/ppermute | solution.py:234
  20.3 4.6 %collective-permute-start.6 = (bf16[256,128]{1,0:T(8,128)(2,1)S(1)}, bf16[256,128]{1,0:T(8,128)(2,1)S(1)}, u32[]{:S(2)}, u32[]{:S(2)}) collective-permute-start(bf16[256,128]{1,0:T(8,128)(2,1)S(1)} %select_select_fusion.1), channel_id=1, source_target_pairs={{0,16},{4,20},{8,24},{12,28},{16,0},{20,4},{24,8},{28,12},{32,48},... | collective-permute-start | bytes 196616 | tf_op jit(solution)/shard_map/ppermute | solution.py:234
  22.8 1.0 %copy-start.2 = (bf16[256,2048]{1,0:T(8,128)(2,1)}, bf16[256,2048]{1,0:T(8,128)(2,1)S(1)}, u32[]{:S(2)}) copy-start(bf16[256,2048]{1,0:T(8,128)(2,1)S(1)} %get-tuple-element.49.rest_2_) | copy-start | bytes 3145732
  24.9 4.7 %collective-permute-start.7 = (bf16[256,128]{1,0:T(8,128)(2,1)S(1)}, bf16[256,128]{1,0:T(8,128)(2,1)S(1)}, u32[]{:S(2)}, u32[]{:S(2)}) collective-permute-start(bf16[256,128]{1,0:T(8,128)(2,1)S(1)} %select_select_fusion), channel_id=1, source_target_pairs={{0,12},{4,8},{8,4},{12,0},{16,28},{20,24},{24,20},{28,16},{32,44},... | collective-permute-start | bytes 196616 | tf_op jit(solution)/shard_map/ppermute | solution.py:234
  29.6 21.0 %copy-start.3 = (bf16[256,2048]{1,0:T(8,128)(2,1)S(1)}, bf16[256,2048]{1,0:T(8,128)(2,1)}, u32[]{:S(2)}) copy-start(bf16[256,2048]{1,0:T(8,128)(2,1)} %copy-done.2) | copy-start | bytes 3145732

commit v5 on v4

--- a/solution.py
+++ b/solution.py
@@ -15,6 +15,7 @@
 ROWS = 256
 CTX = 16384
 MINE = 4
+PIECES = 2
 FETCHED = 3
 F32 = jnp.float32
 BF16 = jnp.bfloat16
@@ -48,41 +49,46 @@
     return (centred * lax.rsqrt(variance + 1e-05) * gain).astype(BF16)
 
 
-def own_kernel(info, tokens, gain_ref, wq, out, columns, gain, rows, sems):
-    copies = [
-        pltpu.make_async_copy(tokens, rows, sems.at[0]),
-        pltpu.make_async_copy(gain_ref, gain, sems.at[1]),
-        pltpu.make_async_copy(wq.at[:, mine(info)], columns, sems.at[2]),
+def own_kernel(info, tokens, gain_ref, wk, wv, out, keys, values, gain, rows, sems):
+    step = ROWS // PIECES
+    pieces = [pl.ds(j * step, step) for j in range(PIECES)]
+    first = pltpu.make_async_copy(gain_ref, gain, sems.at[0])
+    copies = [pltpu.make_async_copy(tokens.at[at], rows.at[at], sems.at[3 + j]) for j, at in enumerate(pieces)]
+    weights = [
+        pltpu.make_async_copy(wk.at[:, mine(info)], keys, sems.at[1]),
+        pltpu.make_async_copy(wv.at[:, mine(info)], values, sems.at[2]),
     ]
-    for copy in copies:
+    for copy in (first, *copies, *weights):
         copy.start()
-    copies[0].wait()
-    copies[1].wait()
-    out[...] = normalise(rows[...], gain[...])
-    copies[2].wait()
-
-
-def query_kernel(info, tokens, own, gain, weight, out, q0, q1, q2, q3):
-    out[...] = normalise(tokens[...], gain[...])
-    latents = jnp.where(info[0] == 1, own[...], out[...])
-    queries = jnp.dot(latents, weight[...], preferred_element_type=F32) * HD ** (-0.5)
-    queries = queries.astype(BF16)
-    for j, q in enumerate((q0, q1, q2, q3)):
-        q[...] = queries[:, j * HD : (j + 1) * HD]
-
-
-def kv_kernel(info, own, other, wk, wv, out, done, sems):
+    first.wait()
+    for at, copy in zip(pieces, copies):
+        copy.wait()
+        out[at, :] = normalise(rows[at, :], gain[...])
+    for copy in weights:
+        copy.wait()
+
+
+def project_kernel(info, tokens, own, gain, wk, wv, wq, q0, q1, q2, q3, out, other, columns, done, sems):
+    fetch = pltpu.make_async_copy(wq.at[:, mine(info)], columns, sems.at[8])
+    fetch.start()
+    other[...] = normalise(tokens[...], gain[...])
     writes = []
     for k, rows in enumerate((own, other)):
         at = pl.ds(k * ROWS, ROWS)
-        keys = jnp.dot(rows[...], wk[:, mine(info)], preferred_element_type=F32).astype(BF16)
-        values = jnp.dot(rows[...], wv[:, mine(info)], preferred_element_type=F32).astype(BF16)
+        keys = jnp.dot(rows[...], wk[...], preferred_element_type=F32).astype(BF16)
+        values = jnp.dot(rows[...], wv[...], preferred_element_type=F32).astype(BF16)
         for h in range(4):
             done[h, at, pl.ds(0, HD)] = keys[:, h * HD : (h + 1) * HD]
             done[h, at, pl.ds(HD, HD)] = values[:, h * HD : (h + 1) * HD]
         for h in range(4):
             writes.append(pltpu.make_async_copy(done.at[h, at], out.at[info[1 + h], at], sems.at[4 * k + h]))
             writes[-1].start()
+    fetch.wait()
+    latents = jnp.where(info[0] == 1, own[...], other[...])
+    queries = jnp.dot(latents, columns[...], preferred_element_type=F32) * HD ** (-0.5)
+    queries = queries.astype(BF16)
+    for j, q in enumerate((q0, q1, q2, q3)):
+        q[...] = queries[:, j * HD : (j + 1) * HD]
     for write in writes:
         write.wait()
 
@@ -194,7 +200,9 @@
     yl = lax.axis_index("yl")
     gain = norm_gain.reshape(1, D)
     in_hbm = functools.partial(pltpu.with_memory_space_constraint, memory_space=pltpu.HBM)
-    gain, query_weight, out_weight = map(in_hbm, (gain, query_weight, out_weight))
+    gain, query_weight, key_weight, value_weight, out_weight = map(
+        in_hbm, (gain, query_weight, key_weight, value_weight, out_weight)
+    )
 
     chips = [(b, z, (x & 2) + a) for b in range(2) for a in range(2)]
     info = [core] + [(h & 1) * 2 + ((h >> 1) ^ (x >> 1)) for h in range(4)]
@@ -207,23 +215,29 @@
     )
 
     other_raw = lax.ppermute(context, "core", SWAP)
-    own, query_columns, gain = pl.pallas_call(
+    own, key_columns, value_columns, gain = pl.pallas_call(
         own_kernel,
-        out_shape=[shape(ROWS, D), shape(D, 4 * HD), shape(1, D, dtype=F32)],
-        in_specs=[SMEM] + [HBM] * 3,
-        out_specs=[VMEM] * 3,
-        scratch_shapes=[pltpu.VMEM((ROWS, D), BF16), pltpu.SemaphoreType.DMA((3,))],
+        out_shape=[shape(ROWS, D), shape(D, 4 * HD), shape(D, 4 * HD), shape(1, D, dtype=F32)],
+        in_specs=[SMEM] + [HBM] * 4,
+        out_specs=[VMEM] * 4,
+        scratch_shapes=[pltpu.VMEM((ROWS, D), BF16), pltpu.SemaphoreType.DMA((3 + PIECES,))],
         compiler_params=params(16),
         cost_estimate=pl.CostEstimate(flops=2**23, bytes_accessed=2**23, transcendentals=0),
-    )(info, in_hbm(context), gain, query_weight)
-    other, *queries = pl.pallas_call(
-        query_kernel,
-        out_shape=[shape(ROWS, D)] + [shape(LAT, HD)] * 4,
-        in_specs=[SMEM] + [VMEM] * 4,
-        out_specs=[VMEM] * 5,
-        compiler_params=params(24),
-        cost_estimate=pl.CostEstimate(flops=2**29, bytes_accessed=2**21, transcendentals=0),
-    )(info, other_raw, own, gain, query_columns)
+    )(info, in_hbm(context), gain, key_weight, value_weight)
+    *queries, kv = pl.pallas_call(
+        project_kernel,
+        out_shape=[shape(LAT, HD)] * 4 + [shape(4, 2 * ROWS, 2 * HD)],
+        in_specs=[SMEM] + [VMEM] * 5 + [HBM],
+        out_specs=[VMEM] * 4 + [HBM],
+        scratch_shapes=[
+            pltpu.VMEM((ROWS, D), BF16),
+            pltpu.VMEM((D, 4 * HD), BF16),
+            pltpu.VMEM((4, 2 * ROWS, 2 * HD), BF16),
+            pltpu.SemaphoreType.DMA((9,)),
+        ],
+        compiler_params=params(32),
+        cost_estimate=pl.CostEstimate(flops=2**31, bytes_accessed=2**22, transcendentals=0),
+    )(info, other_raw, own, gain, key_columns, value_columns, query_weight)
 
     def hop(value, dx, dz, dy):
         pairs = []
@@ -236,16 +250,6 @@
     by_x = hop(queries[3], 1, 0, 0)
     by_y = hop(queries[0], 0, 0, 1)
     by_xy = hop(queries[2], 1, 0, 1)
-
-    kv = pl.pallas_call(
-        kv_kernel,
-        out_shape=shape(4, 2 * ROWS, 2 * HD),
-        in_specs=[SMEM] + [VMEM] * 4,
-        out_specs=HBM,
-        scratch_shapes=[pltpu.VMEM((4, 2 * ROWS, 2 * HD), BF16), pltpu.SemaphoreType.DMA((8,))],
-        compiler_params=params(24),
-        cost_estimate=pl.CostEstimate(flops=2**31, bytes_accessed=2**22, transcendentals=0),
-    )(info, own, other, key_weight, value_weight)
 
     query = jnp.where(
         odd, jnp.where(low, by_xy, by_x), jnp.where(low, by_y, queries[1])

time: 52.5 us -> 51.3 us (0.977)
  Pallas kernels: 13.7 us -> 12.6 us
    pallas_call x2 -> x1, Pallas kernels: 5.67 us -> 4.13 us  [local(): pl.pallas_call(project_kernel, out_shape=[shape(LAT, HD)] * 4 + [shape(4,...]
  transfers between devices with their start and end apart: 9 -> 9, of which waited for: 2 -> 2; matrix products, arithmetic and copies ran while one was open for 0% -> 0% of each run, Pallas kernels for 16% -> 10%
where the time goes in v5:
time: 51.3 us; the launch traced here: 51 us
  blocking collectives  19.2 us (37%)
  starting transfers between devices  15.3 us (30%)
  Pallas kernels  12.6 us (25%)
  waiting for transfers between devices  2.74 us (5%)
  local copies, waits for them, and re-layouts  1.08 us (2%)
    all_to_all x1, blocking collectives, local(): parts = lax.all_to_all(parts.reshape(64, 8, HD), CTX_AXES, 0, 0)  19.2 us
    ppermute x7, starting transfers between devices, hop(): return lax.ppermute(value, ('yl', 'z', 'xh', 'xl'), pairs)  10.4 us
    pallas_call x1, Pallas kernels, local(): pl.pallas_call(project_kernel, out_shape=[shape(LAT, HD)] * 4 + [shape(4,...  4.13 us
    all_to_all x1, starting transfers between devices, local(): kv = lax.all_to_all(kv, ('yl', 'xl'), 0, 0)  3.54 us
    pallas_call x1, Pallas kernels, local(): pl.pallas_call(own_kernel, out_shape=[shape(ROWS, D), shape(D, 4 * HD), s...  3.16 us
    ppermute x7, waiting for transfers between devices, hop(): return lax.ppermute(value, ('yl', 'z', 'xh', 'xl'), pairs)  2.73 us
    pallas_call x1, Pallas kernels, local(): pl.pallas_call(fetch_kernel, out_shape=[shape(2 * HD, D)] * FETCHED, in_s...  1.88 us
    pallas_call x1, Pallas kernels, local(): pl.pallas_call(attend_kernel, out_shape=[shape(LAT // 8, 2, 8, HD)] + [sh...  1.78 us
  transfers between devices with their start and end apart: 9, of which 2 were waited for; matrix products, arithmetic and copies ran while one was open for 0% of the time, Pallas kernels for 10%

profile of v5, /device:TPU:1, one launch (start us, length us, event | category | flops | bytes accessed | tf_op | source)
XLA Modules:
  0.0 51.0 jit_solution(18282251798955378265)
XLA Ops:
  0.0 1.4 %collective-permute-start = (bf16[256,2048]{1,0:T(8,128)(2,1)}, bf16[256,2048]{1,0:T(8,128)(2,1)S(1)}, u32[]{:S(2)}, u32[]{:S(2)}) collective-permute-start(bf16[256,2048]{1,0:T(8,128)(2,1)} %tokens.1), channel_id=1, source_target_pairs={{0,2},{2,0},{1,3},{3,1},{4,6},{6,4},{5,7},{7,5},{8,10},{10,8},{9,1... | collective-permute-start | bytes 3145736 | tf_op jit(solution)/shard_map/ppermute | solution.py:217
  1.4 0.1 stack.55.info
  1.5 3.2 %shard_map.64 = (bf16[256,2048]{1,0:T(8,128)(2,1)S(1)}, bf16[2048,512]{1,0:T(8,128)(2,1)S(1)}, bf16[2048,512]{1,0:T(8,128)(2,1)S(1)}, f32[1,2048]{1,0:T(1,128)S(1)}) custom-call(s32[13]{0:T(128)S(1)} %stack.55.info, bf16[256,2048]{1,0:T(8,128)(2,1)} %tokens.1, f32[1,2048]{1,0:T(1,128)} %bitcast.16, bf16[2048,1024]{1,0:T(8,128)(2,1)} %wk.1, bf16[2048,1024]{1,0:T(8,128)(2,1)} %wv.1), custom_call_target="tpu_custom_call" | custom-call | flops 8388608 | bytes 8388608 | tf_op jit(solution)/shard_map/pallas_call | solution.py:218
  4.7 0.0 collective-permute-done.tokens
  4.7 4.1 %shard_map.65 = (bf16[256,128]{1,0:T(8,128)(2,1)S(1)}, bf16[256,128]{1,0:T(8,128)(2,1)S(1)}, bf16[256,128]{1,0:T(8,128)(2,1)S(1)}, bf16[256,128]{1,0:T(8,128)(2,1)S(1)}, bf16[4,512,256]{2,1,0:T(8,128)(2,1)}) custom-call(s32[13]{0:T(128)S(1)} %stack.55.info, bf16[256,2048]{1,0:T(8,128)(2,1)S(1)} %collective-permute-done.tokens, ...), custom_call_target="tpu_custom_call" | custom-call | flops 2147483648 | bytes 4194304 | tf_op jit(solution)/shard_map/pallas_call | solution.py:227
  8.8 2.4 %collective-permute-start.1 = (bf16[256,128]{1,0:T(8,128)(2,1)S(1)}, bf16[256,128]{1,0:T(8,128)(2,1)S(1)}, u32[]{:S(2)}, u32[]{:S(2)}) collective-permute-start(bf16[256,128]{1,0:T(8,128)(2,1)S(1)} %get-tuple-element.39), channel_id=1, source_target_pairs={{0,68},{4,64},{8,76},{12,72},{16,84},{20,80},{24,92},{28,88},{32,1... | collective-permute-start | bytes 196616 | tf_op jit(solution)/shard_map/ppermute | solution.py:248
  11.2 0.3 collective-permute-start.2
  11.5 0.1 collective-permute-start.3
  11.6 3.5 %all-to-all-start = ((bf16[4,512,256]{2,1,0:T(8,128)(2,1)}), bf16[4,512,256]{2,1,0:T(8,128)(2,1)S(1)}, u32[]{:S(2)}, u32[]{:S(2)}) async-start(bf16[4,512,256]{2,1,0:T(8,128)(2,1)} %get-tuple-element.47), calls=%async_computation | async-start | bytes 2097152 | tf_op jit(solution)/shard_map/all_to_all | solution.py:257
  15.1 0.0 collective-permute-done.1
  15.1 0.0 collective-permute-done.2
  15.1 0.0 collective-permute-done.3
  15.2 3.9 %collective-permute-start.4 = (bf16[256,128]{1,0:T(8,128)(2,1)S(1)}, bf16[256,128]{1,0:T(8,128)(2,1)S(1)}, u32[]{:S(2)}, u32[]{:S(2)}) collective-permute-start(bf16[256,128]{1,0:T(8,128)(2,1)S(1)} %select_select_fusion.1), channel_id=1, source_target_pairs={{0,48},{4,52},{8,56},{12,60},{16,32},{20,36},{24,40},{28,44},{32,1... | collective-permute-start | bytes 196616 | tf_op jit(solution)/shard_map/ppermute | solution.py:248
  19.1 0.0 collective-permute-start.5
  19.1 0.7 %collective-permute-start.6 = (bf16[256,128]{1,0:T(8,128)(2,1)S(1)}, bf16[256,128]{1,0:T(8,128)(2,1)S(1)}, u32[]{:S(2)}, u32[]{:S(2)}) collective-permute-start(bf16[256,128]{1,0:T(8,128)(2,1)S(1)} %select_select_fusion.1), channel_id=1, source_target_pairs={{0,16},{4,20},{8,24},{12,28},{16,0},{20,4},{24,8},{28,12},{32,48},... | collective-permute-start | bytes 196616 | tf_op jit(solution)/shard_map/ppermute | solution.py:248
  19.7 1.9 %shard_map.66 = (bf16[256,2048]{1,0:T(8,128)(2,1)S(1)}, bf16[256,2048]{1,0:T(8,128)(2,1)S(1)}, bf16[256,2048]{1,0:T(8,128)(2,1)S(1)}) custom-call(bf16[1024,2048]{1,0:T(8,128)(2,1)} %wo.3), custom_call_target="tpu_custom_call" | custom-call | flops 1 | bytes 67108864 | tf_op jit(solution)/shard_map/pallas_call | solution.py:259
  21.6 0.0 copy-start
  21.6 1.0 %copy-done = bf16[256,2048]{1,0:T(8,128)(2,1)} copy-done((bf16[256,2048]{1,0:T(8,128)(2,1)}, bf16[256,2048]{1,0:T(8,128)(2,1)S(1)}, u32[]{:S(2)}) %copy-start) | copy-done | bytes 1048600
  22.6 0.0 collective-permute-done.4
  22.6 1.1 %collective-permute-done.5 = bf16[256,128]{1,0:T(8,128)(2,1)S(1)} collective-permute-done((bf16[256,128]{1,0:T(8,128)(2,1)S(1)}, bf16[256,128]{1,0:T(8,128)(2,1)S(1)}, u32[]{:S(2)}, u32[]{:S(2)}) %collective-permute-start.5) | collective-permute-done | bytes 65568 | tf_op jit(solution)/shard_map/ppermute | solution.py:248
  23.7 0.0 collective-permute-done.6
  23.7 3.0 %collective-permute-start.7 = (bf16[256,128]{1,0:T(8,128)(2,1)S(1)}, bf16[256,128]{1,0:T(8,128)(2,1)S(1)}, u32[]{:S(2)}, u32[]{:S(2)}) collective-permute-start(bf16[256,128]{1,0:T(8,128)(2,1)S(1)} %select_select_fusion), channel_id=1, source_target_pairs={{0,12},{4,8},{8,4},{12,0},{16,28},{20,24},{24,20},{28,16},{32,44},... | collective-permute-start | bytes 196616 | tf_op jit(solution)/shard_map/ppermute | solution.py:248
  26.8 1.7 %collective-permute-done.7 = bf16[256,128]{1,0:T(8,128)(2,1)S(1)} collective-permute-done((bf16[256,128]{1,0:T(8,128)(2,1)S(1)}, bf16[256,128]{1,0:T(8,128)(2,1)S(1)}, u32[]{:S(2)}, u32[]{:S(2)}) %collective-permute-start.7) | collective-permute-done | bytes 65568 | tf_op jit(solution)/shard_map/ppermute | solution.py:248
  28.4 0.0 all-to-all-done.kv
  28.4 0.0 copy-start.1
  28.4 1.8 %shard_map.67 = (bf16[32,2,8,128]{3,2,1,0:T(8,128)(2,1)S(1)}, bf16[256,2048]{1,0:T(8,128)(2,1)S(1)}) custom-call(s32[13]{0:T(128)S(1)} %stack.55.info, bf16[256,128]{1,0:T(8,128)(2,1)S(1)} %broadcast_select_fusion.query, bf16[4,512,256]{2,1,0:T(8,128)(2,1)S(1)} %all-to-all-done.kv, bf16[1024,2048]{1,0:T(8,128)(2,1)} %wo.3), custom_call_target="tpu_custom_call" | custom-call | flops 268435456 | bytes 2097152 | tf_op jit(solution)/shard_map/pallas_call | solution.py:275
  30.2 19.2 %all_to_all.10.parts = bf16[64,8,128]{2,1,0:T(8,128)(2,1)S(1)} all-to-all(bf16[64,8,128]{2,1,0:T(8,128)(2,1)S(1)} %bitcast.15), channel_id=1, replica_groups=mesh['yl'=2,'z'=4,'xh'=2,'xl'=2,'core'=2,'batch'=2] {'yl','z','xh','xl',..., dimensions={0} | all-to-all | bytes 262144 | tf_op jit(solution)/shard_map/all_to_all | solution.py:284
  49.4 0.0 copy-done.1
  49.4 1.6 %shard_map.68 = bf16[4,2048]{1,0:T(4,128)(2,1)} custom-call(bf16[64,8,128]{2,1,0:T(8,128)(2,1)S(1)} %all_to_all.10.parts, bf16[256,2048]{1,0:T(8,128)(2,1)S(1)} %get-tuple-element.49.rest_0_, bf16[256,2048]{1,0:T(8,128)(2,1)S(1)} %get-tuple-element.50.rest_1_, bf16[256,2048]{1,0:T(8,128)(2,1)S(1)} %copy-done.1, bf16[256,2048]{1,0:T(8,128)(2,1)S(1)} %get-tuple-element.52.rest_3_), custom_call_target="tpu_custom_call" | custom-call | flops 33554432 | bytes 4194304 | tf_op jit(solution)/shard_map/pallas_call | solution.py:285
  (3 shorter events, 0.0 us)
Async XLA Ops:
  0.0 4.7 %collective-permute-start = (bf16[256,2048]{1,0:T(8,128)(2,1)}, bf16[256,2048]{1,0:T(8,128)(2,1)S(1)}, u32[]{:S(2)}, u32[]{:S(2)}) collective-permute-start(bf16[256,2048]{1,0:T(8,128)(2,1)} %tokens.1), channel_id=1, source_target_pairs={{0,2},{2,0},{1,3},{3,1},{4,6},{6,4},{5,7},{7,5},{8,10},{10,8},{9,1... | collective-permute-start | bytes 3145736 | tf_op jit(solution)/shard_map/ppermute | solution.py:217
  8.8 6.3 %collective-permute-start.1 = (bf16[256,128]{1,0:T(8,128)(2,1)S(1)}, bf16[256,128]{1,0:T(8,128)(2,1)S(1)}, u32[]{:S(2)}, u32[]{:S(2)}) collective-permute-start(bf16[256,128]{1,0:T(8,128)(2,1)S(1)} %get-tuple-element.39), channel_id=1, source_target_pairs={{0,68},{4,64},{8,76},{12,72},{16,84},{20,80},{24,92},{28,88},{32,1... | collective-permute-start | bytes 196616 | tf_op jit(solution)/shard_map/ppermute | solution.py:248
  11.2 3.9 %collective-permute-start.2 = (bf16[256,128]{1,0:T(8,128)(2,1)S(1)}, bf16[256,128]{1,0:T(8,128)(2,1)S(1)}, u32[]{:S(2)}, u32[]{:S(2)}) collective-permute-start(bf16[256,128]{1,0:T(8,128)(2,1)S(1)} %get-tuple-element.40), channel_id=1, source_target_pairs={{0,4},{4,0},{8,12},{12,8},{16,20},{20,16},{24,28},{28,24},{32,36},... | collective-permute-start | bytes 196616 | tf_op jit(solution)/shard_map/ppermute | solution.py:248
  11.5 3.7 %collective-permute-start.3 = (bf16[256,128]{1,0:T(8,128)(2,1)S(1)}, bf16[256,128]{1,0:T(8,128)(2,1)S(1)}, u32[]{:S(2)}, u32[]{:S(2)}) collective-permute-start(bf16[256,128]{1,0:T(8,128)(2,1)S(1)} %get-tuple-element.41), channel_id=1, source_target_pairs={{0,64},{4,68},{8,72},{12,76},{16,80},{20,84},{24,88},{28,92},{32,9... | collective-permute-start | bytes 196616 | tf_op jit(solution)/shard_map/ppermute | solution.py:248
  11.6 16.8 %all-to-all-start = ((bf16[4,512,256]{2,1,0:T(8,128)(2,1)}), bf16[4,512,256]{2,1,0:T(8,128)(2,1)S(1)}, u32[]{:S(2)}, u32[]{:S(2)}) async-start(bf16[4,512,256]{2,1,0:T(8,128)(2,1)} %get-tuple-element.47), calls=%async_computation | async-start | bytes 2097152 | tf_op jit(solution)/shard_map/all_to_all | solution.py:257
  15.2 7.4 %collective-permute-start.4 = (bf16[256,128]{1,0:T(8,128)(2,1)S(1)}, bf16[256,128]{1,0:T(8,128)(2,1)S(1)}, u32[]{:S(2)}, u32[]{:S(2)}) collective-permute-start(bf16[256,128]{1,0:T(8,128)(2,1)S(1)} %select_select_fusion.1), channel_id=1, source_target_pairs={{0,48},{4,52},{8,56},{12,60},{16,32},{20,36},{24,40},{28,44},{32,1... | collective-permute-start | bytes 196616 | tf_op jit(solution)/shard_map/ppermute | solution.py:248
  19.1 4.6 %collective-permute-start.5 = (bf16[256,128]{1,0:T(8,128)(2,1)S(1)}, bf16[256,128]{1,0:T(8,128)(2,1)S(1)}, u32[]{:S(2)}, u32[]{:S(2)}) collective-permute-start(bf16[256,128]{1,0:T(8,128)(2,1)S(1)} %select_select_fusion.1), channel_id=1, source_target_pairs={{0,32},{4,36},{8,40},{12,44},{16,48},{20,52},{24,56},{28,60},{32,0... | collective-permute-start | bytes 196616 | tf_op jit(solution)/shard_map/ppermute | solution.py:248
  19.1 4.6 %collective-permute-start.6 = (bf16[256,128]{1,0:T(8,128)(2,1)S(1)}, bf16[256,128]{1,0:T(8,128)(2,1)S(1)}, u32[]{:S(2)}, u32[]{:S(2)}) collective-permute-start(bf16[256,128]{1,0:T(8,128)(2,1)S(1)} %select_select_fusion.1), channel_id=1, source_target_pairs={{0,16},{4,20},{8,24},{12,28},{16,0},{20,4},{24,8},{28,12},{32,48},... | collective-permute-start | bytes 196616 | tf_op jit(solution)/shard_map/ppermute | solution.py:248
  21.6 1.0 %copy-start = (bf16[256,2048]{1,0:T(8,128)(2,1)}, bf16[256,2048]{1,0:T(8,128)(2,1)S(1)}, u32[]{:S(2)}) copy-start(bf16[256,2048]{1,0:T(8,128)(2,1)S(1)} %get-tuple-element.51.rest_2_) | copy-start | bytes 3145732
  23.7 4.7 %collective-permute-start.7 = (bf16[256,128]{1,0:T(8,128)(2,1)S(1)}, bf16[256,128]{1,0:T(8,128)(2,1)S(1)}, u32[]{:S(2)}, u32[]{:S(2)}) collective-permute-start(bf16[256,128]{1,0:T(8,128)(2,1)S(1)} %select_select_fusion), channel_id=1, source_target_pairs={{0,12},{4,8},{8,4},{12,0},{16,28},{20,24},{24,20},{28,16},{32,44},... | collective-permute-start | bytes 196616 | tf_op jit(solution)/shard_map/ppermute | solution.py:248
  28.4 21.0 %copy-start.1 = (bf16[256,2048]{1,0:T(8,128)(2,1)S(1)}, bf16[256,2048]{1,0:T(8,128)(2,1)}, u32[]{:S(2)}) copy-start(bf16[256,2048]{1,0:T(8,128)(2,1)} %copy-done) | copy-start | bytes 3145732

commit v6 on v5

--- a/solution.py
+++ b/solution.py
@@ -16,7 +16,6 @@
 CTX = 16384
 MINE = 4
 PIECES = 2
-FETCHED = 3
 F32 = jnp.float32
 BF16 = jnp.bfloat16
 CTX_AXES = ("yl", "z", "xh", "xl", "core")
@@ -93,30 +92,13 @@
         write.wait()
 
 
-def fetch_rows(wo, pieces, first, sems):
-    copies = []
-    for j, piece in enumerate(pieces):
-        at = pl.ds((first + j) * 2 * HD, 2 * HD)
-        copies.append(pltpu.make_async_copy(wo.at[at], piece, sems.at[j]))
-        copies[-1].start()
-    return copies
-
-
-def fetch_kernel(wo, *rest):
-    *pieces, sems = rest
-    for copy in fetch_rows(wo, pieces, 0, sems):
-        copy.wait()
-
-
 def thirds(value):
     first = value.astype(BF16).astype(F32)
     second = (value - first).astype(BF16).astype(F32)
     return [first, second, value - first - second]
 
 
-def attend_kernel(info, query, kv, wo, out, *rest):
-    *pieces, sems = rest
-    copies = fetch_rows(wo, pieces, FETCHED, sems)
+def attend_kernel(info, query, kv, out):
     queries = query[...]
     row = lax.broadcasted_iota(jnp.int32, (LAT, ROWS), 0)
     column = lax.broadcasted_iota(jnp.int32, (LAT, ROWS), 1)
@@ -147,12 +129,9 @@
     upper = lax.broadcasted_iota(jnp.int32, (LAT // 8, 8, HD), 1) < MINE
     out[:, 0] = jnp.where(upper, accum, pltpu.roll(stats, MINE, 1)).astype(BF16)
     out[:, 1] = jnp.where(upper, pltpu.roll(accum, MINE, 1), stats).astype(BF16)
-    for copy in copies:
-        copy.wait()
-
-
-def merge_kernel(parts, *rest):
-    *pieces, out = rest
+
+
+def merge_kernel(parts, weight, out):
     row = lax.broadcasted_iota(jnp.int32, (8, HD), 0) < MINE
     k = lax.broadcasted_iota(jnp.int32, (HD, 2 * HD), 0)
     n = lax.broadcasted_iota(jnp.int32, (HD, 2 * HD), 1)
@@ -183,9 +162,10 @@
             total += t * factor
         heads.append(jnp.where(row, accum / total, 0.0).astype(BF16))
     result = jnp.zeros((8, D), F32)
-    for j, piece in enumerate(pieces):
+    for j in range(4):
         attended = jnp.concatenate(heads[2 * j : 2 * j + 2], axis=1)
-        result += jnp.dot(attended, piece[...], preferred_element_type=F32)
+        rows = weight[pl.ds(j * 2 * HD, 2 * HD), :]
+        result += jnp.dot(attended, rows, preferred_element_type=F32)
     out[...] = result.astype(BF16)[:MINE]
 
 
@@ -200,8 +180,8 @@
     yl = lax.axis_index("yl")
     gain = norm_gain.reshape(1, D)
     in_hbm = functools.partial(pltpu.with_memory_space_constraint, memory_space=pltpu.HBM)
-    gain, query_weight, key_weight, value_weight, out_weight = map(
-        in_hbm, (gain, query_weight, key_weight, value_weight, out_weight)
+    gain, query_weight, key_weight, value_weight = map(
+        in_hbm, (gain, query_weight, key_weight, value_weight)
     )
 
     chips = [(b, z, (x & 2) + a) for b in range(2) for a in range(2)]
@@ -256,40 +236,29 @@
     )
     kv = lax.all_to_all(kv, ("yl", "xl"), 0, 0)
     along = [query] + [hop(query, 0, d, 0) for d in (1, 2, 3)]
-    out_rows = pl.pallas_call(
-        fetch_kernel,
-        out_shape=[shape(2 * HD, D)] * FETCHED,
-        in_specs=[HBM],
-        out_specs=[VMEM] * FETCHED,
-        scratch_shapes=[pltpu.SemaphoreType.DMA((FETCHED,))],
-        compiler_params=params(16),
-        cost_estimate=pl.CostEstimate(flops=1, bytes_accessed=2**26, transcendentals=0),
-    )(out_weight)
     query = jnp.where(
         front, jnp.where(ends, along[3], along[2]), jnp.where(ends, along[1], along[0])
     )
-    query, *out_rows = lax.optimization_barrier((query, *out_rows))
     across = hop(query, 3, 0, 0)
     query = jnp.where(left, across, query)
 
-    parts, *more_rows = pl.pallas_call(
+    parts = pl.pallas_call(
         attend_kernel,
-        out_shape=[shape(LAT // 8, 2, 8, HD)] + [shape(2 * HD, D)] * (4 - FETCHED),
-        in_specs=[SMEM] + [VMEM] * 2 + [HBM],
-        out_specs=[VMEM] * (5 - FETCHED),
-        scratch_shapes=[pltpu.SemaphoreType.DMA((4 - FETCHED,))],
+        out_shape=shape(LAT // 8, 2, 8, HD),
+        in_specs=[SMEM] + [VMEM] * 2,
+        out_specs=VMEM,
         compiler_params=params(16),
-        cost_estimate=pl.CostEstimate(flops=2**28, bytes_accessed=2**21, transcendentals=2**19),
-    )(info, query, kv, out_weight)
+        cost_estimate=pl.CostEstimate(flops=2**33, bytes_accessed=2**21, transcendentals=2**19),
+    )(info, query, kv)
     parts = lax.all_to_all(parts.reshape(64, 8, HD), CTX_AXES, 0, 0)
     return pl.pallas_call(
         merge_kernel,
         out_shape=shape(MINE, D),
-        in_specs=[VMEM] * 5,
+        in_specs=[VMEM] * 2,
         out_specs=VMEM,
         compiler_params=params(16),
         cost_estimate=pl.CostEstimate(flops=2**25, bytes_accessed=2**22, transcendentals=2**16),
-    )(parts, *out_rows, *more_rows)
+    )(parts, out_weight)
 
 
 def solution(mesh):

time: 51.3 us -> 50.8 us (level)
  waiting for transfers between devices: 2.74 us -> 6.42 us
  Pallas kernels: 12.6 us -> 10.5 us
  blocking collectives: 19.2 us -> 17.6 us
  local copies, waits for them, and re-layouts: 1.08 us -> 0.09 us
    ppermute x7, waiting for transfers between devices: 2.73 us -> 6.41 us  [hop(): return lax.ppermute(value, ('yl', 'z', 'xh', 'xl'), pairs)]
    pallas_call x2 -> x1, Pallas kernels: 3.66 us -> 1.65 us  [local(): pl.pallas_call(attend_kernel, out_shape=shape(LAT // 8, 2, 8, HD), in_spe...]
    all_to_all x1, blocking collectives: 19.2 us -> 17.6 us  [local(): parts = lax.all_to_all(parts.reshape(64, 8, HD), CTX_AXES, 0, 0)]
    unnamed x4 -> x2, local copies, waits for them, and re-layouts: 0.99 us -> 0.01 us
    ppermute x7, starting transfers between devices: 10.4 us -> 10.9 us  [hop(): return lax.ppermute(value, ('yl', 'z', 'xh', 'xl'), pairs)]
  transfers between devices with their start and end apart: 9 -> 9, of which waited for: 2 -> 3; matrix products, arithmetic and copies ran while one was open for 0% -> 0% of each run, Pallas kernels for 10% -> 6%
where the time goes in v6:
time: 50.8 us; the launch traced here: 50.6 us
  blocking collectives  17.6 us (35%)
  starting transfers between devices  15.8 us (31%)
  Pallas kernels  10.5 us (21%)
  waiting for transfers between devices  6.42 us (13%)
    all_to_all x1, blocking collectives, local(): parts = lax.all_to_all(parts.reshape(64, 8, HD), CTX_AXES, 0, 0)  17.6 us
    ppermute x7, starting transfers between devices, hop(): return lax.ppermute(value, ('yl', 'z', 'xh', 'xl'), pairs)  10.9 us
    ppermute x7, waiting for transfers between devices, hop(): return lax.ppermute(value, ('yl', 'z', 'xh', 'xl'), pairs)  6.41 us
    pallas_call x1, Pallas kernels, local(): pl.pallas_call(project_kernel, out_shape=[shape(LAT, HD)] * 4 + [shape(4,...  4.11 us
    all_to_all x1, starting transfers between devices, local(): kv = lax.all_to_all(kv, ('yl', 'xl'), 0, 0)  3.54 us
    pallas_call x1, Pallas kernels, local(): pl.pallas_call(own_kernel, out_shape=[shape(ROWS, D), shape(D, 4 * HD), s...  3.16 us
    pallas_call x1, Pallas kernels, local(): pl.pallas_call(attend_kernel, out_shape=shape(LAT // 8, 2, 8, HD), in_spe...  1.65 us
    pallas_call x1, Pallas kernels, local(): pl.pallas_call(merge_kernel, out_shape=shape(MINE, D), in_specs=[VMEM] *...  1.61 us
  transfers between devices with their start and end apart: 9, of which 3 were waited for; matrix products, arithmetic and copies ran while one was open for 0% of the time, Pallas kernels for 6%

profile of v6, /device:TPU:1, one launch (start us, length us, event | category | flops | bytes accessed | tf_op | source)
XLA Modules:
  0.0 50.6 jit_solution(9311400402200526637)
XLA Ops:
  0.0 1.4 %collective-permute-start = (bf16[256,2048]{1,0:T(8,128)(2,1)}, bf16[256,2048]{1,0:T(8,128)(2,1)S(1)}, u32[]{:S(2)}, u32[]{:S(2)}) collective-permute-start(bf16[256,2048]{1,0:T(8,128)(2,1)} %tokens.1), channel_id=1, source_target_pairs={{0,2},{2,0},{1,3},{3,1},{4,6},{6,4},{5,7},{7,5},{8,10},{10,8},{9,1... | collective-permute-start | bytes 3145736 | tf_op jit(solution)/shard_map/ppermute | solution.py:197
  1.4 0.1 stack.55.info
  1.5 3.2 %shard_map.64 = (bf16[256,2048]{1,0:T(8,128)(2,1)S(1)}, bf16[2048,512]{1,0:T(8,128)(2,1)S(1)}, bf16[2048,512]{1,0:T(8,128)(2,1)S(1)}, f32[1,2048]{1,0:T(1,128)S(1)}) custom-call(s32[13]{0:T(128)S(1)} %stack.55.info, bf16[256,2048]{1,0:T(8,128)(2,1)} %tokens.1, f32[1,2048]{1,0:T(1,128)} %bitcast.16, bf16[2048,1024]{1,0:T(8,128)(2,1)} %wk.1, bf16[2048,1024]{1,0:T(8,128)(2,1)} %wv.1), custom_call_target="tpu_custom_call" | custom-call | flops 8388608 | bytes 8388608 | tf_op jit(solution)/shard_map/pallas_call | solution.py:198
  4.7 0.0 collective-permute-done.tokens
  4.7 4.1 %shard_map.65 = (bf16[256,128]{1,0:T(8,128)(2,1)S(1)}, bf16[256,128]{1,0:T(8,128)(2,1)S(1)}, bf16[256,128]{1,0:T(8,128)(2,1)S(1)}, bf16[256,128]{1,0:T(8,128)(2,1)S(1)}, bf16[4,512,256]{2,1,0:T(8,128)(2,1)}) custom-call(s32[13]{0:T(128)S(1)} %stack.55.info, bf16[256,2048]{1,0:T(8,128)(2,1)S(1)} %collective-permute-done.tokens, ...), custom_call_target="tpu_custom_call" | custom-call | flops 2147483648 | bytes 4194304 | tf_op jit(solution)/shard_map/pallas_call | solution.py:207
  8.8 2.4 %collective-permute-start.1 = (bf16[256,128]{1,0:T(8,128)(2,1)S(1)}, bf16[256,128]{1,0:T(8,128)(2,1)S(1)}, u32[]{:S(2)}, u32[]{:S(2)}) collective-permute-start(bf16[256,128]{1,0:T(8,128)(2,1)S(1)} %get-tuple-element.30), channel_id=1, source_target_pairs={{0,68},{4,64},{8,76},{12,72},{16,84},{20,80},{24,92},{28,88},{32,1... | collective-permute-start | bytes 196616 | tf_op jit(solution)/shard_map/ppermute | solution.py:228
  11.2 0.3 collective-permute-start.2
  11.5 0.1 collective-permute-start.3
  11.6 3.5 %all-to-all-start = ((bf16[4,512,256]{2,1,0:T(8,128)(2,1)}), bf16[4,512,256]{2,1,0:T(8,128)(2,1)S(1)}, u32[]{:S(2)}, u32[]{:S(2)}) async-start(bf16[4,512,256]{2,1,0:T(8,128)(2,1)} %get-tuple-element.34), calls=%async_computation | async-start | bytes 2097152 | tf_op jit(solution)/shard_map/all_to_all | solution.py:237
  15.1 0.0 collective-permute-done.1
  15.1 0.0 collective-permute-done.2
  15.1 0.0 collective-permute-done.3
  15.2 1.8 %collective-permute-start.6 = (bf16[256,128]{1,0:T(8,128)(2,1)S(1)}, bf16[256,128]{1,0:T(8,128)(2,1)S(1)}, u32[]{:S(2)}, u32[]{:S(2)}) collective-permute-start(bf16[256,128]{1,0:T(8,128)(2,1)S(1)} %select_select_fusion.1), channel_id=1, source_target_pairs={{0,16},{4,20},{8,24},{12,28},{16,0},{20,4},{24,8},{28,12},{32,48},... | collective-permute-start | bytes 196616 | tf_op jit(solution)/shard_map/ppermute | solution.py:228
  16.9 3.3 %collective-permute-start.5 = (bf16[256,128]{1,0:T(8,128)(2,1)S(1)}, bf16[256,128]{1,0:T(8,128)(2,1)S(1)}, u32[]{:S(2)}, u32[]{:S(2)}) collective-permute-start(bf16[256,128]{1,0:T(8,128)(2,1)S(1)} %select_select_fusion.1), channel_id=1, source_target_pairs={{0,32},{4,36},{8,40},{12,44},{16,48},{20,52},{24,56},{28,60},{32,0... | collective-permute-start | bytes 196616 | tf_op jit(solution)/shard_map/ppermute | solution.py:228
  20.2 0.0 collective-permute-start.4
  20.2 0.0 collective-permute-done.6
  20.2 2.3 %collective-permute-done.5 = bf16[256,128]{1,0:T(8,128)(2,1)S(1)} collective-permute-done((bf16[256,128]{1,0:T(8,128)(2,1)S(1)}, bf16[256,128]{1,0:T(8,128)(2,1)S(1)}, u32[]{:S(2)}, u32[]{:S(2)}) %collective-permute-start.5) | collective-permute-done | bytes 65568 | tf_op jit(solution)/shard_map/ppermute | solution.py:228
  22.6 2.4 %collective-permute-done.4 = bf16[256,128]{1,0:T(8,128)(2,1)S(1)} collective-permute-done((bf16[256,128]{1,0:T(8,128)(2,1)S(1)}, bf16[256,128]{1,0:T(8,128)(2,1)S(1)}, u32[]{:S(2)}, u32[]{:S(2)}) %collective-permute-start.4) | collective-permute-done | bytes 65568 | tf_op jit(solution)/shard_map/ppermute | solution.py:228
  25.0 3.1 %collective-permute-start.7 = (bf16[256,128]{1,0:T(8,128)(2,1)S(1)}, bf16[256,128]{1,0:T(8,128)(2,1)S(1)}, u32[]{:S(2)}, u32[]{:S(2)}) collective-permute-start(bf16[256,128]{1,0:T(8,128)(2,1)S(1)} %select_select_fusion), channel_id=1, source_target_pairs={{0,12},{4,8},{8,4},{12,0},{16,28},{20,24},{24,20},{28,16},{32,44},... | collective-permute-start | bytes 196616 | tf_op jit(solution)/shard_map/ppermute | solution.py:228
  28.1 1.7 %collective-permute-done.7 = bf16[256,128]{1,0:T(8,128)(2,1)S(1)} collective-permute-done((bf16[256,128]{1,0:T(8,128)(2,1)S(1)}, bf16[256,128]{1,0:T(8,128)(2,1)S(1)}, u32[]{:S(2)}, u32[]{:S(2)}) %collective-permute-start.7) | collective-permute-done | bytes 65568 | tf_op jit(solution)/shard_map/ppermute | solution.py:228
  29.7 0.0 all-to-all-done.kv
  29.7 0.0 copy-start
  29.8 1.7 %shard_map.66 = bf16[32,2,8,128]{3,2,1,0:T(8,128)(2,1)S(1)} custom-call(s32[13]{0:T(128)S(1)} %stack.55.info, bf16[256,128]{1,0:T(8,128)(2,1)S(1)} %broadcast_select_fusion.query, bf16[4,512,256]{2,1,0:T(8,128)(2,1)S(1)} %all-to-all-done.kv), custom_call_target="tpu_custom_call" | custom-call | flops 8589934592 | bytes 2097152 | tf_op jit(solution)/shard_map/pallas_call | solution.py:245
  31.4 17.6 %all_to_all.10.parts = bf16[64,8,128]{2,1,0:T(8,128)(2,1)S(1)} all-to-all(bf16[64,8,128]{2,1,0:T(8,128)(2,1)S(1)} %bitcast.15), channel_id=1, replica_groups=mesh['yl'=2,'z'=4,'xh'=2,'xl'=2,'core'=2,'batch'=2] {'yl','z','xh','xl',..., dimensions={0} | all-to-all | bytes 262144 | tf_op jit(solution)/shard_map/all_to_all | solution.py:253
  49.0 0.0 copy-done
  49.0 1.6 %shard_map.67 = bf16[4,2048]{1,0:T(4,128)(2,1)} custom-call(bf16[64,8,128]{2,1,0:T(8,128)(2,1)S(1)} %all_to_all.10.parts, bf16[1024,2048]{1,0:T(8,128)(2,1)S(1)} %copy-done), custom_call_target="tpu_custom_call" | custom-call | flops 33554432 | bytes 4194304 | tf_op jit(solution)/shard_map/pallas_call | solution.py:254
  (3 shorter events, 0.0 us)
Async XLA Ops:
  0.0 4.7 %collective-permute-start = (bf16[256,2048]{1,0:T(8,128)(2,1)}, bf16[256,2048]{1,0:T(8,128)(2,1)S(1)}, u32[]{:S(2)}, u32[]{:S(2)}) collective-permute-start(bf16[256,2048]{1,0:T(8,128)(2,1)} %tokens.1), channel_id=1, source_target_pairs={{0,2},{2,0},{1,3},{3,1},{4,6},{6,4},{5,7},{7,5},{8,10},{10,8},{9,1... | collective-permute-start | bytes 3145736 | tf_op jit(solution)/shard_map/ppermute | solution.py:197
  8.8 6.3 %collective-permute-start.1 = (bf16[256,128]{1,0:T(8,128)(2,1)S(1)}, bf16[256,128]{1,0:T(8,128)(2,1)S(1)}, u32[]{:S(2)}, u32[]{:S(2)}) collective-permute-start(bf16[256,128]{1,0:T(8,128)(2,1)S(1)} %get-tuple-element.30), channel_id=1, source_target_pairs={{0,68},{4,64},{8,76},{12,72},{16,84},{20,80},{24,92},{28,88},{32,1... | collective-permute-start | bytes 196616 | tf_op jit(solution)/shard_map/ppermute | solution.py:228
  11.2 3.9 %collective-permute-start.2 = (bf16[256,128]{1,0:T(8,128)(2,1)S(1)}, bf16[256,128]{1,0:T(8,128)(2,1)S(1)}, u32[]{:S(2)}, u32[]{:S(2)}) collective-permute-start(bf16[256,128]{1,0:T(8,128)(2,1)S(1)} %get-tuple-element.31), channel_id=1, source_target_pairs={{0,4},{4,0},{8,12},{12,8},{16,20},{20,16},{24,28},{28,24},{32,36},... | collective-permute-start | bytes 196616 | tf_op jit(solution)/shard_map/ppermute | solution.py:228
  11.5 3.7 %collective-permute-start.3 = (bf16[256,128]{1,0:T(8,128)(2,1)S(1)}, bf16[256,128]{1,0:T(8,128)(2,1)S(1)}, u32[]{:S(2)}, u32[]{:S(2)}) collective-permute-start(bf16[256,128]{1,0:T(8,128)(2,1)S(1)} %get-tuple-element.32), channel_id=1, source_target_pairs={{0,64},{4,68},{8,72},{12,76},{16,80},{20,84},{24,88},{28,92},{32,9... | collective-permute-start | bytes 196616 | tf_op jit(solution)/shard_map/ppermute | solution.py:228
  11.6 18.2 %all-to-all-start = ((bf16[4,512,256]{2,1,0:T(8,128)(2,1)}), bf16[4,512,256]{2,1,0:T(8,128)(2,1)S(1)}, u32[]{:S(2)}, u32[]{:S(2)}) async-start(bf16[4,512,256]{2,1,0:T(8,128)(2,1)} %get-tuple-element.34), calls=%async_computation | async-start | bytes 2097152 | tf_op jit(solution)/shard_map/all_to_all | solution.py:237
  15.2 5.1 %collective-permute-start.6 = (bf16[256,128]{1,0:T(8,128)(2,1)S(1)}, bf16[256,128]{1,0:T(8,128)(2,1)S(1)}, u32[]{:S(2)}, u32[]{:S(2)}) collective-permute-start(bf16[256,128]{1,0:T(8,128)(2,1)S(1)} %select_select_fusion.1), channel_id=1, source_target_pairs={{0,16},{4,20},{8,24},{12,28},{16,0},{20,4},{24,8},{28,12},{32,48},... | collective-permute-start | bytes 196616 | tf_op jit(solution)/shard_map/ppermute | solution.py:228
  16.9 5.6 %collective-permute-start.5 = (bf16[256,128]{1,0:T(8,128)(2,1)S(1)}, bf16[256,128]{1,0:T(8,128)(2,1)S(1)}, u32[]{:S(2)}, u32[]{:S(2)}) collective-permute-start(bf16[256,128]{1,0:T(8,128)(2,1)S(1)} %select_select_fusion.1), channel_id=1, source_target_pairs={{0,32},{4,36},{8,40},{12,44},{16,48},{20,52},{24,56},{28,60},{32,0... | collective-permute-start | bytes 196616 | tf_op jit(solution)/shard_map/ppermute | solution.py:228
  20.2 4.8 %collective-permute-start.4 = (bf16[256,128]{1,0:T(8,128)(2,1)S(1)}, bf16[256,128]{1,0:T(8,128)(2,1)S(1)}, u32[]{:S(2)}, u32[]{:S(2)}) collective-permute-start(bf16[256,128]{1,0:T(8,128)(2,1)S(1)} %select_select_fusion.1), channel_id=1, source_target_pairs={{0,48},{4,52},{8,56},{12,60},{16,32},{20,36},{24,40},{28,44},{32,1... | collective-permute-start | bytes 196616 | tf_op jit(solution)/shard_map/ppermute | solution.py:228
  25.0 4.7 %collective-permute-start.7 = (bf16[256,128]{1,0:T(8,128)(2,1)S(1)}, bf16[256,128]{1,0:T(8,128)(2,1)S(1)}, u32[]{:S(2)}, u32[]{:S(2)}) collective-permute-start(bf16[256,128]{1,0:T(8,128)(2,1)S(1)} %select_select_fusion), channel_id=1, source_target_pairs={{0,12},{4,8},{8,4},{12,0},{16,28},{20,24},{24,20},{28,16},{32,44},... | collective-permute-start | bytes 196616 | tf_op jit(solution)/shard_map/ppermute | solution.py:228
  29.7 19.2 %copy-start = (bf16[1024,2048]{1,0:T(8,128)(2,1)S(1)}, bf16[1024,2048]{1,0:T(8,128)(2,1)}, u32[]{:S(2)}) copy-start(bf16[1024,2048]{1,0:T(8,128)(2,1)} %weight.1) | copy-start | bytes 12582916

commit v7 on v6

--- a/solution.py
+++ b/solution.py
@@ -22,7 +22,6 @@
 SWAP = ((0, 1), (1, 0))
 HBM = pl.BlockSpec(memory_space=pltpu.HBM)
 VMEM = pl.BlockSpec(memory_space=pltpu.VMEM)
-SMEM = pl.BlockSpec(memory_space=pltpu.SMEM)
 
 
 def near(i):
@@ -35,6 +34,17 @@
 
 def params(mib):
     return pltpu.CompilerParams(vmem_limit_bytes=mib * 2**20)
+
+
+def places():
+    core, z, yl = (lax.axis_index(name) for name in ("core", "z", "yl"))
+    xh, xl = lax.axis_index("xh"), lax.axis_index("xl")
+    info = [core] + [(h & 1) * 2 + ((h >> 1) ^ xh) for h in range(4)]
+    for b in range(2):
+        for a in range(2):
+            for half in range(2):
+                info.append((((b * 4 + z) * 4 + xh * 2 + a) * 2 + (core ^ half)) * ROWS)
+    return info
 
 
 def mine(info):
@@ -48,7 +58,8 @@
     return (centred * lax.rsqrt(variance + 1e-05) * gain).astype(BF16)
 
 
-def own_kernel(info, tokens, gain_ref, wk, wv, out, keys, values, gain, rows, sems):
+def own_kernel(tokens, gain_ref, wk, wv, out, keys, values, gain, rows, sems):
+    info = places()
     step = ROWS // PIECES
     pieces = [pl.ds(j * step, step) for j in range(PIECES)]
     first = pltpu.make_async_copy(gain_ref, gain, sems.at[0])
@@ -67,7 +78,8 @@
         copy.wait()
 
 
-def project_kernel(info, tokens, own, gain, wk, wv, wq, q0, q1, q2, q3, out, other, columns, done, sems):
+def project_kernel(tokens, own, gain, wk, wv, wq, q0, q1, q2, q3, out, other, columns, done, sems):
+    info = places()
     fetch = pltpu.make_async_copy(wq.at[:, mine(info)], columns, sems.at[8])
     fetch.start()
     other[...] = normalise(tokens[...], gain[...])
@@ -98,7 +110,8 @@
     return [first, second, value - first - second]
 
 
-def attend_kernel(info, query, kv, out):
+def attend_kernel(query, kv, out):
+    info = places()
     queries = query[...]
     row = lax.broadcasted_iota(jnp.int32, (LAT, ROWS), 0)
     column = lax.broadcasted_iota(jnp.int32, (LAT, ROWS), 1)
@@ -174,7 +187,6 @@
 
 
 def local(context, norm_gain, query_weight, key_weight, value_weight, out_weight):
-    core = lax.axis_index("core")
     x = lax.axis_index(("xh", "xl"))
     z = lax.axis_index("z")
     yl = lax.axis_index("yl")
@@ -184,30 +196,24 @@
         in_hbm, (gain, query_weight, key_weight, value_weight)
     )
 
-    chips = [(b, z, (x & 2) + a) for b in range(2) for a in range(2)]
-    info = [core] + [(h & 1) * 2 + ((h >> 1) ^ (x >> 1)) for h in range(4)]
-    for b, c, a in chips:
-        for half in range(2):
-            info.append((((b * 4 + c) * 4 + a) * 2 + (core ^ half)) * ROWS)
-    info = jnp.stack(info).astype(jnp.int32)
-    info, odd, low, left, ends, front = lax.optimization_barrier(
-        (info, near(x) == 1, yl == 0, x < 2, (z & 1) == 0, z < 2)
+    gain, odd, left, ends, front, low = lax.optimization_barrier(
+        (gain, near(x) == 1, x < 2, (z & 1) == 0, z < 2, yl == 0)
     )
 
     other_raw = lax.ppermute(context, "core", SWAP)
     own, key_columns, value_columns, gain = pl.pallas_call(
         own_kernel,
         out_shape=[shape(ROWS, D), shape(D, 4 * HD), shape(D, 4 * HD), shape(1, D, dtype=F32)],
-        in_specs=[SMEM] + [HBM] * 4,
+        in_specs=[HBM] * 4,
         out_specs=[VMEM] * 4,
         scratch_shapes=[pltpu.VMEM((ROWS, D), BF16), pltpu.SemaphoreType.DMA((3 + PIECES,))],
         compiler_params=params(16),
         cost_estimate=pl.CostEstimate(flops=2**23, bytes_accessed=2**23, transcendentals=0),
-    )(info, in_hbm(context), gain, key_weight, value_weight)
+    )(in_hbm(context), gain, key_weight, value_weight)
     *queries, kv = pl.pallas_call(
         project_kernel,
         out_shape=[shape(LAT, HD)] * 4 + [shape(4, 2 * ROWS, 2 * HD)],
-        in_specs=[SMEM] + [VMEM] * 5 + [HBM],
+        in_specs=[VMEM] * 5 + [HBM],
         out_specs=[VMEM] * 4 + [HBM],
         scratch_shapes=[
             pltpu.VMEM((ROWS, D), BF16),
@@ -217,7 +223,7 @@
         ],
         compiler_params=params(32),
         cost_estimate=pl.CostEstimate(flops=2**31, bytes_accessed=2**22, transcendentals=0),
-    )(info, other_raw, own, gain, key_columns, value_columns, query_weight)
+    )(other_raw, own, gain, key_columns, value_columns, query_weight)
 
     def hop(value, dx, dz, dy):
         pairs = []
@@ -245,11 +251,11 @@
     parts = pl.pallas_call(
         attend_kernel,
         out_shape=shape(LAT // 8, 2, 8, HD),
-        in_specs=[SMEM] + [VMEM] * 2,
+        in_specs=[VMEM] * 2,
         out_specs=VMEM,
         compiler_params=params(16),
         cost_estimate=pl.CostEstimate(flops=2**33, bytes_accessed=2**21, transcendentals=2**19),
-    )(info, query, kv)
+    )(query, kv)
     parts = lax.all_to_all(parts.reshape(64, 8, HD), CTX_AXES, 0, 0)
     return pl.pallas_call(
         merge_kernel,

time: 50.8 us -> 50 us (0.984)
  Pallas kernels: 10.5 us -> 9.47 us
    pallas_call x1, Pallas kernels: 3.16 us -> 2.61 us  [local(): pl.pallas_call(own_kernel, out_shape=[shape(ROWS, D), shape(D, 4 * HD), s...]
    pallas_call x1, Pallas kernels: 1.65 us -> 1.13 us  [local(): pl.pallas_call(attend_kernel, out_shape=shape(LAT // 8, 2, 8, HD), in_spe...]
  transfers between devices with their start and end apart: 9 -> 9, of which waited for: 3 -> 3; matrix products, arithmetic and copies ran while one was open for 0% -> 0% of each run, Pallas kernels for 6% -> 5%
where the time goes in v7:
time: 50 us; the launch traced here: 49.8 us
  blocking collectives  17.7 us (35%)
  starting transfers between devices  15.9 us (32%)
  Pallas kernels  9.47 us (19%)
  waiting for transfers between devices  6.65 us (13%)
    all_to_all x1, blocking collectives, local(): parts = lax.all_to_all(parts.reshape(64, 8, HD), CTX_AXES, 0, 0)  17.7 us
    ppermute x7, starting transfers between devices, hop(): return lax.ppermute(value, ('yl', 'z', 'xh', 'xl'), pairs)  10.9 us
    ppermute x7, waiting for transfers between devices, hop(): return lax.ppermute(value, ('yl', 'z', 'xh', 'xl'), pairs)  6.64 us
    pallas_call x1, Pallas kernels, local(): pl.pallas_call(project_kernel, out_shape=[shape(LAT, HD)] * 4 + [shape(4,...  4.13 us
    all_to_all x1, starting transfers between devices, local(): kv = lax.all_to_all(kv, ('yl', 'xl'), 0, 0)  3.54 us
    pallas_call x1, Pallas kernels, local(): pl.pallas_call(own_kernel, out_shape=[shape(ROWS, D), shape(D, 4 * HD), s...  2.61 us
    pallas_call x1, Pallas kernels, local(): pl.pallas_call(merge_kernel, out_shape=shape(MINE, D), in_specs=[VMEM] *...  1.6 us
    ppermute x1, starting transfers between devices, local(): other_raw = lax.ppermute(context, 'core', SWAP)  1.42 us
  transfers between devices with their start and end apart: 9, of which 3 were waited for; matrix products, arithmetic and copies ran while one was open for 0% of the time, Pallas kernels for 5%

profile of v7, /device:TPU:1, one launch (start us, length us, event | category | flops | bytes accessed | tf_op | source)
XLA Modules:
  0.0 49.8 jit_solution(5741627050052935151)
XLA Ops:
  0.0 1.4 %collective-permute-start = (bf16[256,2048]{1,0:T(8,128)(2,1)}, bf16[256,2048]{1,0:T(8,128)(2,1)S(1)}, u32[]{:S(2)}, u32[]{:S(2)}) collective-permute-start(bf16[256,2048]{1,0:T(8,128)(2,1)} %tokens.1), channel_id=1, source_target_pairs={{0,2},{2,0},{1,3},{3,1},{4,6},{6,4},{5,7},{7,5},{8,10},{10,8},{9,1... | collective-permute-start | bytes 3145736 | tf_op jit(solution)/shard_map/ppermute | solution.py:203
  1.4 2.6 %shard_map.64 = (bf16[256,2048]{1,0:T(8,128)(2,1)S(1)}, bf16[2048,512]{1,0:T(8,128)(2,1)S(1)}, bf16[2048,512]{1,0:T(8,128)(2,1)S(1)}, f32[1,2048]{1,0:T(1,128)S(1)}) custom-call(bf16[256,2048]{1,0:T(8,128)(2,1)} %tokens.1, f32[1,2048]{1,0:T(1,128)} %bitcast.3, bf16[2048,1024]{1,0:T(8,128)(2,1)} %wk.1, bf16[2048,1024]{1,0:T(8,128)(2,1)} %wv.1), custom_call_target="tpu_custom_call" | custom-call | flops 8388608 | bytes 8388608 | tf_op jit(solution)/shard_map/pallas_call | solution.py:204
  4.0 0.0 collective-permute-done.tokens
  4.1 4.1 %shard_map.65 = (bf16[256,128]{1,0:T(8,128)(2,1)S(1)}, bf16[256,128]{1,0:T(8,128)(2,1)S(1)}, bf16[256,128]{1,0:T(8,128)(2,1)S(1)}, bf16[256,128]{1,0:T(8,128)(2,1)S(1)}, bf16[4,512,256]{2,1,0:T(8,128)(2,1)}) custom-call(bf16[256,2048]{1,0:T(8,128)(2,1)S(1)} %collective-permute-done.tokens, bf16[256,2048]{1,0:T(8,128)(2,1)S(1)} %get-tuple-element.26.own, ...), custom_call_target="tpu_custom_call" | custom-call | flops 2147483648 | bytes 4194304 | tf_op jit(solution)/shard_map/pallas_call | solution.py:213
  8.2 2.4 %collective-permute-start.1 = (bf16[256,128]{1,0:T(8,128)(2,1)S(1)}, bf16[256,128]{1,0:T(8,128)(2,1)S(1)}, u32[]{:S(2)}, u32[]{:S(2)}) collective-permute-start(bf16[256,128]{1,0:T(8,128)(2,1)S(1)} %get-tuple-element.30), channel_id=1, source_target_pairs={{0,68},{4,64},{8,76},{12,72},{16,84},{20,80},{24,92},{28,88},{32,1... | collective-permute-start | bytes 196616 | tf_op jit(solution)/shard_map/ppermute | solution.py:234
  10.6 0.2 collective-permute-start.2
  10.8 0.1 collective-permute-start.3
  11.0 3.5 %all-to-all-start = ((bf16[4,512,256]{2,1,0:T(8,128)(2,1)}), bf16[4,512,256]{2,1,0:T(8,128)(2,1)S(1)}, u32[]{:S(2)}, u32[]{:S(2)}) async-start(bf16[4,512,256]{2,1,0:T(8,128)(2,1)} %get-tuple-element.34), calls=%async_computation | async-start | bytes 2097152 | tf_op jit(solution)/shard_map/all_to_all | solution.py:243
  14.5 0.0 collective-permute-done.1
  14.5 0.0 collective-permute-done.2
  14.5 0.0 collective-permute-done.3
  14.5 1.8 %collective-permute-start.6 = (bf16[256,128]{1,0:T(8,128)(2,1)S(1)}, bf16[256,128]{1,0:T(8,128)(2,1)S(1)}, u32[]{:S(2)}, u32[]{:S(2)}) collective-permute-start(bf16[256,128]{1,0:T(8,128)(2,1)S(1)} %select_select_fusion.1), channel_id=1, source_target_pairs={{0,16},{4,20},{8,24},{12,28},{16,0},{20,4},{24,8},{28,12},{32,48},... | collective-permute-start | bytes 196616 | tf_op jit(solution)/shard_map/ppermute | solution.py:234
  16.3 3.3 %collective-permute-start.5 = (bf16[256,128]{1,0:T(8,128)(2,1)S(1)}, bf16[256,128]{1,0:T(8,128)(2,1)S(1)}, u32[]{:S(2)}, u32[]{:S(2)}) collective-permute-start(bf16[256,128]{1,0:T(8,128)(2,1)S(1)} %select_select_fusion.1), channel_id=1, source_target_pairs={{0,32},{4,36},{8,40},{12,44},{16,48},{20,52},{24,56},{28,60},{32,0... | collective-permute-start | bytes 196616 | tf_op jit(solution)/shard_map/ppermute | solution.py:234
  19.6 0.0 collective-permute-start.4
  19.6 0.0 collective-permute-done.6
  19.6 2.3 %collective-permute-done.5 = bf16[256,128]{1,0:T(8,128)(2,1)S(1)} collective-permute-done((bf16[256,128]{1,0:T(8,128)(2,1)S(1)}, bf16[256,128]{1,0:T(8,128)(2,1)S(1)}, u32[]{:S(2)}, u32[]{:S(2)}) %collective-permute-start.5) | collective-permute-done | bytes 65568 | tf_op jit(solution)/shard_map/ppermute | solution.py:234
  22.0 2.6 %collective-permute-done.4 = bf16[256,128]{1,0:T(8,128)(2,1)S(1)} collective-permute-done((bf16[256,128]{1,0:T(8,128)(2,1)S(1)}, bf16[256,128]{1,0:T(8,128)(2,1)S(1)}, u32[]{:S(2)}, u32[]{:S(2)}) %collective-permute-start.4) | collective-permute-done | bytes 65568 | tf_op jit(solution)/shard_map/ppermute | solution.py:234
  24.6 3.1 %collective-permute-start.7 = (bf16[256,128]{1,0:T(8,128)(2,1)S(1)}, bf16[256,128]{1,0:T(8,128)(2,1)S(1)}, u32[]{:S(2)}, u32[]{:S(2)}) collective-permute-start(bf16[256,128]{1,0:T(8,128)(2,1)S(1)} %select_select_fusion), channel_id=1, source_target_pairs={{0,12},{4,8},{8,4},{12,0},{16,28},{20,24},{24,20},{28,16},{32,44},... | collective-permute-start | bytes 196616 | tf_op jit(solution)/shard_map/ppermute | solution.py:234
  27.7 1.7 %collective-permute-done.7 = bf16[256,128]{1,0:T(8,128)(2,1)S(1)} collective-permute-done((bf16[256,128]{1,0:T(8,128)(2,1)S(1)}, bf16[256,128]{1,0:T(8,128)(2,1)S(1)}, u32[]{:S(2)}, u32[]{:S(2)}) %collective-permute-start.7) | collective-permute-done | bytes 65568 | tf_op jit(solution)/shard_map/ppermute | solution.py:234
  29.4 0.0 all-to-all-done.kv
  29.4 0.0 copy-start
  29.4 1.1 %shard_map.66 = bf16[32,2,8,128]{3,2,1,0:T(8,128)(2,1)S(1)} custom-call(bf16[256,128]{1,0:T(8,128)(2,1)S(1)} %broadcast_select_fusion.query, bf16[4,512,256]{2,1,0:T(8,128)(2,1)S(1)} %all-to-all-done.kv), custom_call_target="tpu_custom_call" | custom-call | flops 8589934592 | bytes 2097152 | tf_op jit(solution)/shard_map/pallas_call | solution.py:251
  30.5 17.7 %all_to_all.10.parts = bf16[64,8,128]{2,1,0:T(8,128)(2,1)S(1)} all-to-all(bf16[64,8,128]{2,1,0:T(8,128)(2,1)S(1)} %bitcast.2), channel_id=1, replica_groups=mesh['yl'=2,'z'=4,'xh'=2,'xl'=2,'core'=2,'batch'=2] {'yl','z','xh','xl',..., dimensions={0} | all-to-all | bytes 262144 | tf_op jit(solution)/shard_map/all_to_all | solution.py:259
  48.2 0.0 copy-done
  48.2 1.6 %shard_map.67 = bf16[4,2048]{1,0:T(4,128)(2,1)} custom-call(bf16[64,8,128]{2,1,0:T(8,128)(2,1)S(1)} %all_to_all.10.parts, bf16[1024,2048]{1,0:T(8,128)(2,1)S(1)} %copy-done), custom_call_target="tpu_custom_call" | custom-call | flops 33554432 | bytes 4194304 | tf_op jit(solution)/shard_map/pallas_call | solution.py:260
  (3 shorter events, 0.0 us)
Async XLA Ops:
  0.0 4.0 %collective-permute-start = (bf16[256,2048]{1,0:T(8,128)(2,1)}, bf16[256,2048]{1,0:T(8,128)(2,1)S(1)}, u32[]{:S(2)}, u32[]{:S(2)}) collective-permute-start(bf16[256,2048]{1,0:T(8,128)(2,1)} %tokens.1), channel_id=1, source_target_pairs={{0,2},{2,0},{1,3},{3,1},{4,6},{6,4},{5,7},{7,5},{8,10},{10,8},{9,1... | collective-permute-start | bytes 3145736 | tf_op jit(solution)/shard_map/ppermute | solution.py:203
  8.2 6.3 %collective-permute-start.1 = (bf16[256,128]{1,0:T(8,128)(2,1)S(1)}, bf16[256,128]{1,0:T(8,128)(2,1)S(1)}, u32[]{:S(2)}, u32[]{:S(2)}) collective-permute-start(bf16[256,128]{1,0:T(8,128)(2,1)S(1)} %get-tuple-element.30), channel_id=1, source_target_pairs={{0,68},{4,64},{8,76},{12,72},{16,84},{20,80},{24,92},{28,88},{32,1... | collective-permute-start | bytes 196616 | tf_op jit(solution)/shard_map/ppermute | solution.py:234
  10.6 3.9 %collective-permute-start.2 = (bf16[256,128]{1,0:T(8,128)(2,1)S(1)}, bf16[256,128]{1,0:T(8,128)(2,1)S(1)}, u32[]{:S(2)}, u32[]{:S(2)}) collective-permute-start(bf16[256,128]{1,0:T(8,128)(2,1)S(1)} %get-tuple-element.31), channel_id=1, source_target_pairs={{0,4},{4,0},{8,12},{12,8},{16,20},{20,16},{24,28},{28,24},{32,36},... | collective-permute-start | bytes 196616 | tf_op jit(solution)/shard_map/ppermute | solution.py:234
  10.8 3.7 %collective-permute-start.3 = (bf16[256,128]{1,0:T(8,128)(2,1)S(1)}, bf16[256,128]{1,0:T(8,128)(2,1)S(1)}, u32[]{:S(2)}, u32[]{:S(2)}) collective-permute-start(bf16[256,128]{1,0:T(8,128)(2,1)S(1)} %get-tuple-element.32), channel_id=1, source_target_pairs={{0,64},{4,68},{8,72},{12,76},{16,80},{20,84},{24,88},{28,92},{32,9... | collective-permute-start | bytes 196616 | tf_op jit(solution)/shard_map/ppermute | solution.py:234
  11.0 18.4 %all-to-all-start = ((bf16[4,512,256]{2,1,0:T(8,128)(2,1)}), bf16[4,512,256]{2,1,0:T(8,128)(2,1)S(1)}, u32[]{:S(2)}, u32[]{:S(2)}) async-start(bf16[4,512,256]{2,1,0:T(8,128)(2,1)} %get-tuple-element.34), calls=%async_computation | async-start | bytes 2097152 | tf_op jit(solution)/shard_map/all_to_all | solution.py:243
  14.5 5.1 %collective-permute-start.6 = (bf16[256,128]{1,0:T(8,128)(2,1)S(1)}, bf16[256,128]{1,0:T(8,128)(2,1)S(1)}, u32[]{:S(2)}, u32[]{:S(2)}) collective-permute-start(bf16[256,128]{1,0:T(8,128)(2,1)S(1)} %select_select_fusion.1), channel_id=1, source_target_pairs={{0,16},{4,20},{8,24},{12,28},{16,0},{20,4},{24,8},{28,12},{32,48},... | collective-permute-start | bytes 196616 | tf_op jit(solution)/shard_map/ppermute | solution.py:234
  16.3 5.6 %collective-permute-start.5 = (bf16[256,128]{1,0:T(8,128)(2,1)S(1)}, bf16[256,128]{1,0:T(8,128)(2,1)S(1)}, u32[]{:S(2)}, u32[]{:S(2)}) collective-permute-start(bf16[256,128]{1,0:T(8,128)(2,1)S(1)} %select_select_fusion.1), channel_id=1, source_target_pairs={{0,32},{4,36},{8,40},{12,44},{16,48},{20,52},{24,56},{28,60},{32,0... | collective-permute-start | bytes 196616 | tf_op jit(solution)/shard_map/ppermute | solution.py:234
  19.6 5.0 %collective-permute-start.4 = (bf16[256,128]{1,0:T(8,128)(2,1)S(1)}, bf16[256,128]{1,0:T(8,128)(2,1)S(1)}, u32[]{:S(2)}, u32[]{:S(2)}) collective-permute-start(bf16[256,128]{1,0:T(8,128)(2,1)S(1)} %select_select_fusion.1), channel_id=1, source_target_pairs={{0,48},{4,52},{8,56},{12,60},{16,32},{20,36},{24,40},{28,44},{32,1... | collective-permute-start | bytes 196616 | tf_op jit(solution)/shard_map/ppermute | solution.py:234
  24.6 4.7 %collective-permute-start.7 = (bf16[256,128]{1,0:T(8,128)(2,1)S(1)}, bf16[256,128]{1,0:T(8,128)(2,1)S(1)}, u32[]{:S(2)}, u32[]{:S(2)}) collective-permute-start(bf16[256,128]{1,0:T(8,128)(2,1)S(1)} %select_select_fusion), channel_id=1, source_target_pairs={{0,12},{4,8},{8,4},{12,0},{16,28},{20,24},{24,20},{28,16},{32,44},... | collective-permute-start | bytes 196616 | tf_op jit(solution)/shard_map/ppermute | solution.py:234
  29.4 18.8 %copy-start = (bf16[1024,2048]{1,0:T(8,128)(2,1)S(1)}, bf16[1024,2048]{1,0:T(8,128)(2,1)}, u32[]{:S(2)}) copy-start(bf16[1024,2048]{1,0:T(8,128)(2,1)} %weight.1) | copy-start | bytes 12582916

commit v8 on v7

--- a/solution.py
+++ b/solution.py
@@ -82,9 +82,10 @@
     info = places()
     fetch = pltpu.make_async_copy(wq.at[:, mine(info)], columns, sems.at[8])
     fetch.start()
-    other[...] = normalise(tokens[...], gain[...])
     writes = []
     for k, rows in enumerate((own, other)):
+        if k == 1:
+            other[...] = normalise(tokens[...], gain[...])
         at = pl.ds(k * ROWS, ROWS)
         keys = jnp.dot(rows[...], wk[...], preferred_element_type=F32).astype(BF16)
         values = jnp.dot(rows[...], wv[...], preferred_element_type=F32).astype(BF16)

time: 50 us -> 50 us (level)
  no operation moved by 1% of the time
where the time goes in v8:
time: 50 us; the launch traced here: 49.8 us
  blocking collectives  17.7 us (35%)
  starting transfers between devices  15.9 us (32%)
  Pallas kernels  9.47 us (19%)
  waiting for transfers between devices  6.65 us (13%)
    all_to_all x1, blocking collectives, local(): parts = lax.all_to_all(parts.reshape(64, 8, HD), CTX_AXES, 0, 0)  17.7 us
    ppermute x7, starting transfers between devices, hop(): return lax.ppermute(value, ('yl', 'z', 'xh', 'xl'), pairs)  10.9 us
    ppermute x7, waiting for transfers between devices, hop(): return lax.ppermute(value, ('yl', 'z', 'xh', 'xl'), pairs)  6.64 us
    pallas_call x1, Pallas kernels, local(): pl.pallas_call(project_kernel, out_shape=[shape(LAT, HD)] * 4 + [shape(4,...  4.13 us
    all_to_all x1, starting transfers between devices, local(): kv = lax.all_to_all(kv, ('yl', 'xl'), 0, 0)  3.54 us
    pallas_call x1, Pallas kernels, local(): pl.pallas_call(own_kernel, out_shape=[shape(ROWS, D), shape(D, 4 * HD), s...  2.61 us
    pallas_call x1, Pallas kernels, local(): pl.pallas_call(merge_kernel, out_shape=shape(MINE, D), in_specs=[VMEM] *...  1.6 us
    ppermute x1, starting transfers between devices, local(): other_raw = lax.ppermute(context, 'core', SWAP)  1.42 us
  transfers between devices with their start and end apart: 9, of which 3 were waited for; matrix products, arithmetic and copies ran while one was open for 0% of the time, Pallas kernels for 5%

profile of v8, /device:TPU:1, one launch (start us, length us, event | category | flops | bytes accessed | tf_op | source)
XLA Modules:
  0.0 49.8 jit_solution(5741627050052935151)
XLA Ops:
  0.0 1.4 %collective-permute-start = (bf16[256,2048]{1,0:T(8,128)(2,1)}, bf16[256,2048]{1,0:T(8,128)(2,1)S(1)}, u32[]{:S(2)}, u32[]{:S(2)}) collective-permute-start(bf16[256,2048]{1,0:T(8,128)(2,1)} %tokens.1), channel_id=1, source_target_pairs={{0,2},{2,0},{1,3},{3,1},{4,6},{6,4},{5,7},{7,5},{8,10},{10,8},{9,1... | collective-permute-start | bytes 3145736 | tf_op jit(solution)/shard_map/ppermute | solution.py:204
  1.4 2.6 %shard_map.64 = (bf16[256,2048]{1,0:T(8,128)(2,1)S(1)}, bf16[2048,512]{1,0:T(8,128)(2,1)S(1)}, bf16[2048,512]{1,0:T(8,128)(2,1)S(1)}, f32[1,2048]{1,0:T(1,128)S(1)}) custom-call(bf16[256,2048]{1,0:T(8,128)(2,1)} %tokens.1, f32[1,2048]{1,0:T(1,128)} %bitcast.3, bf16[2048,1024]{1,0:T(8,128)(2,1)} %wk.1, bf16[2048,1024]{1,0:T(8,128)(2,1)} %wv.1), custom_call_target="tpu_custom_call" | custom-call | flops 8388608 | bytes 8388608 | tf_op jit(solution)/shard_map/pallas_call | solution.py:205
  4.0 0.0 collective-permute-done.tokens
  4.1 4.1 %shard_map.65 = (bf16[256,128]{1,0:T(8,128)(2,1)S(1)}, bf16[256,128]{1,0:T(8,128)(2,1)S(1)}, bf16[256,128]{1,0:T(8,128)(2,1)S(1)}, bf16[256,128]{1,0:T(8,128)(2,1)S(1)}, bf16[4,512,256]{2,1,0:T(8,128)(2,1)}) custom-call(bf16[256,2048]{1,0:T(8,128)(2,1)S(1)} %collective-permute-done.tokens, bf16[256,2048]{1,0:T(8,128)(2,1)S(1)} %get-tuple-element.26.own, ...), custom_call_target="tpu_custom_call" | custom-call | flops 2147483648 | bytes 4194304 | tf_op jit(solution)/shard_map/pallas_call | solution.py:214
  8.2 2.4 %collective-permute-start.1 = (bf16[256,128]{1,0:T(8,128)(2,1)S(1)}, bf16[256,128]{1,0:T(8,128)(2,1)S(1)}, u32[]{:S(2)}, u32[]{:S(2)}) collective-permute-start(bf16[256,128]{1,0:T(8,128)(2,1)S(1)} %get-tuple-element.30), channel_id=1, source_target_pairs={{0,68},{4,64},{8,76},{12,72},{16,84},{20,80},{24,92},{28,88},{32,1... | collective-permute-start | bytes 196616 | tf_op jit(solution)/shard_map/ppermute | solution.py:235
  10.6 0.2 collective-permute-start.2
  10.8 0.1 collective-permute-start.3
  11.0 3.5 %all-to-all-start = ((bf16[4,512,256]{2,1,0:T(8,128)(2,1)}), bf16[4,512,256]{2,1,0:T(8,128)(2,1)S(1)}, u32[]{:S(2)}, u32[]{:S(2)}) async-start(bf16[4,512,256]{2,1,0:T(8,128)(2,1)} %get-tuple-element.34), calls=%async_computation | async-start | bytes 2097152 | tf_op jit(solution)/shard_map/all_to_all | solution.py:244
  14.5 0.0 collective-permute-done.1
  14.5 0.0 collective-permute-done.2
  14.5 0.0 collective-permute-done.3
  14.5 1.8 %collective-permute-start.6 = (bf16[256,128]{1,0:T(8,128)(2,1)S(1)}, bf16[256,128]{1,0:T(8,128)(2,1)S(1)}, u32[]{:S(2)}, u32[]{:S(2)}) collective-permute-start(bf16[256,128]{1,0:T(8,128)(2,1)S(1)} %select_select_fusion.1), channel_id=1, source_target_pairs={{0,16},{4,20},{8,24},{12,28},{16,0},{20,4},{24,8},{28,12},{32,48},... | collective-permute-start | bytes 196616 | tf_op jit(solution)/shard_map/ppermute | solution.py:235
  16.3 3.3 %collective-permute-start.5 = (bf16[256,128]{1,0:T(8,128)(2,1)S(1)}, bf16[256,128]{1,0:T(8,128)(2,1)S(1)}, u32[]{:S(2)}, u32[]{:S(2)}) collective-permute-start(bf16[256,128]{1,0:T(8,128)(2,1)S(1)} %select_select_fusion.1), channel_id=1, source_target_pairs={{0,32},{4,36},{8,40},{12,44},{16,48},{20,52},{24,56},{28,60},{32,0... | collective-permute-start | bytes 196616 | tf_op jit(solution)/shard_map/ppermute | solution.py:235
  19.6 0.0 collective-permute-start.4
  19.6 0.0 collective-permute-done.6
  19.6 2.3 %collective-permute-done.5 = bf16[256,128]{1,0:T(8,128)(2,1)S(1)} collective-permute-done((bf16[256,128]{1,0:T(8,128)(2,1)S(1)}, bf16[256,128]{1,0:T(8,128)(2,1)S(1)}, u32[]{:S(2)}, u32[]{:S(2)}) %collective-permute-start.5) | collective-permute-done | bytes 65568 | tf_op jit(solution)/shard_map/ppermute | solution.py:235
  22.0 2.6 %collective-permute-done.4 = bf16[256,128]{1,0:T(8,128)(2,1)S(1)} collective-permute-done((bf16[256,128]{1,0:T(8,128)(2,1)S(1)}, bf16[256,128]{1,0:T(8,128)(2,1)S(1)}, u32[]{:S(2)}, u32[]{:S(2)}) %collective-permute-start.4) | collective-permute-done | bytes 65568 | tf_op jit(solution)/shard_map/ppermute | solution.py:235
  24.6 3.1 %collective-permute-start.7 = (bf16[256,128]{1,0:T(8,128)(2,1)S(1)}, bf16[256,128]{1,0:T(8,128)(2,1)S(1)}, u32[]{:S(2)}, u32[]{:S(2)}) collective-permute-start(bf16[256,128]{1,0:T(8,128)(2,1)S(1)} %select_select_fusion), channel_id=1, source_target_pairs={{0,12},{4,8},{8,4},{12,0},{16,28},{20,24},{24,20},{28,16},{32,44},... | collective-permute-start | bytes 196616 | tf_op jit(solution)/shard_map/ppermute | solution.py:235
  27.7 1.7 %collective-permute-done.7 = bf16[256,128]{1,0:T(8,128)(2,1)S(1)} collective-permute-done((bf16[256,128]{1,0:T(8,128)(2,1)S(1)}, bf16[256,128]{1,0:T(8,128)(2,1)S(1)}, u32[]{:S(2)}, u32[]{:S(2)}) %collective-permute-start.7) | collective-permute-done | bytes 65568 | tf_op jit(solution)/shard_map/ppermute | solution.py:235
  29.4 0.0 all-to-all-done.kv
  29.4 0.0 copy-start
  29.4 1.1 %shard_map.66 = bf16[32,2,8,128]{3,2,1,0:T(8,128)(2,1)S(1)} custom-call(bf16[256,128]{1,0:T(8,128)(2,1)S(1)} %broadcast_select_fusion.query, bf16[4,512,256]{2,1,0:T(8,128)(2,1)S(1)} %all-to-all-done.kv), custom_call_target="tpu_custom_call" | custom-call | flops 8589934592 | bytes 2097152 | tf_op jit(solution)/shard_map/pallas_call | solution.py:252
  30.5 17.7 %all_to_all.10.parts = bf16[64,8,128]{2,1,0:T(8,128)(2,1)S(1)} all-to-all(bf16[64,8,128]{2,1,0:T(8,128)(2,1)S(1)} %bitcast.2), channel_id=1, replica_groups=mesh['yl'=2,'z'=4,'xh'=2,'xl'=2,'core'=2,'batch'=2] {'yl','z','xh','xl',..., dimensions={0} | all-to-all | bytes 262144 | tf_op jit(solution)/shard_map/all_to_all | solution.py:260
  48.2 0.0 copy-done
  48.2 1.6 %shard_map.67 = bf16[4,2048]{1,0:T(4,128)(2,1)} custom-call(bf16[64,8,128]{2,1,0:T(8,128)(2,1)S(1)} %all_to_all.10.parts, bf16[1024,2048]{1,0:T(8,128)(2,1)S(1)} %copy-done), custom_call_target="tpu_custom_call" | custom-call | flops 33554432 | bytes 4194304 | tf_op jit(solution)/shard_map/pallas_call | solution.py:261
  (3 shorter events, 0.0 us)
Async XLA Ops:
  0.0 4.0 %collective-permute-start = (bf16[256,2048]{1,0:T(8,128)(2,1)}, bf16[256,2048]{1,0:T(8,128)(2,1)S(1)}, u32[]{:S(2)}, u32[]{:S(2)}) collective-permute-start(bf16[256,2048]{1,0:T(8,128)(2,1)} %tokens.1), channel_id=1, source_target_pairs={{0,2},{2,0},{1,3},{3,1},{4,6},{6,4},{5,7},{7,5},{8,10},{10,8},{9,1... | collective-permute-start | bytes 3145736 | tf_op jit(solution)/shard_map/ppermute | solution.py:204
  8.2 6.3 %collective-permute-start.1 = (bf16[256,128]{1,0:T(8,128)(2,1)S(1)}, bf16[256,128]{1,0:T(8,128)(2,1)S(1)}, u32[]{:S(2)}, u32[]{:S(2)}) collective-permute-start(bf16[256,128]{1,0:T(8,128)(2,1)S(1)} %get-tuple-element.30), channel_id=1, source_target_pairs={{0,68},{4,64},{8,76},{12,72},{16,84},{20,80},{24,92},{28,88},{32,1... | collective-permute-start | bytes 196616 | tf_op jit(solution)/shard_map/ppermute | solution.py:235
  10.6 3.9 %collective-permute-start.2 = (bf16[256,128]{1,0:T(8,128)(2,1)S(1)}, bf16[256,128]{1,0:T(8,128)(2,1)S(1)}, u32[]{:S(2)}, u32[]{:S(2)}) collective-permute-start(bf16[256,128]{1,0:T(8,128)(2,1)S(1)} %get-tuple-element.31), channel_id=1, source_target_pairs={{0,4},{4,0},{8,12},{12,8},{16,20},{20,16},{24,28},{28,24},{32,36},... | collective-permute-start | bytes 196616 | tf_op jit(solution)/shard_map/ppermute | solution.py:235
  10.8 3.7 %collective-permute-start.3 = (bf16[256,128]{1,0:T(8,128)(2,1)S(1)}, bf16[256,128]{1,0:T(8,128)(2,1)S(1)}, u32[]{:S(2)}, u32[]{:S(2)}) collective-permute-start(bf16[256,128]{1,0:T(8,128)(2,1)S(1)} %get-tuple-element.32), channel_id=1, source_target_pairs={{0,64},{4,68},{8,72},{12,76},{16,80},{20,84},{24,88},{28,92},{32,9... | collective-permute-start | bytes 196616 | tf_op jit(solution)/shard_map/ppermute | solution.py:235
  11.0 18.4 %all-to-all-start = ((bf16[4,512,256]{2,1,0:T(8,128)(2,1)}), bf16[4,512,256]{2,1,0:T(8,128)(2,1)S(1)}, u32[]{:S(2)}, u32[]{:S(2)}) async-start(bf16[4,512,256]{2,1,0:T(8,128)(2,1)} %get-tuple-element.34), calls=%async_computation | async-start | bytes 2097152 | tf_op jit(solution)/shard_map/all_to_all | solution.py:244
  14.5 5.1 %collective-permute-start.6 = (bf16[256,128]{1,0:T(8,128)(2,1)S(1)}, bf16[256,128]{1,0:T(8,128)(2,1)S(1)}, u32[]{:S(2)}, u32[]{:S(2)}) collective-permute-start(bf16[256,128]{1,0:T(8,128)(2,1)S(1)} %select_select_fusion.1), channel_id=1, source_target_pairs={{0,16},{4,20},{8,24},{12,28},{16,0},{20,4},{24,8},{28,12},{32,48},... | collective-permute-start | bytes 196616 | tf_op jit(solution)/shard_map/ppermute | solution.py:235
  16.3 5.6 %collective-permute-start.5 = (bf16[256,128]{1,0:T(8,128)(2,1)S(1)}, bf16[256,128]{1,0:T(8,128)(2,1)S(1)}, u32[]{:S(2)}, u32[]{:S(2)}) collective-permute-start(bf16[256,128]{1,0:T(8,128)(2,1)S(1)} %select_select_fusion.1), channel_id=1, source_target_pairs={{0,32},{4,36},{8,40},{12,44},{16,48},{20,52},{24,56},{28,60},{32,0... | collective-permute-start | bytes 196616 | tf_op jit(solution)/shard_map/ppermute | solution.py:235
  19.6 5.0 %collective-permute-start.4 = (bf16[256,128]{1,0:T(8,128)(2,1)S(1)}, bf16[256,128]{1,0:T(8,128)(2,1)S(1)}, u32[]{:S(2)}, u32[]{:S(2)}) collective-permute-start(bf16[256,128]{1,0:T(8,128)(2,1)S(1)} %select_select_fusion.1), channel_id=1, source_target_pairs={{0,48},{4,52},{8,56},{12,60},{16,32},{20,36},{24,40},{28,44},{32,1... | collective-permute-start | bytes 196616 | tf_op jit(solution)/shard_map/ppermute | solution.py:235
  24.6 4.7 %collective-permute-start.7 = (bf16[256,128]{1,0:T(8,128)(2,1)S(1)}, bf16[256,128]{1,0:T(8,128)(2,1)S(1)}, u32[]{:S(2)}, u32[]{:S(2)}) collective-permute-start(bf16[256,128]{1,0:T(8,128)(2,1)S(1)} %select_select_fusion), channel_id=1, source_target_pairs={{0,12},{4,8},{8,4},{12,0},{16,28},{20,24},{24,20},{28,16},{32,44},... | collective-permute-start | bytes 196616 | tf_op jit(solution)/shard_map/ppermute | solution.py:235
  29.4 18.8 %copy-start = (bf16[1024,2048]{1,0:T(8,128)(2,1)S(1)}, bf16[1024,2048]{1,0:T(8,128)(2,1)}, u32[]{:S(2)}) copy-start(bf16[1024,2048]{1,0:T(8,128)(2,1)} %weight.1) | copy-start | bytes 12582916
